TPU v7x, 512 devices: a whole 4x4x16 slice. The times are simulated.
512 devices in a mesh: section: 16 (over z), tensor: 32 (over y, x, core).
Axes of the slice: x: 4, y: 4, z: 16, core: 2. Of those that a mesh axis runs over, the one named last changes fastest.
Arguments:
- tokens: bfloat16 [128, 6144], P(None, 'tensor'), may hold values from -6 to 6
- targets: bfloat16 [128, 6144], P(None, 'tensor'), may hold values from -6 to 6
- doc_ids: int32 [128], replicated, may hold values from 0 to 7, never falling along the last dimension, each value on 1 to 32 neighbouring positions
- norm_gains: float32 [16, 6144], P('section'), may hold values from 0.5 to 1.5
- w_qk: bfloat16 [16, 6144, 4096], P('section', None, 'tensor')
- w_val: bfloat16 [16, 6144, 4096], P('section', None, 'tensor'), may hold values from -0.078125 to 0.078125
- w_out: bfloat16 [16, 4096, 6144], P('section', None, 'tensor'), may hold values from -0.09375 to 0.09375
Outputs:
- section_outputs: bfloat16 [16, 128, 6144], P('section', None, 'tensor')
- losses: float32 [8], replicated
Inputs may be any that keep to these rules, and one draw needn't show every extreme that they name: `doc_ids`: ids never fall along the row; each of the 8 documents holds 1 to 32 tokens, one exactly 32.
All inputs are finite; a program needn't handle non-finite values.
Results may differ from a plain program's by a relative error of at most 0.03.
Values may be sent and summed in bfloat16 or wider, within the bound.
No kernel may reach another device: no remote copies, remote signals or barrier semaphores. Data moves between devices by JAX's collectives and lax.ppermute only.
A program may use at most 64 MiB of HBM per device.

v0:
```python
import jax
import jax.numpy as jnp
from jax import lax
from jax.sharding import PartitionSpec as P

D = 6144
HD = 64
DOCS = 8


def for_sending(array):
    return jax.tree.map(lambda a: a.astype(jnp.bfloat16) if a.dtype == jnp.float32 else a, array)


def from_behind(value, axis, steps):
    count = lax.axis_size(axis)
    first, last = (max(0, -steps), min(count, count - steps))
    return lax.ppermute(value, axis, [(source, source + steps) for source in range(first, last)])


def local(tokens, targets, doc_ids, norm_gains, w_qk, w_val, w_out):
    section_index = lax.axis_index("section")
    section_count = lax.axis_size("section")
    row_count = tokens.shape[0]
    cols_own = tokens.shape[1]
    sixteenth = row_count // 16
    slice_lens = [5 * sixteenth, 4 * sixteenth, 4 * sixteenth, 3 * sixteenth]
    slice_starts = [sum(slice_lens[:order_num]) for order_num in range(len(slice_lens))]
    slice_total = len(slice_lens)
    longest = max(slice_lens)
    padded_rows = row_count + longest
    start_table = jnp.array(slice_starts, jnp.int32)
    tokens_pad = jnp.concatenate([tokens, jnp.zeros((longest, cols_own), tokens.dtype)], 0)
    inner_own = w_qk.shape[2]
    heads_own = inner_own // HD
    gain_row = norm_gains[0]
    qk_weight = w_qk[0]
    val_weight = w_val[0]
    out_weight = w_out[0]
    zero_index = jnp.zeros((), jnp.int32)

    def add_heads(total, piece):
        rows_w = lax.slice_in_dim(out_weight, 0, piece.shape[1], axis=0)
        return total + jnp.dot(piece, rows_w, preferred_element_type=jnp.float32)

    def make_branch(slice_num):
        length = slice_lens[slice_num]
        begin = slice_starts[slice_num]
        finish = begin + length

        def branch(operands):
            full_rows, key_cache, val_cache = operands
            x_float = full_rows[:length].astype(jnp.float32)
            row_mean = jnp.mean(x_float, -1, keepdims=True)
            centered = x_float - row_mean
            row_var = jnp.mean(centered * centered, -1, keepdims=True)
            normed = (centered * lax.rsqrt(row_var + 1e-05) * gain_row[None, :]).astype(
                jnp.bfloat16
            )
            qk_rows = jnp.dot(normed, qk_weight, preferred_element_type=jnp.float32).astype(
                jnp.bfloat16
            )
            val_rows = jnp.dot(normed, val_weight, preferred_element_type=jnp.float32).astype(
                jnp.bfloat16
            )
            query_heads = qk_rows.reshape(length, heads_own, HD)
            qk_float = query_heads.astype(jnp.float32)
            key_rows = (
                qk_float * lax.rsqrt(jnp.mean(qk_float * qk_float, -1, keepdims=True) + 1e-06)
            ).astype(jnp.bfloat16)
            key_cache = key_cache.at[begin:finish].set(key_rows.reshape(length, inner_own))
            val_cache = val_cache.at[begin:finish].set(val_rows)
            key_part = key_cache[:finish].reshape(finish, heads_own, HD)
            val_part = val_cache[:finish].reshape(finish, heads_own, HD)
            scores = (
                jnp.einsum(
                    "qhd,khd->hqk", query_heads, key_part, preferred_element_type=jnp.float32
                )
                / HD
            )
            key_pos = jnp.arange(finish, dtype=jnp.int32)
            query_pos = begin + jnp.arange(length, dtype=jnp.int32)
            key_doc = doc_ids[:finish]
            query_doc = doc_ids[begin:finish]
            allowed = (key_pos[None, :] <= query_pos[:, None]) & (
                key_doc[None, :] == query_doc[:, None]
            )
            masked = jnp.where(allowed[None], scores, -1e30)
            peak = jnp.max(masked, -1, keepdims=True)
            expo = jnp.where(allowed[None], jnp.exp(masked - peak), 0.0)
            weights = (expo / jnp.sum(expo, -1, keepdims=True)).astype(jnp.bfloat16)
            attended = jnp.einsum(
                "hqk,khd->qhd", weights, val_part, preferred_element_type=jnp.float32
            )
            attended = attended.astype(jnp.bfloat16).reshape(length, inner_own)
            if length < longest:
                attended = jnp.concatenate(
                    [attended, jnp.zeros((longest - length, inner_own), jnp.bfloat16)], 0
                )
            return (key_cache, val_cache, attended)

        return branch

    branches = [make_branch(slice_num) for slice_num in range(slice_total)]

    def advance(step_num, state_tuple):
        received, key_cache, val_cache, out_cache = state_tuple
        order_num = step_num - section_index
        active = (order_num >= 0) & (order_num < slice_total)
        slot = jnp.clip(order_num, 0, slice_total - 1)
        row_start = start_table[slot]
        first_rows = lax.dynamic_slice_in_dim(tokens_pad, row_start, longest, 0)
        own_rows = jnp.where(section_index == 0, first_rows, received)
        full_rows = lax.all_gather(own_rows, "tensor", axis=1, tiled=True)
        new_keys, new_vals, attended = lax.switch(slot, branches, (full_rows, key_cache, val_cache))
        key_cache = jnp.where(active, new_keys, key_cache)
        val_cache = jnp.where(active, new_vals, val_cache)
        empty = jnp.zeros((longest, cols_own), jnp.float32)
        mixed = add_heads(
            empty,
            jax.tree.map(
                lambda part: lax.all_gather(part, "tensor", axis=1, tiled=True),
                for_sending(attended),
            ),
        )
        layer_rows = (own_rows.astype(jnp.float32) + mixed).astype(jnp.bfloat16)
        written = lax.dynamic_update_slice(out_cache, layer_rows, (row_start, zero_index))
        out_cache = jnp.where(active, written, out_cache)
        passed = from_behind(layer_rows, "section", 1)
        return (passed, key_cache, val_cache, out_cache)

    initial = (
        jnp.zeros((longest, cols_own), jnp.bfloat16),
        jnp.zeros((row_count, inner_own), jnp.bfloat16),
        jnp.zeros((row_count, inner_own), jnp.bfloat16),
        jnp.zeros((padded_rows, cols_own), jnp.bfloat16),
    )
    final_state = lax.fori_loop(0, section_count + slice_total - 1, advance, initial)
    section_rows = final_state[3][:row_count]
    diff = section_rows.astype(jnp.float32) - targets.astype(jnp.float32)
    token_sums = jnp.sum(diff * diff, -1)
    doc_table = (doc_ids[:, None] == jnp.arange(DOCS, dtype=jnp.int32)[None, :]).astype(jnp.float32)
    partial_sums = jnp.sum(doc_table * token_sums[:, None], 0)
    doc_counts = jnp.sum(doc_table, 0)
    last_flag = (section_index == section_count - 1).astype(jnp.float32)
    totals = lax.psum(partial_sums * last_flag, ("section", "tensor"))
    losses = totals / (doc_counts * D)
    return (section_rows[None], losses)


def solution(mesh):
    placed = (
        P(None, "tensor"),
        P(None, "tensor"),
        P(),
        P("section", None),
        P("section", None, "tensor"),
        P("section", None, "tensor"),
        P("section", None, "tensor"),
    )
    return jax.shard_map(
        local,
        mesh=mesh,
        in_specs=placed,
        out_specs=(P("section", None, "tensor"), P()),
        check_vma=False,
    )
```

profile of v0, /device:TPU:1, one launch (start us, length us, event | category | flops | bytes accessed | tf_op | source)
XLA Modules:
  0.0 1411.2 jit_solution(16317456066616115482)
XLA Ops:
  4.9 1297.7 %while.30 = (s32[]{:T(128)}, bf16[40,192]{1,0:T(8,128)(2,1)S(1)}, bf16[128,128]{0,1:T(8,128)(2,1)S(1)}, bf16[128,128]{0,1:T(8,128)(2,1)S(1)}, bf16[168,192]{1,0:...) while((s32[]{:T(128)}, bf16[40,192]{1,0:T(8,128)(2,1)S(1)}, ...), condition=%wide.region_25.26_spmd.clone.clone, body=%wide.region_0.25_spmd.sunk.clone.clone.sunk | while | flops 193686624 | bytes 10948707 | solution.py:138
  7.5 28.6 %all-gather.3 = bf16[32,192,40]{1,2,0:T(8,128)(2,1)S(1)} all-gather(bf16[1,192,40]{1,2,0:T(8,128)(2,1)S(1)} %fusion.109), channel_id=1, replica_groups=mesh['section'=16,'tensor'=32] {'tensor'}, dimensions={0}, use_global_device_ids=true | all-gather | bytes 506880 | tf_op jit(solution)/shard_map/while/body/eval_jaxpr/all_gather | solution.py:114
  37.0 8.3 conditional.5
  45.3 24.7 %all_gather.22 = bf16[40,4096]{1,0:T(8,128)(2,1)S(1)} all-gather(bf16[40,128]{1,0:T(8,128)(2,1)S(1)} %get-tuple-element.754), channel_id=1, replica_groups=mesh['section'=16,'tensor'=32] {'tensor'}, dimensions={1}, use_global_device_ids=true | all-gather | bytes 337920 | tf_op jit(solution)/shard_map/while/body/eval_jaxpr/all_gather | solution.py:122
  77.4 22.4 %all-gather.3 = bf16[32,192,40]{1,2,0:T(8,128)(2,1)S(1)} all-gather(bf16[1,192,40]{1,2,0:T(8,128)(2,1)S(1)} %fusion.109), channel_id=1, replica_groups=mesh['section'=16,'tensor'=32] {'tensor'}, dimensions={0}, use_global_device_ids=true | all-gather | bytes 506880 | tf_op jit(solution)/shard_map/while/body/eval_jaxpr/all_gather | solution.py:114
  100.7 10.0 conditional.5
  110.7 24.2 %all_gather.22 = bf16[40,4096]{1,0:T(8,128)(2,1)S(1)} all-gather(bf16[40,128]{1,0:T(8,128)(2,1)S(1)} %get-tuple-element.754), channel_id=1, replica_groups=mesh['section'=16,'tensor'=32] {'tensor'}, dimensions={1}, use_global_device_ids=true | all-gather | bytes 337920 | tf_op jit(solution)/shard_map/while/body/eval_jaxpr/all_gather | solution.py:122
  143.1 22.7 %all-gather.3 = bf16[32,192,40]{1,2,0:T(8,128)(2,1)S(1)} all-gather(bf16[1,192,40]{1,2,0:T(8,128)(2,1)S(1)} %fusion.109), channel_id=1, replica_groups=mesh['section'=16,'tensor'=32] {'tensor'}, dimensions={0}, use_global_device_ids=true | all-gather | bytes 506880 | tf_op jit(solution)/shard_map/while/body/eval_jaxpr/all_gather | solution.py:114
  166.7 10.0 conditional.5
  176.7 24.2 %all_gather.22 = bf16[40,4096]{1,0:T(8,128)(2,1)S(1)} all-gather(bf16[40,128]{1,0:T(8,128)(2,1)S(1)} %get-tuple-element.754), channel_id=1, replica_groups=mesh['section'=16,'tensor'=32] {'tensor'}, dimensions={1}, use_global_device_ids=true | all-gather | bytes 337920 | tf_op jit(solution)/shard_map/while/body/eval_jaxpr/all_gather | solution.py:122
  210.8 22.7 %all-gather.3 = bf16[32,192,40]{1,2,0:T(8,128)(2,1)S(1)} all-gather(bf16[1,192,40]{1,2,0:T(8,128)(2,1)S(1)} %fusion.109), channel_id=1, replica_groups=mesh['section'=16,'tensor'=32] {'tensor'}, dimensions={0}, use_global_device_ids=true | all-gather | bytes 506880 | tf_op jit(solution)/shard_map/while/body/eval_jaxpr/all_gather | solution.py:114
  234.4 9.9 conditional.5
  244.3 24.2 %all_gather.22 = bf16[40,4096]{1,0:T(8,128)(2,1)S(1)} all-gather(bf16[40,128]{1,0:T(8,128)(2,1)S(1)} %get-tuple-element.754), channel_id=1, replica_groups=mesh['section'=16,'tensor'=32] {'tensor'}, dimensions={1}, use_global_device_ids=true | all-gather | bytes 337920 | tf_op jit(solution)/shard_map/while/body/eval_jaxpr/all_gather | solution.py:122
  278.6 22.7 %all-gather.3 = bf16[32,192,40]{1,2,0:T(8,128)(2,1)S(1)} all-gather(bf16[1,192,40]{1,2,0:T(8,128)(2,1)S(1)} %fusion.109), channel_id=1, replica_groups=mesh['section'=16,'tensor'=32] {'tensor'}, dimensions={0}, use_global_device_ids=true | all-gather | bytes 506880 | tf_op jit(solution)/shard_map/while/body/eval_jaxpr/all_gather | solution.py:114
  302.2 9.9 conditional.5
  312.1 24.1 %all_gather.22 = bf16[40,4096]{1,0:T(8,128)(2,1)S(1)} all-gather(bf16[40,128]{1,0:T(8,128)(2,1)S(1)} %get-tuple-element.754), channel_id=1, replica_groups=mesh['section'=16,'tensor'=32] {'tensor'}, dimensions={1}, use_global_device_ids=true | all-gather | bytes 337920 | tf_op jit(solution)/shard_map/while/body/eval_jaxpr/all_gather | solution.py:122
  345.5 23.3 %all-gather.3 = bf16[32,192,40]{1,2,0:T(8,128)(2,1)S(1)} all-gather(bf16[1,192,40]{1,2,0:T(8,128)(2,1)S(1)} %fusion.109), channel_id=1, replica_groups=mesh['section'=16,'tensor'=32] {'tensor'}, dimensions={0}, use_global_device_ids=true | all-gather | bytes 506880 | tf_op jit(solution)/shard_map/while/body/eval_jaxpr/all_gather | solution.py:114
  369.7 9.9 conditional.5
  379.6 24.1 %all_gather.22 = bf16[40,4096]{1,0:T(8,128)(2,1)S(1)} all-gather(bf16[40,128]{1,0:T(8,128)(2,1)S(1)} %get-tuple-element.754), channel_id=1, replica_groups=mesh['section'=16,'tensor'=32] {'tensor'}, dimensions={1}, use_global_device_ids=true | all-gather | bytes 337920 | tf_op jit(solution)/shard_map/while/body/eval_jaxpr/all_gather | solution.py:122
  413.1 23.3 %all-gather.3 = bf16[32,192,40]{1,2,0:T(8,128)(2,1)S(1)} all-gather(bf16[1,192,40]{1,2,0:T(8,128)(2,1)S(1)} %fusion.109), channel_id=1, replica_groups=mesh['section'=16,'tensor'=32] {'tensor'}, dimensions={0}, use_global_device_ids=true | all-gather | bytes 506880 | tf_op jit(solution)/shard_map/while/body/eval_jaxpr/all_gather | solution.py:114
  437.4 9.9 conditional.5
  447.3 24.1 %all_gather.22 = bf16[40,4096]{1,0:T(8,128)(2,1)S(1)} all-gather(bf16[40,128]{1,0:T(8,128)(2,1)S(1)} %get-tuple-element.754), channel_id=1, replica_groups=mesh['section'=16,'tensor'=32] {'tensor'}, dimensions={1}, use_global_device_ids=true | all-gather | bytes 337920 | tf_op jit(solution)/shard_map/while/body/eval_jaxpr/all_gather | solution.py:122
  481.0 23.7 %all-gather.3 = bf16[32,192,40]{1,2,0:T(8,128)(2,1)S(1)} all-gather(bf16[1,192,40]{1,2,0:T(8,128)(2,1)S(1)} %fusion.109), channel_id=1, replica_groups=mesh['section'=16,'tensor'=32] {'tensor'}, dimensions={0}, use_global_device_ids=true | all-gather | bytes 506880 | tf_op jit(solution)/shard_map/while/body/eval_jaxpr/all_gather | solution.py:114
  505.6 9.9 conditional.5
  515.5 23.8 %all_gather.22 = bf16[40,4096]{1,0:T(8,128)(2,1)S(1)} all-gather(bf16[40,128]{1,0:T(8,128)(2,1)S(1)} %get-tuple-element.754), channel_id=1, replica_groups=mesh['section'=16,'tensor'=32] {'tensor'}, dimensions={1}, use_global_device_ids=true | all-gather | bytes 337920 | tf_op jit(solution)/shard_map/while/body/eval_jaxpr/all_gather | solution.py:122
  548.7 23.7 %all-gather.3 = bf16[32,192,40]{1,2,0:T(8,128)(2,1)S(1)} all-gather(bf16[1,192,40]{1,2,0:T(8,128)(2,1)S(1)} %fusion.109), channel_id=1, replica_groups=mesh['section'=16,'tensor'=32] {'tensor'}, dimensions={0}, use_global_device_ids=true | all-gather | bytes 506880 | tf_op jit(solution)/shard_map/while/body/eval_jaxpr/all_gather | solution.py:114
  573.4 9.9 conditional.5
  583.3 23.7 %all_gather.22 = bf16[40,4096]{1,0:T(8,128)(2,1)S(1)} all-gather(bf16[40,128]{1,0:T(8,128)(2,1)S(1)} %get-tuple-element.754), channel_id=1, replica_groups=mesh['section'=16,'tensor'=32] {'tensor'}, dimensions={1}, use_global_device_ids=true | all-gather | bytes 337920 | tf_op jit(solution)/shard_map/while/body/eval_jaxpr/all_gather | solution.py:122
  616.9 23.8 %all-gather.3 = bf16[32,192,40]{1,2,0:T(8,128)(2,1)S(1)} all-gather(bf16[1,192,40]{1,2,0:T(8,128)(2,1)S(1)} %fusion.109), channel_id=1, replica_groups=mesh['section'=16,'tensor'=32] {'tensor'}, dimensions={0}, use_global_device_ids=true | all-gather | bytes 506880 | tf_op jit(solution)/shard_map/while/body/eval_jaxpr/all_gather | solution.py:114
  641.6 9.9 conditional.5
  651.5 23.6 %all_gather.22 = bf16[40,4096]{1,0:T(8,128)(2,1)S(1)} all-gather(bf16[40,128]{1,0:T(8,128)(2,1)S(1)} %get-tuple-element.754), channel_id=1, replica_groups=mesh['section'=16,'tensor'=32] {'tensor'}, dimensions={1}, use_global_device_ids=true | all-gather | bytes 337920 | tf_op jit(solution)/shard_map/while/body/eval_jaxpr/all_gather | solution.py:122
  677.2 5.2 collective-permute-start
  685.9 23.8 %all-gather.3 = bf16[32,192,40]{1,2,0:T(8,128)(2,1)S(1)} all-gather(bf16[1,192,40]{1,2,0:T(8,128)(2,1)S(1)} %fusion.109), channel_id=1, replica_groups=mesh['section'=16,'tensor'=32] {'tensor'}, dimensions={0}, use_global_device_ids=true | all-gather | bytes 506880 | tf_op jit(solution)/shard_map/while/body/eval_jaxpr/all_gather | solution.py:114
  710.6 9.9 conditional.5
  720.5 23.6 %all_gather.22 = bf16[40,4096]{1,0:T(8,128)(2,1)S(1)} all-gather(bf16[40,128]{1,0:T(8,128)(2,1)S(1)} %get-tuple-element.754), channel_id=1, replica_groups=mesh['section'=16,'tensor'=32] {'tensor'}, dimensions={1}, use_global_device_ids=true | all-gather | bytes 337920 | tf_op jit(solution)/shard_map/while/body/eval_jaxpr/all_gather | solution.py:122
  754.6 23.9 %all-gather.3 = bf16[32,192,40]{1,2,0:T(8,128)(2,1)S(1)} all-gather(bf16[1,192,40]{1,2,0:T(8,128)(2,1)S(1)} %fusion.109), channel_id=1, replica_groups=mesh['section'=16,'tensor'=32] {'tensor'}, dimensions={0}, use_global_device_ids=true | all-gather | bytes 506880 | tf_op jit(solution)/shard_map/while/body/eval_jaxpr/all_gather | solution.py:114
  779.3 9.9 conditional.5
  789.2 23.6 %all_gather.22 = bf16[40,4096]{1,0:T(8,128)(2,1)S(1)} all-gather(bf16[40,128]{1,0:T(8,128)(2,1)S(1)} %get-tuple-element.754), channel_id=1, replica_groups=mesh['section'=16,'tensor'=32] {'tensor'}, dimensions={1}, use_global_device_ids=true | all-gather | bytes 337920 | tf_op jit(solution)/shard_map/while/body/eval_jaxpr/all_gather | solution.py:122
  814.8 5.1 collective-permute-start
  823.4 23.9 %all-gather.3 = bf16[32,192,40]{1,2,0:T(8,128)(2,1)S(1)} all-gather(bf16[1,192,40]{1,2,0:T(8,128)(2,1)S(1)} %fusion.109), channel_id=1, replica_groups=mesh['section'=16,'tensor'=32] {'tensor'}, dimensions={0}, use_global_device_ids=true | all-gather | bytes 506880 | tf_op jit(solution)/shard_map/while/body/eval_jaxpr/all_gather | solution.py:114
  848.2 9.9 conditional.5
  858.1 23.5 %all_gather.22 = bf16[40,4096]{1,0:T(8,128)(2,1)S(1)} all-gather(bf16[40,128]{1,0:T(8,128)(2,1)S(1)} %get-tuple-element.754), channel_id=1, replica_groups=mesh['section'=16,'tensor'=32] {'tensor'}, dimensions={1}, use_global_device_ids=true | all-gather | bytes 337920 | tf_op jit(solution)/shard_map/while/body/eval_jaxpr/all_gather | solution.py:122
  883.6 5.1 collective-permute-start
  892.2 23.9 %all-gather.3 = bf16[32,192,40]{1,2,0:T(8,128)(2,1)S(1)} all-gather(bf16[1,192,40]{1,2,0:T(8,128)(2,1)S(1)} %fusion.109), channel_id=1, replica_groups=mesh['section'=16,'tensor'=32] {'tensor'}, dimensions={0}, use_global_device_ids=true | all-gather | bytes 506880 | tf_op jit(solution)/shard_map/while/body/eval_jaxpr/all_gather | solution.py:114
  917.0 9.9 conditional.5
  926.9 23.5 %all_gather.22 = bf16[40,4096]{1,0:T(8,128)(2,1)S(1)} all-gather(bf16[40,128]{1,0:T(8,128)(2,1)S(1)} %get-tuple-element.754), channel_id=1, replica_groups=mesh['section'=16,'tensor'=32] {'tensor'}, dimensions={1}, use_global_device_ids=true | all-gather | bytes 337920 | tf_op jit(solution)/shard_map/while/body/eval_jaxpr/all_gather | solution.py:122
  952.4 5.1 collective-permute-start
  961.0 23.9 %all-gather.3 = bf16[32,192,40]{1,2,0:T(8,128)(2,1)S(1)} all-gather(bf16[1,192,40]{1,2,0:T(8,128)(2,1)S(1)} %fusion.109), channel_id=1, replica_groups=mesh['section'=16,'tensor'=32] {'tensor'}, dimensions={0}, use_global_device_ids=true | all-gather | bytes 506880 | tf_op jit(solution)/shard_map/while/body/eval_jaxpr/all_gather | solution.py:114
  985.9 9.9 conditional.5
  995.8 23.5 %all_gather.22 = bf16[40,4096]{1,0:T(8,128)(2,1)S(1)} all-gather(bf16[40,128]{1,0:T(8,128)(2,1)S(1)} %get-tuple-element.754), channel_id=1, replica_groups=mesh['section'=16,'tensor'=32] {'tensor'}, dimensions={1}, use_global_device_ids=true | all-gather | bytes 337920 | tf_op jit(solution)/shard_map/while/body/eval_jaxpr/all_gather | solution.py:122
  1021.3 5.1 collective-permute-start
  1029.8 23.9 %all-gather.3 = bf16[32,192,40]{1,2,0:T(8,128)(2,1)S(1)} all-gather(bf16[1,192,40]{1,2,0:T(8,128)(2,1)S(1)} %fusion.109), channel_id=1, replica_groups=mesh['section'=16,'tensor'=32] {'tensor'}, dimensions={0}, use_global_device_ids=true | all-gather | bytes 506880 | tf_op jit(solution)/shard_map/while/body/eval_jaxpr/all_gather | solution.py:114
  1054.7 9.9 conditional.5
  1064.6 23.5 %all_gather.22 = bf16[40,4096]{1,0:T(8,128)(2,1)S(1)} all-gather(bf16[40,128]{1,0:T(8,128)(2,1)S(1)} %get-tuple-element.754), channel_id=1, replica_groups=mesh['section'=16,'tensor'=32] {'tensor'}, dimensions={1}, use_global_device_ids=true | all-gather | bytes 337920 | tf_op jit(solution)/shard_map/while/body/eval_jaxpr/all_gather | solution.py:122
  1098.7 23.9 %all-gather.3 = bf16[32,192,40]{1,2,0:T(8,128)(2,1)S(1)} all-gather(bf16[1,192,40]{1,2,0:T(8,128)(2,1)S(1)} %fusion.109), channel_id=1, replica_groups=mesh['section'=16,'tensor'=32] {'tensor'}, dimensions={0}, use_global_device_ids=true | all-gather | bytes 506880 | tf_op jit(solution)/shard_map/while/body/eval_jaxpr/all_gather | solution.py:114
  1123.5 9.9 conditional.5
  1133.4 23.5 %all_gather.22 = bf16[40,4096]{1,0:T(8,128)(2,1)S(1)} all-gather(bf16[40,128]{1,0:T(8,128)(2,1)S(1)} %get-tuple-element.754), channel_id=1, replica_groups=mesh['section'=16,'tensor'=32] {'tensor'}, dimensions={1}, use_global_device_ids=true | all-gather | bytes 337920 | tf_op jit(solution)/shard_map/while/body/eval_jaxpr/all_gather | solution.py:122
  1167.5 24.0 %all-gather.3 = bf16[32,192,40]{1,2,0:T(8,128)(2,1)S(1)} all-gather(bf16[1,192,40]{1,2,0:T(8,128)(2,1)S(1)} %fusion.109), channel_id=1, replica_groups=mesh['section'=16,'tensor'=32] {'tensor'}, dimensions={0}, use_global_device_ids=true | all-gather | bytes 506880 | tf_op jit(solution)/shard_map/while/body/eval_jaxpr/all_gather | solution.py:114
  1192.4 9.9 conditional.5
  1202.3 23.4 %all_gather.22 = bf16[40,4096]{1,0:T(8,128)(2,1)S(1)} all-gather(bf16[40,128]{1,0:T(8,128)(2,1)S(1)} %get-tuple-element.754), channel_id=1, replica_groups=mesh['section'=16,'tensor'=32] {'tensor'}, dimensions={1}, use_global_device_ids=true | all-gather | bytes 337920 | tf_op jit(solution)/shard_map/while/body/eval_jaxpr/all_gather | solution.py:122
  1236.3 24.0 %all-gather.3 = bf16[32,192,40]{1,2,0:T(8,128)(2,1)S(1)} all-gather(bf16[1,192,40]{1,2,0:T(8,128)(2,1)S(1)} %fusion.109), channel_id=1, replica_groups=mesh['section'=16,'tensor'=32] {'tensor'}, dimensions={0}, use_global_device_ids=true | all-gather | bytes 506880 | tf_op jit(solution)/shard_map/while/body/eval_jaxpr/all_gather | solution.py:114
  1261.2 9.9 conditional.5
  1271.1 23.4 %all_gather.22 = bf16[40,4096]{1,0:T(8,128)(2,1)S(1)} all-gather(bf16[40,128]{1,0:T(8,128)(2,1)S(1)} %get-tuple-element.754), channel_id=1, replica_groups=mesh['section'=16,'tensor'=32] {'tensor'}, dimensions={1}, use_global_device_ids=true | all-gather | bytes 337920 | tf_op jit(solution)/shard_map/while/body/eval_jaxpr/all_gather | solution.py:122
  1302.9 107.2 %psum.7 = f32[8]{0:T(128)S(1)} all-reduce(f32[8]{0:T(128)S(1)} %broadcast_multiply_fusion.4), channel_id=1, replica_groups=mesh['section'=16,'tensor'=32] {'section','tensor'}, use_global_device_ids=true, to_apply=%region_28.29 | all-reduce | flops 8 | bytes 64 | tf_op jit(solution)/shard_map/psum | solution.py:146
  (722 shorter events, 333.6 us)
Async XLA Ops:
  0.6 4.0 copy-start.3
  0.6 4.2 copy-start
  0.7 4.2 copy-start.1
  0.7 4.2 copy-start.2
  0.7 4.2 copy-start.5
  4.9 1297.8 %copy-start.4 = (bf16[128,192]{0,1:T(8,128)(2,1)S(1)}, bf16[128,192]{0,1:T(8,128)(2,1)}, u32[]{:S(2)}) copy-start(bf16[128,192]{0,1:T(8,128)(2,1)} %param.31) | copy-start | bytes 147460
  72.0 2.8 collective-permute-start
  136.9 3.7 collective-permute-start
  202.9 5.4 collective-permute-start
  270.5 5.5 collective-permute-start
  338.2 4.7 collective-permute-start
  405.7 4.8 collective-permute-start
  473.4 5.1 collective-permute-start
  541.3 4.9 collective-permute-start
  609.0 5.4 collective-permute-start
  677.2 6.1 collective-permute-start
  746.1 5.9 collective-permute-start
  814.8 6.0 collective-permute-start
  883.6 6.0 collective-permute-start
  952.4 6.0 collective-permute-start
  1021.3 6.0 collective-permute-start
  1090.1 6.0 collective-permute-start
  1158.9 6.0 collective-permute-start
  1227.7 6.0 collective-permute-start
  1296.5 6.0 collective-permute-start
where the time goes:
time: 1420 us; the launch traced here: 1410 us
  blocking collectives  1010 us (71%)
  local copies, waits for them, and re-layouts  126 us (9%)
  matrix products  114 us (8%)
  starting transfers between devices  83.1 us (6%)
  loops' own time  39.8 us (3%)
  other arithmetic  23.9 us (2%)
    all_gather x19, blocking collectives, advance(): lax.all_gather(part, 'tensor', axis=1, tiled=True)  452 us
    all_gather x19, blocking collectives, advance(): full_rows = lax.all_gather(own_rows, 'tensor', axis=1, tiled=True)  452 us
    psum x1, blocking collectives, local(): totals = lax.psum(partial_sums * last_flag, ('section', 'tensor'))  107 us
    ppermute x19, starting transfers between devices, from_behind(): lax.ppermute(value, axis, [(source, source + steps) for source in range(f...  83.1 us
    dot_general x19, matrix products, add_heads(): return total + jnp.dot(piece, rows_w, preferred_element_type=jnp.float32)  38.1 us
    another operation x1, loops' own time, local(): lax.fori_loop(0, section_count + slice_total - 1, advance, initial)  38.1 us
    dot_general x19, matrix products, branch(): jnp.dot(normed, val_weight, preferred_element_type=jnp.float32)  34.3 us
    scatter x19, local copies, waits for them, and re-layouts, branch(): key_cache.at[begin:finish].set(key_rows.reshape(length, inner_own))  28.5 us
  transfers between devices with their start and end apart: 19, of which 15 were waited for; matrix products, arithmetic and copies ran while one was open for 0% of the time, Pallas kernels for 0%

commit v1 on v0

v1 whole, which is shorter than its diff:
```python
import functools

import jax
import jax.numpy as jnp
from jax import lax
from jax.experimental import pallas as pl
from jax.experimental.pallas import tpu as pltpu
from jax.sharding import Mesh
from jax.sharding import PartitionSpec as P

D = 6144
HD = 64
DOCS = 8
MOST = 32
NEG = -1e30
PLANE = ("y", "x")


def qkv_attention(order_ref, rows_ref, gain_ref, w_ref, bias_ref, kin_ref, vin_ref, send_ref, kout_ref, vout_ref):
    chips, length, cols = rows_ref.shape
    width = kin_ref.shape[1]
    heads = width // HD
    total = jnp.zeros((length, cols), jnp.float32)
    for chip in range(chips):
        total += rows_ref[chip].astype(jnp.float32)
    mean = jnp.sum(total, -1, keepdims=True) / (chips * cols)
    total = jnp.zeros((length, cols), jnp.float32)
    for chip in range(chips):
        centered = rows_ref[chip].astype(jnp.float32) - mean
        total += centered * centered
    scale = lax.rsqrt(jnp.sum(total, -1, keepdims=True) / (chips * cols) + 1e-05)
    acc = jnp.zeros((length, 2 * width), jnp.float32)
    for chip in range(chips):
        centered = rows_ref[chip].astype(jnp.float32) - mean
        normed = (centered * scale * gain_ref[chip : chip + 1, :]).astype(jnp.bfloat16)
        acc += jnp.dot(normed, w_ref[chip * cols : (chip + 1) * cols, :], preferred_element_type=jnp.float32)
    rounded = acc.astype(jnp.bfloat16).astype(jnp.float32)
    qk, val = rounded[:, :width], rounded[:, width:]
    head_of = lax.broadcasted_iota(jnp.int32, (length, width), 1) // HD
    squares = qk * qk
    inverse = jnp.zeros((length, width), jnp.float32)
    stack = []
    for head in range(heads):
        mine = head_of == head
        square_mean = jnp.sum(jnp.where(mine, squares, 0.0), -1, keepdims=True) / HD
        inverse = jnp.where(mine, lax.rsqrt(square_mean + 1e-06), inverse)
        stack.append(jnp.where(mine, qk, 0.0))
    key = (qk * inverse).astype(jnp.bfloat16).astype(jnp.float32)
    queries = jnp.concatenate(stack, 0).astype(jnp.bfloat16)
    keys = jnp.concatenate([kin_ref[...], key], 0).astype(jnp.bfloat16)
    vals = jnp.concatenate([vin_ref[...], val], 0).astype(jnp.bfloat16)
    scores = lax.dot_general(queries, keys, (((1,), (1,)), ((), ())), preferred_element_type=jnp.float32) / HD
    scores = scores + bias_ref[order_ref[0]]
    peak = jnp.max(scores, -1, keepdims=True)
    expo = jnp.exp(scores - peak)
    weights = (expo / jnp.sum(expo, -1, keepdims=True)).astype(jnp.bfloat16)
    mixed = jnp.dot(weights, vals, preferred_element_type=jnp.float32)
    attended = jnp.zeros((length, width), jnp.float32)
    for head in range(heads):
        attended = jnp.where(head_of == head, mixed[head * length : (head + 1) * length], attended)
    attended = attended.astype(jnp.bfloat16)
    for chip in range(chips):
        send_ref[chip] = attended
    kout_ref[...] = key
    vout_ref[...] = val


def project_out(heads_ref, w_ref, rows_ref, out_ref):
    chips, _, width = heads_ref.shape
    acc = rows_ref[...].astype(jnp.float32)
    mixed = jnp.zeros(acc.shape, jnp.float32)
    for chip in range(chips):
        mixed += jnp.dot(
            heads_ref[chip], w_ref[chip * width : (chip + 1) * width, :], preferred_element_type=jnp.float32
        )
    out_ref[...] = (acc + mixed).astype(jnp.bfloat16)


def local(tokens, targets, doc_ids, norm_gains, w_qk, w_val, w_out):
    section = lax.axis_index("section")
    section_count = lax.axis_size("section")
    core = lax.axis_index("core")
    chips = lax.axis_size("y") * lax.axis_size("x")
    row_count, cols_own = tokens.shape
    cols = 2 * cols_own
    width = 2 * w_qk.shape[2]
    heads = width // HD
    slices = 2
    length = (row_count // 2 + MOST // 2) // slices
    part = slices * length

    def swap(value):
        return lax.ppermute(value, "core", [(0, 1), (1, 0)])

    def both(own, other):
        return [jnp.where(core == 0, own, other), jnp.where(core == 0, other, own)]

    position = jnp.arange(row_count, dtype=jnp.int32)
    previous = jnp.concatenate([doc_ids[:1] - 1, doc_ids[:-1]])
    far = jnp.abs(position - row_count // 2) * row_count + position
    cut = jnp.min(jnp.where(doc_ids != previous, far, row_count * row_count)) % row_count
    start = jnp.where(core == 0, 0, cut)
    count = jnp.where(core == 0, cut, row_count - cut)
    place = jnp.arange(part, dtype=jnp.int32)
    pick = ((start + place)[:, None] == position[None, :]) & (place < count)[:, None]
    pick_bf = pick.astype(jnp.bfloat16)

    def picked(rows):
        return jnp.dot(pick_bf, rows, preferred_element_type=jnp.float32)

    tokens_chip = jnp.concatenate(both(tokens, swap(tokens)), 1)
    first_rows = picked(tokens_chip).astype(jnp.bfloat16)
    docs = jnp.sum(jnp.where(pick, doc_ids[None, :], 0), 1)
    docs = jnp.where(place < count, docs, DOCS)
    same = (docs[:, None] == docs[None, :]) & (place[None, :] <= place[:, None])
    allowed = jnp.stack(
        [
            jnp.concatenate([jnp.zeros((length, length), bool), same[:length, :length]], 1),
            same[length:],
        ]
    )
    bias = jnp.tile(jnp.where(allowed, 0.0, NEG).astype(jnp.float32), (1, heads, 1))

    w_in = jnp.concatenate(both(w_qk[0], swap(w_qk[0])) + both(w_val[0], swap(w_val[0])), 1)
    w_last = jnp.concatenate(both(w_out[0], swap(w_out[0])), 1)
    gains = norm_gains[0].reshape(chips, cols)

    vmem = pl.BlockSpec(memory_space=pltpu.VMEM)
    smem = pl.BlockSpec(memory_space=pltpu.SMEM)
    params = pltpu.CompilerParams(vmem_limit_bytes=32 * 1024 * 1024)
    attend = pl.pallas_call(
        qkv_attention,
        out_shape=(
            jax.ShapeDtypeStruct((chips, length, width), jnp.bfloat16),
            jax.ShapeDtypeStruct((length, width), jnp.float32),
            jax.ShapeDtypeStruct((length, width), jnp.float32),
        ),
        in_specs=[smem] + [vmem] * 6,
        out_specs=(vmem,) * 3,
        compiler_params=params,
        cost_estimate=pl.CostEstimate(
            flops=2 * length * D * 2 * width, bytes_accessed=4 * D * width, transcendentals=heads * length * part
        ),
    )
    project = pl.pallas_call(
        project_out,
        out_shape=jax.ShapeDtypeStruct((length, cols), jnp.bfloat16),
        in_specs=[vmem] * 3,
        out_specs=vmem,
        compiler_params=params,
        cost_estimate=pl.CostEstimate(
            flops=2 * length * chips * width * cols, bytes_accessed=2 * chips * width * cols, transcendentals=0
        ),
    )

    keys = jnp.zeros((length, width), jnp.float32)
    vals = jnp.zeros((length, width), jnp.float32)
    done = [jnp.zeros((length, cols), jnp.bfloat16) for _ in range(slices)]
    received = jnp.zeros((length, cols), jnp.bfloat16)
    for step in range(section_count + slices - 1):
        order = step - section
        turn = jnp.clip(order, 0, slices - 1)
        mine = min(step, slices - 1)
        rows = jnp.where(section == 0, first_rows[mine * length : (mine + 1) * length], received)
        gathered = lax.all_to_all(
            jnp.broadcast_to(rows[None], (chips,) + rows.shape), PLANE, 0, 0, tiled=True
        )
        send, keys, vals = attend(turn.reshape(1), gathered, gains, w_in, bias, keys, vals)
        attended = lax.all_to_all(send, PLANE, 0, 0, tiled=True)
        rows = project(attended, w_last, rows)
        if step < section_count + slices - 2:
            received = lax.ppermute(rows, "section", [(z, z + 1) for z in range(section_count - 1)])
        done = [jnp.where(order == number, rows, kept) for number, kept in enumerate(done)]

    part_rows = jnp.concatenate(done, 0)
    targets_chip = jnp.concatenate(both(targets, swap(targets)), 1)
    diff = part_rows.astype(jnp.float32) - picked(targets_chip)
    token_sums = jnp.sum(diff * diff, -1)
    doc_names = jnp.arange(128, dtype=jnp.int32)[None, :]
    in_doc = docs[:, None] == doc_names
    sums = jnp.sum(jnp.where(in_doc, token_sums[:, None], 0.0), 0)
    sums = jnp.where((section == section_count - 1) & (doc_names[0] < DOCS), sums, 0.0)

    def share(value, axes):
        number = 1
        for axis in axes:
            number *= lax.axis_size(axis)
        pieces = jnp.broadcast_to(value[None], (number,) + value.shape)
        return jnp.sum(lax.all_to_all(pieces, axes, 0, 0, tiled=True), 0)

    totals = share(share(sums[None], ("y", "x", "core")), ("section",))[0, :DOCS]
    doc_counts = jnp.sum((doc_ids[:, None] == jnp.arange(DOCS, dtype=jnp.int32)[None, :]).astype(jnp.float32), 0)
    losses = totals / (doc_counts * D)

    halves = [part_rows[:, :cols_own], part_rows[:, cols_own:]]
    keep = jnp.where(core == 0, halves[0], halves[1])
    give = jnp.where(core == 0, halves[1], halves[0])
    stacked = jnp.concatenate(both(keep, swap(give)), 0)
    source = jnp.where(position < cut, position, position - cut + part)
    back = (source[:, None] == jnp.arange(2 * part, dtype=jnp.int32)[None, :]).astype(jnp.bfloat16)
    section_rows = jnp.dot(back, stacked, preferred_element_type=jnp.float32).astype(jnp.bfloat16)
    return (section_rows[None], losses)


def solution(mesh):
    names = ("section", "y", "x", "core")
    fine = Mesh(mesh.devices.reshape(mesh.devices.shape[0], 4, 4, 2), names)
    tensor = ("y", "x", "core")
    placed = (
        P(None, tensor),
        P(None, tensor),
        P(),
        P("section", None),
        P("section", None, tensor),
        P("section", None, tensor),
        P("section", None, tensor),
    )
    return jax.shard_map(
        local,
        mesh=fine,
        in_specs=placed,
        out_specs=(P("section", None, tensor), P()),
        check_vma=False,
    )
```

time: 1420 us -> 793 us (0.56)
  blocking collectives: 1010 us -> 164 us
  starting transfers between devices: 83.1 us -> 261 us
  waiting for transfers between devices: 12.5 us -> 176 us
  matrix products: 114 us -> 1.43 us
  Pallas kernels: 0 us -> 62.6 us
  loops' own time: 39.8 us -> 0 us
  local copies, waits for them, and re-layouts: 126 us -> 90.6 us
    all_gather x38 -> x0, blocking collectives: 904 us -> none  [the longest x19 452 us: advance(): lax.all_gather(part, 'tensor', axis=1, tiled=True)]
    all_to_all x0 -> x15, blocking collectives: none -> 164 us  [local(): attended = lax.all_to_all(send, PLANE, 0, 0, tiled=True)]
    all_to_all x0 -> x21, waiting for transfers between devices: none -> 160 us  [the longest x17 139 us: local(): lax.all_to_all(jnp.broadcast_to(rows[None], (chips,) + rows.shape), PLANE...]
    all_to_all x0 -> x21, starting transfers between devices: none -> 114 us  [the longest x17 73.7 us: local(): lax.all_to_all(jnp.broadcast_to(rows[None], (chips,) + rows.shape), PLANE...]
    dot_general x95 -> x3, matrix products: 114 us -> 1.43 us  [the longest x1 0.9 us: local(): jnp.dot(back, stacked, preferred_element_type=jnp.float32)]
    psum x1 -> x0, blocking collectives: 107 us -> none  [local(): totals = lax.psum(partial_sums * last_flag, ('section', 'tensor'))]
    unnamed x14 -> x236, local copies, waits for them, and re-layouts: 4.12 us -> 71.1 us
    ppermute x19 -> x22, starting transfers between devices: 83.1 us -> 147 us  [the longest x6 75.5 us: swap(): return lax.ppermute(value, 'core', [(0, 1), (1, 0)])]
  transfers between devices with their start and end apart: 19 -> 43, of which waited for: 15 -> 36; matrix products, arithmetic and copies ran while one was open for 0% -> 3% of each run, Pallas kernels for 0% -> 1%
where the time goes in v1:
time: 793 us; the launch traced here: 778 us
  starting transfers between devices  261 us (33%)
  waiting for transfers between devices  176 us (22%)
  blocking collectives  164 us (21%)
  local copies, waits for them, and re-layouts  90.6 us (11%)
  Pallas kernels  62.6 us (8%)
  other arithmetic  16.7 us (2%)
    all_to_all x15, blocking collectives, local(): attended = lax.all_to_all(send, PLANE, 0, 0, tiled=True)  164 us
    all_to_all x17, waiting for transfers between devices, local(): lax.all_to_all(jnp.broadcast_to(rows[None], (chips,) + rows.shape), PLANE...  139 us
    ppermute x6, starting transfers between devices, swap(): return lax.ppermute(value, 'core', [(0, 1), (1, 0)])  75.5 us
    all_to_all x17, starting transfers between devices, local(): lax.all_to_all(jnp.broadcast_to(rows[None], (chips,) + rows.shape), PLANE...  73.7 us
    ppermute x16, starting transfers between devices, local(): lax.ppermute(rows, 'section', [(z, z + 1) for z in range(section_count -...  71.2 us
    unnamed x236, local copies, waits for them, and re-layouts  71.1 us
    pallas_call x17, Pallas kernels, local(): attend(turn.reshape(1), gathered, gains, w_in, bias, keys, vals)  52.2 us
    all_to_all x2, starting transfers between devices, share(): return jnp.sum(lax.all_to_all(pieces, axes, 0, 0, tiled=True), 0)  29.5 us
  transfers between devices with their start and end apart: 43, of which 36 were waited for; matrix products, arithmetic and copies ran while one was open for 3% of the time, Pallas kernels for 1%

profile of v1, /device:TPU:1, one launch (start us, length us, event | category | flops | bytes accessed | tf_op | source)
XLA Modules:
  0.0 778.2 jit_solution(198992488161700864)
XLA Ops:
  0.6 8.9 %collective-permute-start = (bf16[128,192]{0,1:T(8,128)(2,1)}, bf16[128,192]{0,1:T(8,128)(2,1)S(1)}, u32[]{:S(2)}, u32[]{:S(2)}) collective-permute-start(bf16[128,192]{0,1:T(8,128)(2,1)} %param.7), channel_id=1, source_target_pairs={{0,1},{1,0},{2,3},{3,2},{4,5},{5,4},{6,7},{7,6},{8,9},{9,8},{10,11... | collective-permute-start | bytes 147464 | tf_op jit(solution)/shard_map/ppermute | solution.py:93
  63.0 5.8 all-to-all-start.2
  68.9 8.9 %all-to-all-done.2.rows_ref = bf16[16,40,384]{2,1,0:T(8,128)(2,1)} async-done(((bf16[16,40,384]{2,1,0:T(8,128)(2,1)}), bf16[16,40,384]{2,1,0:T(8,128)(2,1)}, u32[]{:S(2)}, u32[]{:S(2)}) %all-to-all-start.2) | async-done | bytes 491552 | tf_op jit(solution)/shard_map/all_to_all | solution.py:165
  83.6 10.7 %all_to_all.180.heads_ref = bf16[16,40,256]{2,1,0:T(8,128)(2,1)S(1)} all-to-all(bf16[16,40,256]{2,1,0:T(8,128)(2,1)S(1)} %get-tuple-element.54), channel_id=1, replica_groups=mesh['section'=16,'y'=4,'x'=4,'core'=2] {'y','x'}, dimensions={0} | all-to-all | bytes 655360 | tf_op jit(solution)/shard_map/all_to_all | solution.py:169
  100.5 4.2 all-to-all-start.4
  104.7 8.8 %all-to-all-done.4.rows_ref = bf16[16,40,384]{2,1,0:T(8,128)(2,1)} async-done(((bf16[16,40,384]{2,1,0:T(8,128)(2,1)}), bf16[16,40,384]{2,1,0:T(8,128)(2,1)}, u32[]{:S(2)}, u32[]{:S(2)}) %all-to-all-start.4) | async-done | bytes 491552 | tf_op jit(solution)/shard_map/all_to_all | solution.py:165
  121.0 10.7 %all_to_all.181.heads_ref = bf16[16,40,256]{2,1,0:T(8,128)(2,1)S(1)} all-to-all(bf16[16,40,256]{2,1,0:T(8,128)(2,1)S(1)} %get-tuple-element.57), channel_id=1, replica_groups=mesh['section'=16,'y'=4,'x'=4,'core'=2] {'y','x'}, dimensions={0} | all-to-all | bytes 655360 | tf_op jit(solution)/shard_map/all_to_all | solution.py:169
  138.0 4.7 all-to-all-start.6
  142.7 8.8 %all-to-all-done.6.rows_ref = bf16[16,40,384]{2,1,0:T(8,128)(2,1)} async-done(((bf16[16,40,384]{2,1,0:T(8,128)(2,1)}), bf16[16,40,384]{2,1,0:T(8,128)(2,1)}, u32[]{:S(2)}, u32[]{:S(2)}) %all-to-all-start.6) | async-done | bytes 491552 | tf_op jit(solution)/shard_map/all_to_all | solution.py:165
  158.2 10.7 %all_to_all.182.heads_ref = bf16[16,40,256]{2,1,0:T(8,128)(2,1)S(1)} all-to-all(bf16[16,40,256]{2,1,0:T(8,128)(2,1)S(1)} %get-tuple-element.60), channel_id=1, replica_groups=mesh['section'=16,'y'=4,'x'=4,'core'=2] {'y','x'}, dimensions={0} | all-to-all | bytes 655360 | tf_op jit(solution)/shard_map/all_to_all | solution.py:169
  175.4 4.2 all-to-all-start.8
  179.6 8.8 %all-to-all-done.8.rows_ref = bf16[16,40,384]{2,1,0:T(8,128)(2,1)} async-done(((bf16[16,40,384]{2,1,0:T(8,128)(2,1)}), bf16[16,40,384]{2,1,0:T(8,128)(2,1)}, u32[]{:S(2)}, u32[]{:S(2)}) %all-to-all-start.8) | async-done | bytes 491552 | tf_op jit(solution)/shard_map/all_to_all | solution.py:165
  195.9 10.7 %all_to_all.183.heads_ref = bf16[16,40,256]{2,1,0:T(8,128)(2,1)S(1)} all-to-all(bf16[16,40,256]{2,1,0:T(8,128)(2,1)S(1)} %get-tuple-element.63), channel_id=1, replica_groups=mesh['section'=16,'y'=4,'x'=4,'core'=2] {'y','x'}, dimensions={0} | all-to-all | bytes 655360 | tf_op jit(solution)/shard_map/all_to_all | solution.py:169
  207.1 5.1 collective-permute-start.8
  214.1 4.2 all-to-all-start.10
  218.3 8.8 %all-to-all-done.10.rows_ref = bf16[16,40,384]{2,1,0:T(8,128)(2,1)} async-done(((bf16[16,40,384]{2,1,0:T(8,128)(2,1)}), bf16[16,40,384]{2,1,0:T(8,128)(2,1)}, u32[]{:S(2)}, u32[]{:S(2)}) %all-to-all-start.10) | async-done | bytes 491552 | tf_op jit(solution)/shard_map/all_to_all | solution.py:165
  233.8 12.8 %all_to_all.184.heads_ref = bf16[16,40,256]{2,1,0:T(8,128)(2,1)S(1)} all-to-all(bf16[16,40,256]{2,1,0:T(8,128)(2,1)S(1)} %get-tuple-element.66), channel_id=1, replica_groups=mesh['section'=16,'y'=4,'x'=4,'core'=2] {'y','x'}, dimensions={0} | all-to-all | bytes 655360 | tf_op jit(solution)/shard_map/all_to_all | solution.py:169
  247.2 4.4 collective-permute-start.9
  253.5 4.2 all-to-all-start.12
  257.7 10.5 %all-to-all-done.12.rows_ref = bf16[16,40,384]{2,1,0:T(8,128)(2,1)} async-done(((bf16[16,40,384]{2,1,0:T(8,128)(2,1)}), bf16[16,40,384]{2,1,0:T(8,128)(2,1)}, u32[]{:S(2)}, u32[]{:S(2)}) %all-to-all-start.12) | async-done | bytes 491552 | tf_op jit(solution)/shard_map/all_to_all | solution.py:165
  275.7 10.6 %all_to_all.185.heads_ref = bf16[16,40,256]{2,1,0:T(8,128)(2,1)S(1)} all-to-all(bf16[16,40,256]{2,1,0:T(8,128)(2,1)S(1)} %get-tuple-element.69), channel_id=1, replica_groups=mesh['section'=16,'y'=4,'x'=4,'core'=2] {'y','x'}, dimensions={0} | all-to-all | bytes 655360 | tf_op jit(solution)/shard_map/all_to_all | solution.py:169
  286.9 5.2 collective-permute-start.10
  293.9 4.2 all-to-all-start.14
  298.2 8.9 %all-to-all-done.14.rows_ref = bf16[16,40,384]{2,1,0:T(8,128)(2,1)} async-done(((bf16[16,40,384]{2,1,0:T(8,128)(2,1)}), bf16[16,40,384]{2,1,0:T(8,128)(2,1)}, u32[]{:S(2)}, u32[]{:S(2)}) %all-to-all-start.14) | async-done | bytes 491552 | tf_op jit(solution)/shard_map/all_to_all | solution.py:165
  313.8 10.6 %all_to_all.186.heads_ref = bf16[16,40,256]{2,1,0:T(8,128)(2,1)S(1)} all-to-all(bf16[16,40,256]{2,1,0:T(8,128)(2,1)S(1)} %get-tuple-element.72), channel_id=1, replica_groups=mesh['section'=16,'y'=4,'x'=4,'core'=2] {'y','x'}, dimensions={0} | all-to-all | bytes 655360 | tf_op jit(solution)/shard_map/all_to_all | solution.py:169
  325.0 5.0 collective-permute-start.11
  331.9 4.4 all-to-all-start.16
  336.3 8.8 %all-to-all-done.16.rows_ref = bf16[16,40,384]{2,1,0:T(8,128)(2,1)} async-done(((bf16[16,40,384]{2,1,0:T(8,128)(2,1)}), bf16[16,40,384]{2,1,0:T(8,128)(2,1)}, u32[]{:S(2)}, u32[]{:S(2)}) %all-to-all-start.16) | async-done | bytes 491552 | tf_op jit(solution)/shard_map/all_to_all | solution.py:165
  352.6 10.7 %all_to_all.187.heads_ref = bf16[16,40,256]{2,1,0:T(8,128)(2,1)S(1)} all-to-all(bf16[16,40,256]{2,1,0:T(8,128)(2,1)S(1)} %get-tuple-element.75), channel_id=1, replica_groups=mesh['section'=16,'y'=4,'x'=4,'core'=2] {'y','x'}, dimensions={0} | all-to-all | bytes 655360 | tf_op jit(solution)/shard_map/all_to_all | solution.py:169
  363.8 5.0 collective-permute-start.12
  370.6 4.2 all-to-all-start.18
  374.9 8.8 %all-to-all-done.18.rows_ref = bf16[16,40,384]{2,1,0:T(8,128)(2,1)} async-done(((bf16[16,40,384]{2,1,0:T(8,128)(2,1)}), bf16[16,40,384]{2,1,0:T(8,128)(2,1)}, u32[]{:S(2)}, u32[]{:S(2)}) %all-to-all-start.18) | async-done | bytes 491552 | tf_op jit(solution)/shard_map/all_to_all | solution.py:165
  390.4 10.7 %all_to_all.188.heads_ref = bf16[16,40,256]{2,1,0:T(8,128)(2,1)S(1)} all-to-all(bf16[16,40,256]{2,1,0:T(8,128)(2,1)S(1)} %get-tuple-element.78), channel_id=1, replica_groups=mesh['section'=16,'y'=4,'x'=4,'core'=2] {'y','x'}, dimensions={0} | all-to-all | bytes 655360 | tf_op jit(solution)/shard_map/all_to_all | solution.py:169
  401.6 4.9 collective-permute-start.13
  408.4 4.2 all-to-all-start.20
  412.6 8.8 %all-to-all-done.20.rows_ref = bf16[16,40,384]{2,1,0:T(8,128)(2,1)} async-done(((bf16[16,40,384]{2,1,0:T(8,128)(2,1)}), bf16[16,40,384]{2,1,0:T(8,128)(2,1)}, u32[]{:S(2)}, u32[]{:S(2)}) %all-to-all-start.20) | async-done | bytes 491552 | tf_op jit(solution)/shard_map/all_to_all | solution.py:165
  428.9 10.7 %all_to_all.189.heads_ref = bf16[16,40,256]{2,1,0:T(8,128)(2,1)S(1)} all-to-all(bf16[16,40,256]{2,1,0:T(8,128)(2,1)S(1)} %get-tuple-element.81), channel_id=1, replica_groups=mesh['section'=16,'y'=4,'x'=4,'core'=2] {'y','x'}, dimensions={0} | all-to-all | bytes 655360 | tf_op jit(solution)/shard_map/all_to_all | solution.py:169
  440.1 4.9 collective-permute-start.14
  446.9 4.2 all-to-all-start.22
  451.1 8.8 %all-to-all-done.22.rows_ref = bf16[16,40,384]{2,1,0:T(8,128)(2,1)} async-done(((bf16[16,40,384]{2,1,0:T(8,128)(2,1)}), bf16[16,40,384]{2,1,0:T(8,128)(2,1)}, u32[]{:S(2)}, u32[]{:S(2)}) %all-to-all-start.22) | async-done | bytes 491552 | tf_op jit(solution)/shard_map/all_to_all | solution.py:165
  466.6 11.8 %all_to_all.190.heads_ref = bf16[16,40,256]{2,1,0:T(8,128)(2,1)S(1)} all-to-all(bf16[16,40,256]{2,1,0:T(8,128)(2,1)S(1)} %get-tuple-element.84), channel_id=1, replica_groups=mesh['section'=16,'y'=4,'x'=4,'core'=2] {'y','x'}, dimensions={0} | all-to-all | bytes 655360 | tf_op jit(solution)/shard_map/all_to_all | solution.py:169
  478.9 5.1 collective-permute-start.15
  485.9 4.2 all-to-all-start.24
  490.2 10.3 %all-to-all-done.24.rows_ref = bf16[16,40,384]{2,1,0:T(8,128)(2,1)} async-done(((bf16[16,40,384]{2,1,0:T(8,128)(2,1)}), bf16[16,40,384]{2,1,0:T(8,128)(2,1)}, u32[]{:S(2)}, u32[]{:S(2)}) %all-to-all-start.24) | async-done | bytes 491552 | tf_op jit(solution)/shard_map/all_to_all | solution.py:165
  507.9 12.1 %all_to_all.191.heads_ref = bf16[16,40,256]{2,1,0:T(8,128)(2,1)S(1)} all-to-all(bf16[16,40,256]{2,1,0:T(8,128)(2,1)S(1)} %get-tuple-element.87), channel_id=1, replica_groups=mesh['section'=16,'y'=4,'x'=4,'core'=2] {'y','x'}, dimensions={0} | all-to-all | bytes 655360 | tf_op jit(solution)/shard_map/all_to_all | solution.py:169
  520.6 5.3 collective-permute-start.16
  527.8 4.4 all-to-all-start.26
  532.2 9.0 %all-to-all-done.26.rows_ref = bf16[16,40,384]{2,1,0:T(8,128)(2,1)} async-done(((bf16[16,40,384]{2,1,0:T(8,128)(2,1)}), bf16[16,40,384]{2,1,0:T(8,128)(2,1)}, u32[]{:S(2)}, u32[]{:S(2)}) %all-to-all-start.26) | async-done | bytes 491552 | tf_op jit(solution)/shard_map/all_to_all | solution.py:165
  547.9 10.6 %all_to_all.192.heads_ref = bf16[16,40,256]{2,1,0:T(8,128)(2,1)S(1)} all-to-all(bf16[16,40,256]{2,1,0:T(8,128)(2,1)S(1)} %get-tuple-element.90), channel_id=1, replica_groups=mesh['section'=16,'y'=4,'x'=4,'core'=2] {'y','x'}, dimensions={0} | all-to-all | bytes 655360 | tf_op jit(solution)/shard_map/all_to_all | solution.py:169
  565.1 4.2 all-to-all-start.28
  569.4 8.8 %all-to-all-done.28.rows_ref = bf16[16,40,384]{2,1,0:T(8,128)(2,1)} async-done(((bf16[16,40,384]{2,1,0:T(8,128)(2,1)}), bf16[16,40,384]{2,1,0:T(8,128)(2,1)}, u32[]{:S(2)}, u32[]{:S(2)}) %all-to-all-start.28) | async-done | bytes 491552 | tf_op jit(solution)/shard_map/all_to_all | solution.py:165
  585.6 10.5 %all_to_all.193.heads_ref = bf16[16,40,256]{2,1,0:T(8,128)(2,1)S(1)} all-to-all(bf16[16,40,256]{2,1,0:T(8,128)(2,1)S(1)} %get-tuple-element.93), channel_id=1, replica_groups=mesh['section'=16,'y'=4,'x'=4,'core'=2] {'y','x'}, dimensions={0} | all-to-all | bytes 655360 | tf_op jit(solution)/shard_map/all_to_all | solution.py:169
  596.7 4.7 collective-permute-start.18
  603.3 4.2 all-to-all-start.30
  607.6 8.8 %all-to-all-done.30.rows_ref = bf16[16,40,384]{2,1,0:T(8,128)(2,1)} async-done(((bf16[16,40,384]{2,1,0:T(8,128)(2,1)}), bf16[16,40,384]{2,1,0:T(8,128)(2,1)}, u32[]{:S(2)}, u32[]{:S(2)}) %all-to-all-start.30) | async-done | bytes 491552 | tf_op jit(solution)/shard_map/all_to_all | solution.py:165
  623.9 10.7 %all_to_all.194.heads_ref = bf16[16,40,256]{2,1,0:T(8,128)(2,1)S(1)} all-to-all(bf16[16,40,256]{2,1,0:T(8,128)(2,1)S(1)} %get-tuple-element.96), channel_id=1, replica_groups=mesh['section'=16,'y'=4,'x'=4,'core'=2] {'y','x'}, dimensions={0} | all-to-all | bytes 655360 | tf_op jit(solution)/shard_map/all_to_all | solution.py:169
  635.1 4.4 collective-permute-start.19
  645.6 58.0 %collective-permute-start.21 = (bf16[128,192]{0,1:T(8,128)(2,1)}, bf16[128,192]{0,1:T(8,128)(2,1)}, u32[]{:S(2)}, u32[]{:S(2)}) collective-permute-start(bf16[128,192]{0,1:T(8,128)(2,1)} %param.8), channel_id=1, source_target_pairs={{0,1},{1,0},{2,3},{3,2},{4,5},{5,4},{6,7},{7,6},{8,9},{9,8},{10,11... | collective-permute-start | bytes 147464 | tf_op jit(solution)/shard_map/ppermute | solution.py:93
  711.3 6.8 all-to-all-start.33
  720.2 5.8 all-to-all-done.33.heads_ref
  729.0 9.4 %all-to-all-start.34 = ((f32[32,1,128]{2,1,0:T(1,128)}), f32[32,1,128]{2,1,0:T(1,128)S(1)}, u32[]{:S(2)}, u32[]{:S(2)}) async-start(f32[32,1,128]{2,1,0:T(1,128)} %broadcast_in_dim.111), calls=%async_computation.34 | async-start | bytes 32768 | tf_op jit(solution)/shard_map/all_to_all | solution.py:189
  740.7 4.7 all-to-all-done.34
  746.0 20.1 %all-to-all-start.35 = ((f32[16,1,128]{2,1,0:T(1,128)}), f32[16,1,128]{2,1,0:T(1,128)S(1)}, u32[]{:S(2)}, u32[]{:S(2)}) async-start(f32[16,1,128]{2,1,0:T(1,128)} %broadcast_in_dim.112), calls=%async_computation.35 | async-start | bytes 16384 | tf_op jit(solution)/shard_map/all_to_all | solution.py:189
  767.2 10.3 %all-to-all-done.35 = f32[16,1,128]{2,1,0:T(1,128)S(1)} async-done(((f32[16,1,128]{2,1,0:T(1,128)}), f32[16,1,128]{2,1,0:T(1,128)S(1)}, u32[]{:S(2)}, u32[]{:S(2)}) %all-to-all-start.35) | async-done | bytes 8224 | tf_op jit(solution)/shard_map/all_to_all | solution.py:189
  (378 shorter events, 228.7 us)
Async XLA Ops:
  0.6 24.8 %copy-start.111 = (bf16[128,192]{0,1:T(8,128)(2,1)S(1)}, bf16[128,192]{0,1:T(8,128)(2,1)}, u32[]{:S(2)}) copy-start(bf16[128,192]{0,1:T(8,128)(2,1)} %param.7) | copy-start | bytes 147460
  0.6 24.1 %copy-start.114 = (f32[1,6144]{1,0:T(1,128)S(1)}, f32[1,6144]{1,0:T(1,128)}, u32[]{:S(2)}) copy-start(f32[1,6144]{1,0:T(1,128)} %param.10) | copy-start | bytes 73732
  0.6 24.8 %collective-permute-start = (bf16[128,192]{0,1:T(8,128)(2,1)}, bf16[128,192]{0,1:T(8,128)(2,1)S(1)}, u32[]{:S(2)}, u32[]{:S(2)}) collective-permute-start(bf16[128,192]{0,1:T(8,128)(2,1)} %param.7), channel_id=1, source_target_pairs={{0,1},{1,0},{2,3},{3,2},{4,5},{5,4},{6,7},{7,6},{8,9},{9,8},{10,11... | collective-permute-start | bytes 147464 | tf_op jit(solution)/shard_map/ppermute | solution.py:93
  9.6 20.6 %collective-permute-start.1 = (bf16[6144,128]{1,0:T(8,128)(2,1)}, bf16[6144,128]{1,0:T(8,128)(2,1)}, u32[]{:S(2)}, u32[]{:S(2)}) collective-permute-start(bf16[6144,128]{1,0:T(8,128)(2,1)} %bitcast.59), channel_id=1, source_target_pairs={{0,1},{1,0},{2,3},{3,2},{4,5},{5,4},{6,7},{7,6},{8,9},{9,8},{10,11... | collective-permute-start | bytes 4718600 | tf_op jit(solution)/shard_map/ppermute | solution.py:93
  11.5 20.9 %collective-permute-start.2 = (bf16[6144,128]{1,0:T(8,128)(2,1)}, bf16[6144,128]{1,0:T(8,128)(2,1)}, u32[]{:S(2)}, u32[]{:S(2)}) collective-permute-start(bf16[6144,128]{1,0:T(8,128)(2,1)} %bitcast.60), channel_id=1, source_target_pairs={{0,1},{1,0},{2,3},{3,2},{4,5},{5,4},{6,7},{7,6},{8,9},{9,8},{10,11... | collective-permute-start | bytes 4718600 | tf_op jit(solution)/shard_map/ppermute | solution.py:93
  13.9 36.5 %collective-permute-start.3 = (bf16[4096,192]{0,1:T(8,128)(2,1)}, bf16[4096,192]{0,1:T(8,128)(2,1)}, u32[]{:S(2)}, u32[]{:S(2)}) collective-permute-start(bf16[4096,192]{0,1:T(8,128)(2,1)} %bitcast.58), channel_id=1, source_target_pairs={{0,1},{1,0},{2,3},{3,2},{4,5},{5,4},{6,7},{7,6},{8,9},{9,8},{10,11... | collective-permute-start | bytes 4718600 | tf_op jit(solution)/shard_map/ppermute | solution.py:93
  26.5 14.0 %all-to-all-start = ((bf16[16,40,384]{2,1,0:T(8,128)(2,1)}), bf16[16,40,384]{2,1,0:T(8,128)(2,1)S(1)}, u32[]{:S(2)}, u32[]{:S(2)}) async-start(bf16[16,40,384]{2,1,0:T(8,128)(2,1)} %broadcast_in_dim.80), calls=%async_computation | async-start | bytes 983040 | tf_op jit(solution)/shard_map/all_to_all | solution.py:165
  46.2 12.1 %all-to-all-start.1 = ((bf16[16,40,256]{2,1,0:T(8,128)(2,1)}), bf16[16,40,256]{2,1,0:T(8,128)(2,1)}, u32[]{:S(2)}, u32[]{:S(2)}) async-start(bf16[16,40,256]{2,1,0:T(8,128)(2,1)} %get-tuple-element.51), calls=%async_computation.1 | async-start | bytes 655360 | tf_op jit(solution)/shard_map/all_to_all | solution.py:169
  59.9 2.3 collective-permute-start.4
  63.0 14.7 %all-to-all-start.2 = ((bf16[16,40,384]{2,1,0:T(8,128)(2,1)}), bf16[16,40,384]{2,1,0:T(8,128)(2,1)}, u32[]{:S(2)}, u32[]{:S(2)}) async-start(bf16[16,40,384]{2,1,0:T(8,128)(2,1)} %broadcast_in_dim.86), calls=%async_computation.2 | async-start | bytes 983040 | tf_op jit(solution)/shard_map/all_to_all | solution.py:165
  94.9 4.7 collective-permute-start.5
  100.5 13.1 %all-to-all-start.4 = ((bf16[16,40,384]{2,1,0:T(8,128)(2,1)}), bf16[16,40,384]{2,1,0:T(8,128)(2,1)}, u32[]{:S(2)}, u32[]{:S(2)}) async-start(bf16[16,40,384]{2,1,0:T(8,128)(2,1)} %broadcast_in_dim.87), calls=%async_computation.4 | async-start | bytes 983040 | tf_op jit(solution)/shard_map/all_to_all | solution.py:165
  132.2 26.0 %copy-start.18 = (bf16[40,384]{1,0:T(8,128)(2,1)}, bf16[40,384]{1,0:T(8,128)(2,1)S(1)}, u32[]{:S(2)}) copy-start(bf16[40,384]{1,0:T(8,128)(2,1)S(1)} %shard_map.91) | copy-start | bytes 92164
  132.2 4.9 collective-permute-start.6
  138.0 13.5 %all-to-all-start.6 = ((bf16[16,40,384]{2,1,0:T(8,128)(2,1)}), bf16[16,40,384]{2,1,0:T(8,128)(2,1)}, u32[]{:S(2)}, u32[]{:S(2)}) async-start(bf16[16,40,384]{2,1,0:T(8,128)(2,1)} %broadcast_in_dim.88), calls=%async_computation.6 | async-start | bytes 983040 | tf_op jit(solution)/shard_map/all_to_all | solution.py:165
  169.5 26.4 %copy-start.20 = (bf16[40,384]{1,0:T(8,128)(2,1)}, bf16[40,384]{1,0:T(8,128)(2,1)S(1)}, u32[]{:S(2)}) copy-start(bf16[40,384]{1,0:T(8,128)(2,1)S(1)} %shard_map.93) | copy-start | bytes 92164
  169.5 5.0 collective-permute-start.7
  175.4 13.1 %all-to-all-start.8 = ((bf16[16,40,384]{2,1,0:T(8,128)(2,1)}), bf16[16,40,384]{2,1,0:T(8,128)(2,1)}, u32[]{:S(2)}, u32[]{:S(2)}) async-start(bf16[16,40,384]{2,1,0:T(8,128)(2,1)} %broadcast_in_dim.89), calls=%async_computation.8 | async-start | bytes 983040 | tf_op jit(solution)/shard_map/all_to_all | solution.py:165
  207.1 26.7 %copy-start.22 = (bf16[40,384]{1,0:T(8,128)(2,1)}, bf16[40,384]{1,0:T(8,128)(2,1)S(1)}, u32[]{:S(2)}) copy-start(bf16[40,384]{1,0:T(8,128)(2,1)S(1)} %shard_map.95) | copy-start | bytes 92164
  207.1 6.1 collective-permute-start.8
  214.1 13.1 %all-to-all-start.10 = ((bf16[16,40,384]{2,1,0:T(8,128)(2,1)}), bf16[16,40,384]{2,1,0:T(8,128)(2,1)}, u32[]{:S(2)}, u32[]{:S(2)}) async-start(bf16[16,40,384]{2,1,0:T(8,128)(2,1)} %broadcast_in_dim.90), calls=%async_computation.10 | async-start | bytes 983040 | tf_op jit(solution)/shard_map/all_to_all | solution.py:165
  233.8 18.8 %copy-start.62 = (f32[40,256]{1,0:T(8,128)}, f32[40,256]{1,0:T(8,128)S(1)}, u32[]{:S(2)}) copy-start(f32[40,256]{1,0:T(8,128)S(1)} %get-tuple-element.67.kin_ref) | copy-start | bytes 122884
  247.2 28.5 %copy-start.24 = (bf16[40,384]{1,0:T(8,128)(2,1)}, bf16[40,384]{1,0:T(8,128)(2,1)S(1)}, u32[]{:S(2)}) copy-start(bf16[40,384]{1,0:T(8,128)(2,1)S(1)} %shard_map.97) | copy-start | bytes 92164
  247.2 5.4 collective-permute-start.9
  253.5 14.7 %all-to-all-start.12 = ((bf16[16,40,384]{2,1,0:T(8,128)(2,1)}), bf16[16,40,384]{2,1,0:T(8,128)(2,1)}, u32[]{:S(2)}, u32[]{:S(2)}) async-start(bf16[16,40,384]{2,1,0:T(8,128)(2,1)} %broadcast_in_dim.91), calls=%async_computation.12 | async-start | bytes 983040 | tf_op jit(solution)/shard_map/all_to_all | solution.py:165
  286.9 26.8 %copy-start.26 = (bf16[40,384]{1,0:T(8,128)(2,1)}, bf16[40,384]{1,0:T(8,128)(2,1)S(1)}, u32[]{:S(2)}) copy-start(bf16[40,384]{1,0:T(8,128)(2,1)S(1)} %shard_map.99) | copy-start | bytes 92164
  286.9 6.2 collective-permute-start.10
  293.9 13.1 %all-to-all-start.14 = ((bf16[16,40,384]{2,1,0:T(8,128)(2,1)}), bf16[16,40,384]{2,1,0:T(8,128)(2,1)}, u32[]{:S(2)}, u32[]{:S(2)}) async-start(bf16[16,40,384]{2,1,0:T(8,128)(2,1)} %broadcast_in_dim.92), calls=%async_computation.14 | async-start | bytes 983040 | tf_op jit(solution)/shard_map/all_to_all | solution.py:165
  324.9 27.6 %copy-start.28 = (bf16[40,384]{1,0:T(8,128)(2,1)}, bf16[40,384]{1,0:T(8,128)(2,1)S(1)}, u32[]{:S(2)}) copy-start(bf16[40,384]{1,0:T(8,128)(2,1)S(1)} %shard_map.101) | copy-start | bytes 92164
  325.0 6.0 collective-permute-start.11
  331.9 13.2 %all-to-all-start.16 = ((bf16[16,40,384]{2,1,0:T(8,128)(2,1)}), bf16[16,40,384]{2,1,0:T(8,128)(2,1)}, u32[]{:S(2)}, u32[]{:S(2)}) async-start(bf16[16,40,384]{2,1,0:T(8,128)(2,1)} %broadcast_in_dim.93), calls=%async_computation.16 | async-start | bytes 983040 | tf_op jit(solution)/shard_map/all_to_all | solution.py:165
  363.8 26.6 %copy-start.30 = (bf16[40,384]{1,0:T(8,128)(2,1)}, bf16[40,384]{1,0:T(8,128)(2,1)S(1)}, u32[]{:S(2)}) copy-start(bf16[40,384]{1,0:T(8,128)(2,1)S(1)} %shard_map.103) | copy-start | bytes 92164
  363.8 6.0 collective-permute-start.12
  370.6 13.1 %all-to-all-start.18 = ((bf16[16,40,384]{2,1,0:T(8,128)(2,1)}), bf16[16,40,384]{2,1,0:T(8,128)(2,1)}, u32[]{:S(2)}, u32[]{:S(2)}) async-start(bf16[16,40,384]{2,1,0:T(8,128)(2,1)} %broadcast_in_dim.94), calls=%async_computation.18 | async-start | bytes 983040 | tf_op jit(solution)/shard_map/all_to_all | solution.py:165
  401.6 27.2 %copy-start.32 = (bf16[40,384]{1,0:T(8,128)(2,1)}, bf16[40,384]{1,0:T(8,128)(2,1)S(1)}, u32[]{:S(2)}) copy-start(bf16[40,384]{1,0:T(8,128)(2,1)S(1)} %shard_map.105) | copy-start | bytes 92164
  401.6 5.9 collective-permute-start.13
  408.4 13.1 %all-to-all-start.20 = ((bf16[16,40,384]{2,1,0:T(8,128)(2,1)}), bf16[16,40,384]{2,1,0:T(8,128)(2,1)}, u32[]{:S(2)}, u32[]{:S(2)}) async-start(bf16[16,40,384]{2,1,0:T(8,128)(2,1)} %broadcast_in_dim.95), calls=%async_computation.20 | async-start | bytes 983040 | tf_op jit(solution)/shard_map/all_to_all | solution.py:165
  440.1 26.4 %copy-start.34 = (bf16[40,384]{1,0:T(8,128)(2,1)}, bf16[40,384]{1,0:T(8,128)(2,1)S(1)}, u32[]{:S(2)}) copy-start(bf16[40,384]{1,0:T(8,128)(2,1)S(1)} %shard_map.107) | copy-start | bytes 92164
  440.1 5.8 collective-permute-start.14
  446.9 13.0 %all-to-all-start.22 = ((bf16[16,40,384]{2,1,0:T(8,128)(2,1)}), bf16[16,40,384]{2,1,0:T(8,128)(2,1)}, u32[]{:S(2)}, u32[]{:S(2)}) async-start(bf16[16,40,384]{2,1,0:T(8,128)(2,1)} %broadcast_in_dim.96), calls=%async_computation.22 | async-start | bytes 983040 | tf_op jit(solution)/shard_map/all_to_all | solution.py:165
  478.9 29.0 %copy-start.36 = (bf16[40,384]{1,0:T(8,128)(2,1)}, bf16[40,384]{1,0:T(8,128)(2,1)S(1)}, u32[]{:S(2)}) copy-start(bf16[40,384]{1,0:T(8,128)(2,1)S(1)} %shard_map.109) | copy-start | bytes 92164
  478.9 6.1 collective-permute-start.15
  485.9 14.5 %all-to-all-start.24 = ((bf16[16,40,384]{2,1,0:T(8,128)(2,1)}), bf16[16,40,384]{2,1,0:T(8,128)(2,1)}, u32[]{:S(2)}, u32[]{:S(2)}) async-start(bf16[16,40,384]{2,1,0:T(8,128)(2,1)} %broadcast_in_dim.97), calls=%async_computation.24 | async-start | bytes 983040 | tf_op jit(solution)/shard_map/all_to_all | solution.py:165
  507.9 19.0 %copy-start.84 = (f32[40,256]{1,0:T(8,128)}, f32[40,256]{1,0:T(8,128)S(1)}, u32[]{:S(2)}) copy-start(f32[40,256]{1,0:T(8,128)S(1)} %get-tuple-element.89.vin_ref) | copy-start | bytes 122884
  507.9 19.0 %copy-start.107 = (bf16[80,384]{1,0:T(8,128)(2,1)S(1)}, bf16[80,384]{1,0:T(8,128)(2,1)}, u32[]{:S(2)}) copy-start(bf16[80,384]{1,0:T(8,128)(2,1)} %copy-done.94) | copy-start | bytes 184324
  520.6 27.3 %copy-start.38 = (bf16[40,384]{1,0:T(8,128)(2,1)}, bf16[40,384]{1,0:T(8,128)(2,1)S(1)}, u32[]{:S(2)}) copy-start(bf16[40,384]{1,0:T(8,128)(2,1)S(1)} %shard_map.111) | copy-start | bytes 92164
  520.6 6.3 collective-permute-start.16
  527.8 13.5 %all-to-all-start.26 = ((bf16[16,40,384]{2,1,0:T(8,128)(2,1)}), bf16[16,40,384]{2,1,0:T(8,128)(2,1)}, u32[]{:S(2)}, u32[]{:S(2)}) async-start(bf16[16,40,384]{2,1,0:T(8,128)(2,1)} %broadcast_in_dim.98), calls=%async_computation.26 | async-start | bytes 983040 | tf_op jit(solution)/shard_map/all_to_all | solution.py:165
  559.1 26.5 %copy-start.40 = (bf16[40,384]{1,0:T(8,128)(2,1)}, bf16[40,384]{1,0:T(8,128)(2,1)S(1)}, u32[]{:S(2)}) copy-start(bf16[40,384]{1,0:T(8,128)(2,1)S(1)} %shard_map.113) | copy-start | bytes 92164
  559.1 5.1 collective-permute-start.17
  565.1 13.1 %all-to-all-start.28 = ((bf16[16,40,384]{2,1,0:T(8,128)(2,1)}), bf16[16,40,384]{2,1,0:T(8,128)(2,1)}, u32[]{:S(2)}, u32[]{:S(2)}) async-start(bf16[16,40,384]{2,1,0:T(8,128)(2,1)} %broadcast_in_dim.99), calls=%async_computation.28 | async-start | bytes 983040 | tf_op jit(solution)/shard_map/all_to_all | solution.py:165
  596.7 27.1 %copy-start.42 = (bf16[40,384]{1,0:T(8,128)(2,1)}, bf16[40,384]{1,0:T(8,128)(2,1)S(1)}, u32[]{:S(2)}) copy-start(bf16[40,384]{1,0:T(8,128)(2,1)S(1)} %shard_map.115) | copy-start | bytes 92164
  596.7 5.7 collective-permute-start.18
  603.3 13.1 %all-to-all-start.30 = ((bf16[16,40,384]{2,1,0:T(8,128)(2,1)}), bf16[16,40,384]{2,1,0:T(8,128)(2,1)}, u32[]{:S(2)}, u32[]{:S(2)}) async-start(bf16[16,40,384]{2,1,0:T(8,128)(2,1)} %broadcast_in_dim.104), calls=%async_computation.30 | async-start | bytes 983040 | tf_op jit(solution)/shard_map/all_to_all | solution.py:165
  635.1 75.4 %copy-start.44 = (bf16[40,384]{1,0:T(8,128)(2,1)}, bf16[40,384]{1,0:T(8,128)(2,1)S(1)}, u32[]{:S(2)}) copy-start(bf16[40,384]{1,0:T(8,128)(2,1)S(1)} %shard_map.117) | copy-start | bytes 92164
  635.1 5.4 collective-permute-start.19
  640.5 70.0 %copy-start.46 = (bf16[40,384]{1,0:T(8,128)(2,1)}, bf16[40,384]{1,0:T(8,128)(2,1)S(1)}, u32[]{:S(2)}) copy-start(bf16[40,384]{1,0:T(8,128)(2,1)S(1)} %broadcast_select_fusion.12.rows_ref) | copy-start | bytes 92164
  641.4 62.3 %all-to-all-start.32 = ((bf16[16,40,384]{2,1,0:T(8,128)(2,1)}), bf16[16,40,384]{2,1,0:T(8,128)(2,1)}, u32[]{:S(2)}, u32[]{:S(2)}) async-start(bf16[16,40,384]{2,1,0:T(8,128)(2,1)} %broadcast_in_dim.106), calls=%async_computation.32 | async-start | bytes 983040 | tf_op jit(solution)/shard_map/all_to_all | solution.py:165
  645.6 73.1 %collective-permute-start.21 = (bf16[128,192]{0,1:T(8,128)(2,1)}, bf16[128,192]{0,1:T(8,128)(2,1)}, u32[]{:S(2)}, u32[]{:S(2)}) collective-permute-start(bf16[128,192]{0,1:T(8,128)(2,1)} %param.8), channel_id=1, source_target_pairs={{0,1},{1,0},{2,3},{3,2},{4,5},{5,4},{6,7},{7,6},{8,9},{9,8},{10,11... | collective-permute-start | bytes 147464 | tf_op jit(solution)/shard_map/ppermute | solution.py:93
  711.3 14.7 %all-to-all-start.33 = ((bf16[16,40,256]{2,1,0:T(8,128)(2,1)}), bf16[16,40,256]{2,1,0:T(8,128)(2,1)S(1)}, u32[]{:S(2)}, u32[]{:S(2)}) async-start(bf16[16,40,256]{2,1,0:T(8,128)(2,1)} %copy-done.17), calls=%async_computation.33 | async-start | bytes 655360 | tf_op jit(solution)/shard_map/all_to_all | solution.py:169
  726.9 50.6 %copy-start.116 = (f32[8]{0:T(128)S(1)}, f32[8]{0:T(128)}, u32[]{:S(2)}) copy-start(f32[8]{0:T(128)} %convert_reduce_fusion) | copy-start | bytes 100
  729.0 16.4 %all-to-all-start.34 = ((f32[32,1,128]{2,1,0:T(1,128)}), f32[32,1,128]{2,1,0:T(1,128)S(1)}, u32[]{:S(2)}, u32[]{:S(2)}) async-start(f32[32,1,128]{2,1,0:T(1,128)} %broadcast_in_dim.111), calls=%async_computation.34 | async-start | bytes 32768 | tf_op jit(solution)/shard_map/all_to_all | solution.py:189
  738.4 27.8 %collective-permute-start.20 = (bf16[80,192]{1,0:T(8,128)(2,1)S(1)}, bf16[80,192]{1,0:T(8,128)(2,1)S(1)}, u32[]{:S(2)}, u32[]{:S(2)}) collective-permute-start(bf16[80,192]{1,0:T(8,128)(2,1)S(1)} %broadcast_select_fusion.10), channel_id=1, source_target_pairs={{0,1},{1,0},{2,3},{3,2},{4,5},{5,4},{6,7},{7,6},{8,9},{9,8},{10,11... | collective-permute-start | bytes 92168 | tf_op jit(solution)/shard_map/ppermute | solution.py:93
  746.0 31.4 %all-to-all-start.35 = ((f32[16,1,128]{2,1,0:T(1,128)}), f32[16,1,128]{2,1,0:T(1,128)S(1)}, u32[]{:S(2)}, u32[]{:S(2)}) async-start(f32[16,1,128]{2,1,0:T(1,128)} %broadcast_in_dim.112), calls=%async_computation.35 | async-start | bytes 16384 | tf_op jit(solution)/shard_map/all_to_all | solution.py:189
  (96 other events, 683.9 us)

commit v2 on v1

--- a/solution.py
+++ b/solution.py
@@ -1,5 +1,3 @@
-import functools
-
 import jax
 import jax.numpy as jnp
 from jax import lax
@@ -16,7 +14,9 @@
 PLANE = ("y", "x")
 
 
-def qkv_attention(order_ref, rows_ref, gain_ref, w_ref, bias_ref, kin_ref, vin_ref, send_ref, kout_ref, vout_ref):
+def qkv_attention(
+    flag_ref, rows_ref, gain_ref, w_ref, bias_ref, kin_ref, vin_ref, send_ref, kout_ref, vout_ref, next_ref
+):
     chips, length, cols = rows_ref.shape
     width = kin_ref.shape[1]
     heads = width // HD
@@ -50,7 +50,7 @@
     keys = jnp.concatenate([kin_ref[...], key], 0).astype(jnp.bfloat16)
     vals = jnp.concatenate([vin_ref[...], val], 0).astype(jnp.bfloat16)
     scores = lax.dot_general(queries, keys, (((1,), (1,)), ((), ())), preferred_element_type=jnp.float32) / HD
-    scores = scores + bias_ref[order_ref[0]]
+    scores = scores + jnp.where(flag_ref[0:1, 0:1] > 0.0, bias_ref[1], bias_ref[0])
     peak = jnp.max(scores, -1, keepdims=True)
     expo = jnp.exp(scores - peak)
     weights = (expo / jnp.sum(expo, -1, keepdims=True)).astype(jnp.bfloat16)
@@ -63,9 +63,11 @@
         send_ref[chip] = attended
     kout_ref[...] = key
     vout_ref[...] = val
-
-
-def project_out(heads_ref, w_ref, rows_ref, out_ref):
+    is_order = lax.broadcasted_iota(jnp.int32, flag_ref.shape, 0) == 0
+    next_ref[...] = flag_ref[...] + jnp.where(is_order, 1.0, 0.0)
+
+
+def project_out(flag_ref, heads_ref, w_ref, rows_ref, kept_ref, out_ref, done_ref):
     chips, _, width = heads_ref.shape
     acc = rows_ref[...].astype(jnp.float32)
     mixed = jnp.zeros(acc.shape, jnp.float32)
@@ -73,7 +75,22 @@
         mixed += jnp.dot(
             heads_ref[chip], w_ref[chip * width : (chip + 1) * width, :], preferred_element_type=jnp.float32
         )
-    out_ref[...] = (acc + mixed).astype(jnp.bfloat16)
+    rows = (acc + mixed).astype(jnp.bfloat16)
+    out_ref[...] = rows
+    for number in range(kept_ref.shape[0]):
+        mine = flag_ref[0:1, 0:1] == float(number)
+        done_ref[number] = jnp.where(mine, rows.astype(jnp.float32), kept_ref[number].astype(jnp.float32)).astype(
+            jnp.bfloat16
+        )
+
+
+def spread(flag_ref, tokens_ref, received_ref, rows_ref, send_ref):
+    first = flag_ref[1:2, 0:1] > 0.0
+    rows = jnp.where(first, tokens_ref[...].astype(jnp.float32), received_ref[...].astype(jnp.float32))
+    rows = rows.astype(jnp.bfloat16)
+    rows_ref[...] = rows
+    for chip in range(send_ref.shape[0]):
+        send_ref[chip] = rows
 
 
 def local(tokens, targets, doc_ids, norm_gains, w_qk, w_val, w_out):
@@ -110,6 +127,7 @@
 
     tokens_chip = jnp.concatenate(both(tokens, swap(tokens)), 1)
     first_rows = picked(tokens_chip).astype(jnp.bfloat16)
+    first_parts = [first_rows[number * length : (number + 1) * length] for number in range(slices)]
     docs = jnp.sum(jnp.where(pick, doc_ids[None, :], 0), 1)
     docs = jnp.where(place < count, docs, DOCS)
     same = (docs[:, None] == docs[None, :]) & (place[None, :] <= place[:, None])
@@ -122,21 +140,23 @@
     bias = jnp.tile(jnp.where(allowed, 0.0, NEG).astype(jnp.float32), (1, heads, 1))
 
     w_in = jnp.concatenate(both(w_qk[0], swap(w_qk[0])) + both(w_val[0], swap(w_val[0])), 1)
-    w_last = jnp.concatenate(both(w_out[0], swap(w_out[0])), 1)
+    w_out_t = jnp.swapaxes(w_out[0], 0, 1)
+    w_last = jnp.swapaxes(jnp.concatenate(both(w_out_t, swap(w_out_t)), 0), 0, 1)
     gains = norm_gains[0].reshape(chips, cols)
 
     vmem = pl.BlockSpec(memory_space=pltpu.VMEM)
-    smem = pl.BlockSpec(memory_space=pltpu.SMEM)
-    params = pltpu.CompilerParams(vmem_limit_bytes=32 * 1024 * 1024)
+    params = pltpu.CompilerParams(vmem_limit_bytes=16 * 1024 * 1024)
+    flag_tile = jax.ShapeDtypeStruct((8, 128), jnp.float32)
     attend = pl.pallas_call(
         qkv_attention,
         out_shape=(
             jax.ShapeDtypeStruct((chips, length, width), jnp.bfloat16),
             jax.ShapeDtypeStruct((length, width), jnp.float32),
             jax.ShapeDtypeStruct((length, width), jnp.float32),
-        ),
-        in_specs=[smem] + [vmem] * 6,
-        out_specs=(vmem,) * 3,
+            flag_tile,
+        ),
+        in_specs=[vmem] * 7,
+        out_specs=(vmem,) * 4,
         compiler_params=params,
         cost_estimate=pl.CostEstimate(
             flops=2 * length * D * 2 * width, bytes_accessed=4 * D * width, transcendentals=heads * length * part
@@ -144,37 +164,55 @@
     )
     project = pl.pallas_call(
         project_out,
-        out_shape=jax.ShapeDtypeStruct((length, cols), jnp.bfloat16),
-        in_specs=[vmem] * 3,
-        out_specs=vmem,
+        out_shape=(
+            jax.ShapeDtypeStruct((length, cols), jnp.bfloat16),
+            jax.ShapeDtypeStruct((slices, length, cols), jnp.bfloat16),
+        ),
+        in_specs=[vmem] * 5,
+        out_specs=(vmem,) * 2,
         compiler_params=params,
         cost_estimate=pl.CostEstimate(
             flops=2 * length * chips * width * cols, bytes_accessed=2 * chips * width * cols, transcendentals=0
         ),
     )
 
+    place_rows = pl.pallas_call(
+        spread,
+        out_shape=(
+            jax.ShapeDtypeStruct((length, cols), jnp.bfloat16),
+            jax.ShapeDtypeStruct((chips, length, cols), jnp.bfloat16),
+        ),
+        in_specs=[vmem] * 3,
+        out_specs=(vmem,) * 2,
+        compiler_params=params,
+        cost_estimate=pl.CostEstimate(flops=0, bytes_accessed=2 * chips * length * cols, transcendentals=0),
+    )
+    tile_row = lax.broadcasted_iota(jnp.int32, flag_tile.shape, 0)
+    flags = jnp.where(
+        tile_row == 0, -section.astype(jnp.float32), jnp.where((tile_row == 1) & (section == 0), 1.0, 0.0)
+    )
+    targets_chip = jnp.concatenate(both(targets, swap(targets)), 1)
+    goal = picked(targets_chip)
+
     keys = jnp.zeros((length, width), jnp.float32)
     vals = jnp.zeros((length, width), jnp.float32)
-    done = [jnp.zeros((length, cols), jnp.bfloat16) for _ in range(slices)]
+    done = jnp.zeros((slices, length, cols), jnp.bfloat16)
     received = jnp.zeros((length, cols), jnp.bfloat16)
     for step in range(section_count + slices - 1):
-        order = step - section
-        turn = jnp.clip(order, 0, slices - 1)
         mine = min(step, slices - 1)
-        rows = jnp.where(section == 0, first_rows[mine * length : (mine + 1) * length], received)
-        gathered = lax.all_to_all(
-            jnp.broadcast_to(rows[None], (chips,) + rows.shape), PLANE, 0, 0, tiled=True
-        )
-        send, keys, vals = attend(turn.reshape(1), gathered, gains, w_in, bias, keys, vals)
+        rows, send = place_rows(flags, first_parts[mine], received)
+        gathered = lax.all_to_all(send, PLANE, 0, 0, tiled=True)
+        send, keys, vals, next_flags = attend(flags, gathered, gains, w_in, bias, keys, vals)
         attended = lax.all_to_all(send, PLANE, 0, 0, tiled=True)
-        rows = project(attended, w_last, rows)
+        if step == 0:
+            attended, goal, w_last, first_parts = lax.optimization_barrier((attended, goal, w_last, first_parts))
+        rows, done = project(flags, attended, w_last, rows, done)
+        flags = next_flags
         if step < section_count + slices - 2:
             received = lax.ppermute(rows, "section", [(z, z + 1) for z in range(section_count - 1)])
-        done = [jnp.where(order == number, rows, kept) for number, kept in enumerate(done)]
-
-    part_rows = jnp.concatenate(done, 0)
-    targets_chip = jnp.concatenate(both(targets, swap(targets)), 1)
-    diff = part_rows.astype(jnp.float32) - picked(targets_chip)
+
+    part_rows = done.reshape(part, cols)
+    diff = part_rows.astype(jnp.float32) - goal
     token_sums = jnp.sum(diff * diff, -1)
     doc_names = jnp.arange(128, dtype=jnp.int32)[None, :]
     in_doc = docs[:, None] == doc_names

time: 793 us -> 684 us (0.86)
  blocking collectives: 164 us -> 355 us
  waiting for transfers between devices: 176 us -> 42.1 us
  starting transfers between devices: 261 us -> 188 us
  local copies, waits for them, and re-layouts: 90.6 us -> 19.1 us
  Pallas kernels: 62.6 us -> 48.7 us
    all_to_all x0 -> x16, blocking collectives: none -> 193 us  [local(): gathered = lax.all_to_all(send, PLANE, 0, 0, tiled=True)]
    all_to_all x17 -> x1, waiting for transfers between devices: 139 us -> 3.66 us  [local(): gathered = lax.all_to_all(send, PLANE, 0, 0, tiled=True)]
    all_to_all x17 -> x1, starting transfers between devices: 73.7 us -> 3.57 us  [local(): gathered = lax.all_to_all(send, PLANE, 0, 0, tiled=True)]
    unnamed x236 -> x28, local copies, waits for them, and re-layouts: 71.1 us -> 13.9 us
    all_to_all x2, starting transfers between devices: 29.5 us -> 85.7 us  [share(): return jnp.sum(lax.all_to_all(pieces, axes, 0, 0, tiled=True), 0)]
    ppermute x6, starting transfers between devices: 75.5 us -> 19.8 us  [swap(): return lax.ppermute(value, 'core', [(0, 1), (1, 0)])]
    broadcast_in_dim x17 -> x2, local copies, waits for them, and re-layouts: 14.4 us -> 0.01 us  [the longest x1 0.01 us: local(): done = jnp.zeros((slices, length, cols), jnp.bfloat16)]
    pallas_call x34 -> x51, Pallas kernels: 62.6 us -> 48.7 us  [the longest x17 36.4 us: local(): attend(flags, gathered, gains, w_in, bias, keys, vals)]
  transfers between devices with their start and end apart: 43 -> 27, of which waited for: 36 -> 20; matrix products, arithmetic and copies ran while one was open for 3% -> 4% of each run, Pallas kernels for 1% -> 1%
where the time goes in v2:
time: 684 us; the launch traced here: 674 us
  blocking collectives  355 us (52%)
  starting transfers between devices  188 us (27%)
  Pallas kernels  48.7 us (7%)
  waiting for transfers between devices  42.1 us (6%)
  local copies, waits for them, and re-layouts  19.1 us (3%)
  other arithmetic  16 us (2%)
    all_to_all x16, blocking collectives, local(): gathered = lax.all_to_all(send, PLANE, 0, 0, tiled=True)  193 us
    all_to_all x15, blocking collectives, local(): attended = lax.all_to_all(send, PLANE, 0, 0, tiled=True)  162 us
    all_to_all x2, starting transfers between devices, share(): return jnp.sum(lax.all_to_all(pieces, axes, 0, 0, tiled=True), 0)  85.7 us
    ppermute x16, starting transfers between devices, local(): lax.ppermute(rows, 'section', [(z, z + 1) for z in range(section_count -...  71.2 us
    pallas_call x17, Pallas kernels, local(): attend(flags, gathered, gains, w_in, bias, keys, vals)  36.4 us
    ppermute x6, starting transfers between devices, swap(): return lax.ppermute(value, 'core', [(0, 1), (1, 0)])  19.8 us
    ppermute x16, waiting for transfers between devices, local(): lax.ppermute(rows, 'section', [(z, z + 1) for z in range(section_count -...  15.8 us
    all_to_all x2, waiting for transfers between devices, share(): return jnp.sum(lax.all_to_all(pieces, axes, 0, 0, tiled=True), 0)  14.9 us
  transfers between devices with their start and end apart: 27, of which 20 were waited for; matrix products, arithmetic and copies ran while one was open for 4% of the time, Pallas kernels for 1%

profile of v2, /device:TPU:1, one launch (start us, length us, event | category | flops | bytes accessed | tf_op | source)
XLA Modules:
  0.0 674.0 jit_solution(230393351619571815)
XLA Ops:
  0.7 8.9 %collective-permute-start = (bf16[128,192]{0,1:T(8,128)(2,1)}, bf16[128,192]{0,1:T(8,128)(2,1)S(1)}, u32[]{:S(2)}, u32[]{:S(2)}) collective-permute-start(bf16[128,192]{0,1:T(8,128)(2,1)} %param.7), channel_id=1, source_target_pairs={{0,1},{1,0},{2,3},{3,2},{4,5},{5,4},{6,7},{7,6},{8,9},{9,8},{10,11... | collective-permute-start | bytes 147464 | tf_op jit(solution)/shard_map/ppermute | solution.py:110
  23.5 3.9 copy.18
  29.8 3.6 all-to-all-start
  37.6 3.2 pad_maximum_fusion.w_ref
  40.8 3.7 all-to-all-done.rows_ref
  44.5 2.8 copy-done
  47.2 2.8 shard_map.87
  50.0 3.7 all-to-all-start.1
  53.7 3.8 copy.20
  59.5 2.9 maximum_bitcast_fusion.w_ref
  67.2 15.3 %all_to_all.180.rows_ref = bf16[16,40,384]{2,1,0:T(8,128)(2,1)S(1)} all-to-all(bf16[16,40,384]{2,1,0:T(8,128)(2,1)S(1)} %get-tuple-element.146), channel_id=1, replica_groups=mesh['section'=16,'y'=4,'x'=4,'core'=2] {'y','x'}, dimensions={0} | all-to-all | bytes 983040 | tf_op jit(solution)/shard_map/all_to_all | solution.py:204
  82.5 2.8 copy-done.1
  87.4 10.6 %all_to_all.181.heads_ref = bf16[16,40,256]{2,1,0:T(8,128)(2,1)S(1)} all-to-all(bf16[16,40,256]{2,1,0:T(8,128)(2,1)S(1)} %get-tuple-element.150), channel_id=1, replica_groups=mesh['section'=16,'y'=4,'x'=4,'core'=2] {'y','x'}, dimensions={0} | all-to-all | bytes 655360 | tf_op jit(solution)/shard_map/all_to_all | solution.py:206
  98.6 3.6 collective-permute-start.6
  103.2 11.4 %all_to_all.182.rows_ref = bf16[16,40,384]{2,1,0:T(8,128)(2,1)S(1)} all-to-all(bf16[16,40,384]{2,1,0:T(8,128)(2,1)S(1)} %get-tuple-element.154), channel_id=1, replica_groups=mesh['section'=16,'y'=4,'x'=4,'core'=2] {'y','x'}, dimensions={0} | all-to-all | bytes 983040 | tf_op jit(solution)/shard_map/all_to_all | solution.py:204
  116.7 10.5 %all_to_all.183.heads_ref = bf16[16,40,256]{2,1,0:T(8,128)(2,1)S(1)} all-to-all(bf16[16,40,256]{2,1,0:T(8,128)(2,1)S(1)} %get-tuple-element.158), channel_id=1, replica_groups=mesh['section'=16,'y'=4,'x'=4,'core'=2] {'y','x'}, dimensions={0} | all-to-all | bytes 655360 | tf_op jit(solution)/shard_map/all_to_all | solution.py:206
  127.8 3.6 collective-permute-start.7
  132.6 11.9 %all_to_all.184.rows_ref = bf16[16,40,384]{2,1,0:T(8,128)(2,1)S(1)} all-to-all(bf16[16,40,384]{2,1,0:T(8,128)(2,1)S(1)} %get-tuple-element.162), channel_id=1, replica_groups=mesh['section'=16,'y'=4,'x'=4,'core'=2] {'y','x'}, dimensions={0} | all-to-all | bytes 983040 | tf_op jit(solution)/shard_map/all_to_all | solution.py:204
  146.5 10.8 %all_to_all.185.heads_ref = bf16[16,40,256]{2,1,0:T(8,128)(2,1)S(1)} all-to-all(bf16[16,40,256]{2,1,0:T(8,128)(2,1)S(1)} %get-tuple-element.166), channel_id=1, replica_groups=mesh['section'=16,'y'=4,'x'=4,'core'=2] {'y','x'}, dimensions={0} | all-to-all | bytes 655360 | tf_op jit(solution)/shard_map/all_to_all | solution.py:206
  157.8 4.1 collective-permute-start.8
  163.0 11.4 %all_to_all.186.rows_ref = bf16[16,40,384]{2,1,0:T(8,128)(2,1)S(1)} all-to-all(bf16[16,40,384]{2,1,0:T(8,128)(2,1)S(1)} %get-tuple-element.170), channel_id=1, replica_groups=mesh['section'=16,'y'=4,'x'=4,'core'=2] {'y','x'}, dimensions={0} | all-to-all | bytes 983040 | tf_op jit(solution)/shard_map/all_to_all | solution.py:204
  176.5 11.8 %all_to_all.187.heads_ref = bf16[16,40,256]{2,1,0:T(8,128)(2,1)S(1)} all-to-all(bf16[16,40,256]{2,1,0:T(8,128)(2,1)S(1)} %get-tuple-element.174), channel_id=1, replica_groups=mesh['section'=16,'y'=4,'x'=4,'core'=2] {'y','x'}, dimensions={0} | all-to-all | bytes 655360 | tf_op jit(solution)/shard_map/all_to_all | solution.py:206
  188.9 4.8 collective-permute-start.9
  194.8 11.9 %all_to_all.188.rows_ref = bf16[16,40,384]{2,1,0:T(8,128)(2,1)S(1)} all-to-all(bf16[16,40,384]{2,1,0:T(8,128)(2,1)S(1)} %get-tuple-element.178), channel_id=1, replica_groups=mesh['section'=16,'y'=4,'x'=4,'core'=2] {'y','x'}, dimensions={0} | all-to-all | bytes 983040 | tf_op jit(solution)/shard_map/all_to_all | solution.py:204
  208.7 10.7 %all_to_all.189.heads_ref = bf16[16,40,256]{2,1,0:T(8,128)(2,1)S(1)} all-to-all(bf16[16,40,256]{2,1,0:T(8,128)(2,1)S(1)} %get-tuple-element.182), channel_id=1, replica_groups=mesh['section'=16,'y'=4,'x'=4,'core'=2] {'y','x'}, dimensions={0} | all-to-all | bytes 655360 | tf_op jit(solution)/shard_map/all_to_all | solution.py:206
  220.0 4.8 collective-permute-start.10
  225.9 12.6 %all_to_all.190.rows_ref = bf16[16,40,384]{2,1,0:T(8,128)(2,1)S(1)} all-to-all(bf16[16,40,384]{2,1,0:T(8,128)(2,1)S(1)} %get-tuple-element.186), channel_id=1, replica_groups=mesh['section'=16,'y'=4,'x'=4,'core'=2] {'y','x'}, dimensions={0} | all-to-all | bytes 983040 | tf_op jit(solution)/shard_map/all_to_all | solution.py:204
  240.5 10.5 %all_to_all.191.heads_ref = bf16[16,40,256]{2,1,0:T(8,128)(2,1)S(1)} all-to-all(bf16[16,40,256]{2,1,0:T(8,128)(2,1)S(1)} %get-tuple-element.190), channel_id=1, replica_groups=mesh['section'=16,'y'=4,'x'=4,'core'=2] {'y','x'}, dimensions={0} | all-to-all | bytes 655360 | tf_op jit(solution)/shard_map/all_to_all | solution.py:206
  251.5 5.2 collective-permute-start.11
  257.8 11.4 %all_to_all.192.rows_ref = bf16[16,40,384]{2,1,0:T(8,128)(2,1)S(1)} all-to-all(bf16[16,40,384]{2,1,0:T(8,128)(2,1)S(1)} %get-tuple-element.194), channel_id=1, replica_groups=mesh['section'=16,'y'=4,'x'=4,'core'=2] {'y','x'}, dimensions={0} | all-to-all | bytes 983040 | tf_op jit(solution)/shard_map/all_to_all | solution.py:204
  271.3 10.5 %all_to_all.193.heads_ref = bf16[16,40,256]{2,1,0:T(8,128)(2,1)S(1)} all-to-all(bf16[16,40,256]{2,1,0:T(8,128)(2,1)S(1)} %get-tuple-element.198), channel_id=1, replica_groups=mesh['section'=16,'y'=4,'x'=4,'core'=2] {'y','x'}, dimensions={0} | all-to-all | bytes 655360 | tf_op jit(solution)/shard_map/all_to_all | solution.py:206
  282.4 3.9 collective-permute-start.12
  287.4 11.6 %all_to_all.194.rows_ref = bf16[16,40,384]{2,1,0:T(8,128)(2,1)S(1)} all-to-all(bf16[16,40,384]{2,1,0:T(8,128)(2,1)S(1)} %get-tuple-element.202), channel_id=1, replica_groups=mesh['section'=16,'y'=4,'x'=4,'core'=2] {'y','x'}, dimensions={0} | all-to-all | bytes 983040 | tf_op jit(solution)/shard_map/all_to_all | solution.py:204
  301.1 10.5 %all_to_all.195.heads_ref = bf16[16,40,256]{2,1,0:T(8,128)(2,1)S(1)} all-to-all(bf16[16,40,256]{2,1,0:T(8,128)(2,1)S(1)} %get-tuple-element.206), channel_id=1, replica_groups=mesh['section'=16,'y'=4,'x'=4,'core'=2] {'y','x'}, dimensions={0} | all-to-all | bytes 655360 | tf_op jit(solution)/shard_map/all_to_all | solution.py:206
  312.2 4.8 collective-permute-start.13
  318.1 13.6 %all_to_all.196.rows_ref = bf16[16,40,384]{2,1,0:T(8,128)(2,1)S(1)} all-to-all(bf16[16,40,384]{2,1,0:T(8,128)(2,1)S(1)} %get-tuple-element.210), channel_id=1, replica_groups=mesh['section'=16,'y'=4,'x'=4,'core'=2] {'y','x'}, dimensions={0} | all-to-all | bytes 983040 | tf_op jit(solution)/shard_map/all_to_all | solution.py:204
  333.7 11.3 %all_to_all.197.heads_ref = bf16[16,40,256]{2,1,0:T(8,128)(2,1)S(1)} all-to-all(bf16[16,40,256]{2,1,0:T(8,128)(2,1)S(1)} %get-tuple-element.214), channel_id=1, replica_groups=mesh['section'=16,'y'=4,'x'=4,'core'=2] {'y','x'}, dimensions={0} | all-to-all | bytes 655360 | tf_op jit(solution)/shard_map/all_to_all | solution.py:206
  345.6 5.2 collective-permute-start.14
  351.9 11.6 %all_to_all.198.rows_ref = bf16[16,40,384]{2,1,0:T(8,128)(2,1)S(1)} all-to-all(bf16[16,40,384]{2,1,0:T(8,128)(2,1)S(1)} %get-tuple-element.218), channel_id=1, replica_groups=mesh['section'=16,'y'=4,'x'=4,'core'=2] {'y','x'}, dimensions={0} | all-to-all | bytes 983040 | tf_op jit(solution)/shard_map/all_to_all | solution.py:204
  365.6 10.5 %all_to_all.199.heads_ref = bf16[16,40,256]{2,1,0:T(8,128)(2,1)S(1)} all-to-all(bf16[16,40,256]{2,1,0:T(8,128)(2,1)S(1)} %get-tuple-element.222), channel_id=1, replica_groups=mesh['section'=16,'y'=4,'x'=4,'core'=2] {'y','x'}, dimensions={0} | all-to-all | bytes 655360 | tf_op jit(solution)/shard_map/all_to_all | solution.py:206
  376.7 5.1 collective-permute-start.15
  382.9 11.4 %all_to_all.200.rows_ref = bf16[16,40,384]{2,1,0:T(8,128)(2,1)S(1)} all-to-all(bf16[16,40,384]{2,1,0:T(8,128)(2,1)S(1)} %get-tuple-element.226), channel_id=1, replica_groups=mesh['section'=16,'y'=4,'x'=4,'core'=2] {'y','x'}, dimensions={0} | all-to-all | bytes 983040 | tf_op jit(solution)/shard_map/all_to_all | solution.py:204
  396.4 10.5 %all_to_all.201.heads_ref = bf16[16,40,256]{2,1,0:T(8,128)(2,1)S(1)} all-to-all(bf16[16,40,256]{2,1,0:T(8,128)(2,1)S(1)} %get-tuple-element.230), channel_id=1, replica_groups=mesh['section'=16,'y'=4,'x'=4,'core'=2] {'y','x'}, dimensions={0} | all-to-all | bytes 655360 | tf_op jit(solution)/shard_map/all_to_all | solution.py:206
  407.5 5.0 collective-permute-start.16
  413.6 11.4 %all_to_all.202.rows_ref = bf16[16,40,384]{2,1,0:T(8,128)(2,1)S(1)} all-to-all(bf16[16,40,384]{2,1,0:T(8,128)(2,1)S(1)} %get-tuple-element.234), channel_id=1, replica_groups=mesh['section'=16,'y'=4,'x'=4,'core'=2] {'y','x'}, dimensions={0} | all-to-all | bytes 983040 | tf_op jit(solution)/shard_map/all_to_all | solution.py:204
  427.1 10.5 %all_to_all.203.heads_ref = bf16[16,40,256]{2,1,0:T(8,128)(2,1)S(1)} all-to-all(bf16[16,40,256]{2,1,0:T(8,128)(2,1)S(1)} %get-tuple-element.238), channel_id=1, replica_groups=mesh['section'=16,'y'=4,'x'=4,'core'=2] {'y','x'}, dimensions={0} | all-to-all | bytes 655360 | tf_op jit(solution)/shard_map/all_to_all | solution.py:206
  438.2 4.9 collective-permute-start.17
  444.2 11.7 %all_to_all.204.rows_ref = bf16[16,40,384]{2,1,0:T(8,128)(2,1)S(1)} all-to-all(bf16[16,40,384]{2,1,0:T(8,128)(2,1)S(1)} %get-tuple-element.242), channel_id=1, replica_groups=mesh['section'=16,'y'=4,'x'=4,'core'=2] {'y','x'}, dimensions={0} | all-to-all | bytes 983040 | tf_op jit(solution)/shard_map/all_to_all | solution.py:204
  457.9 11.8 %all_to_all.205.heads_ref = bf16[16,40,256]{2,1,0:T(8,128)(2,1)S(1)} all-to-all(bf16[16,40,256]{2,1,0:T(8,128)(2,1)S(1)} %get-tuple-element.246), channel_id=1, replica_groups=mesh['section'=16,'y'=4,'x'=4,'core'=2] {'y','x'}, dimensions={0} | all-to-all | bytes 655360 | tf_op jit(solution)/shard_map/all_to_all | solution.py:206
  470.3 5.1 collective-permute-start.18
  476.5 11.9 %all_to_all.206.rows_ref = bf16[16,40,384]{2,1,0:T(8,128)(2,1)S(1)} all-to-all(bf16[16,40,384]{2,1,0:T(8,128)(2,1)S(1)} %get-tuple-element.250), channel_id=1, replica_groups=mesh['section'=16,'y'=4,'x'=4,'core'=2] {'y','x'}, dimensions={0} | all-to-all | bytes 983040 | tf_op jit(solution)/shard_map/all_to_all | solution.py:204
  490.5 10.7 %all_to_all.207.heads_ref = bf16[16,40,256]{2,1,0:T(8,128)(2,1)S(1)} all-to-all(bf16[16,40,256]{2,1,0:T(8,128)(2,1)S(1)} %get-tuple-element.254), channel_id=1, replica_groups=mesh['section'=16,'y'=4,'x'=4,'core'=2] {'y','x'}, dimensions={0} | all-to-all | bytes 655360 | tf_op jit(solution)/shard_map/all_to_all | solution.py:206
  501.7 4.5 collective-permute-start.19
  507.3 12.3 %all_to_all.208.rows_ref = bf16[16,40,384]{2,1,0:T(8,128)(2,1)S(1)} all-to-all(bf16[16,40,384]{2,1,0:T(8,128)(2,1)S(1)} %get-tuple-element.258), channel_id=1, replica_groups=mesh['section'=16,'y'=4,'x'=4,'core'=2] {'y','x'}, dimensions={0} | all-to-all | bytes 983040 | tf_op jit(solution)/shard_map/all_to_all | solution.py:204
  521.6 10.5 %all_to_all.209.heads_ref = bf16[16,40,256]{2,1,0:T(8,128)(2,1)S(1)} all-to-all(bf16[16,40,256]{2,1,0:T(8,128)(2,1)S(1)} %get-tuple-element.262), channel_id=1, replica_groups=mesh['section'=16,'y'=4,'x'=4,'core'=2] {'y','x'}, dimensions={0} | all-to-all | bytes 655360 | tf_op jit(solution)/shard_map/all_to_all | solution.py:206
  532.7 5.2 collective-permute-start.20
  539.0 11.4 %all_to_all.210.rows_ref = bf16[16,40,384]{2,1,0:T(8,128)(2,1)S(1)} all-to-all(bf16[16,40,384]{2,1,0:T(8,128)(2,1)S(1)} %get-tuple-element.266), channel_id=1, replica_groups=mesh['section'=16,'y'=4,'x'=4,'core'=2] {'y','x'}, dimensions={0} | all-to-all | bytes 983040 | tf_op jit(solution)/shard_map/all_to_all | solution.py:204
  550.4 2.8 shard_map.135
  553.2 3.5 all-to-all-start.33
  556.9 7.7 %all-to-all-done.33.heads_ref = bf16[16,40,256]{2,1,0:T(8,128)(2,1)S(1)} async-done(((bf16[16,40,256]{2,1,0:T(8,128)(2,1)}), bf16[16,40,256]{2,1,0:T(8,128)(2,1)S(1)}, u32[]{:S(2)}, u32[]{:S(2)}) %all-to-all-start.33) | async-done | bytes 327712 | tf_op jit(solution)/shard_map/all_to_all | solution.py:206
  568.5 65.6 %all-to-all-start.34 = ((f32[32,1,128]{2,1,0:T(1,128)}), f32[32,1,128]{2,1,0:T(1,128)S(1)}, u32[]{:S(2)}, u32[]{:S(2)}) async-start(f32[32,1,128]{2,1,0:T(1,128)} %broadcast_in_dim.107), calls=%async_computation.34 | async-start | bytes 32768 | tf_op jit(solution)/shard_map/all_to_all | solution.py:227
  636.5 4.6 all-to-all-done.34
  641.7 20.1 %all-to-all-start.35 = ((f32[16,1,128]{2,1,0:T(1,128)}), f32[16,1,128]{2,1,0:T(1,128)S(1)}, u32[]{:S(2)}, u32[]{:S(2)}) async-start(f32[16,1,128]{2,1,0:T(1,128)} %broadcast_in_dim.108), calls=%async_computation.35 | async-start | bytes 16384 | tf_op jit(solution)/shard_map/all_to_all | solution.py:227
  662.9 10.3 %all-to-all-done.35 = f32[16,1,128]{2,1,0:T(1,128)S(1)} async-done(((f32[16,1,128]{2,1,0:T(1,128)}), f32[16,1,128]{2,1,0:T(1,128)S(1)}, u32[]{:S(2)}, u32[]{:S(2)}) %all-to-all-start.35) | async-done | bytes 8224 | tf_op jit(solution)/shard_map/all_to_all | solution.py:227
  (142 shorter events, 88.2 us)
Async XLA Ops:
  0.6 28.0 %copy-start.8 = (bf16[128,192]{0,1:T(8,128)(2,1)S(1)}, bf16[128,192]{0,1:T(8,128)(2,1)}, u32[]{:S(2)}) copy-start(bf16[128,192]{0,1:T(8,128)(2,1)} %param.7) | copy-start | bytes 147460
  0.6 28.0 %copy-start.7 = (bf16[128,192]{0,1:T(8,128)(2,1)S(1)}, bf16[128,192]{0,1:T(8,128)(2,1)}, u32[]{:S(2)}) copy-start(bf16[128,192]{0,1:T(8,128)(2,1)} %param.8) | copy-start | bytes 147460
  0.6 27.3 %copy-start.9 = (f32[1,6144]{1,0:T(1,128)S(1)}, f32[1,6144]{1,0:T(1,128)}, u32[]{:S(2)}) copy-start(f32[1,6144]{1,0:T(1,128)} %param.10) | copy-start | bytes 73732
  0.7 28.0 %collective-permute-start = (bf16[128,192]{0,1:T(8,128)(2,1)}, bf16[128,192]{0,1:T(8,128)(2,1)S(1)}, u32[]{:S(2)}, u32[]{:S(2)}) collective-permute-start(bf16[128,192]{0,1:T(8,128)(2,1)} %param.7), channel_id=1, source_target_pairs={{0,1},{1,0},{2,3},{3,2},{4,5},{5,4},{6,7},{7,6},{8,9},{9,8},{10,11... | collective-permute-start | bytes 147464 | tf_op jit(solution)/shard_map/ppermute | solution.py:110
  9.6 19.1 %collective-permute-start.3 = (bf16[128,192]{0,1:T(8,128)(2,1)}, bf16[128,192]{0,1:T(8,128)(2,1)S(1)}, u32[]{:S(2)}, u32[]{:S(2)}) collective-permute-start(bf16[128,192]{0,1:T(8,128)(2,1)} %param.8), channel_id=1, source_target_pairs={{0,1},{1,0},{2,3},{3,2},{4,5},{5,4},{6,7},{7,6},{8,9},{9,8},{10,11... | collective-permute-start | bytes 147464 | tf_op jit(solution)/shard_map/ppermute | solution.py:110
  11.5 22.1 %collective-permute-start.1 = (bf16[6144,128]{1,0:T(8,128)(2,1)}, bf16[6144,128]{1,0:T(8,128)(2,1)}, u32[]{:S(2)}, u32[]{:S(2)}) collective-permute-start(bf16[6144,128]{1,0:T(8,128)(2,1)} %bitcast.52), channel_id=1, source_target_pairs={{0,1},{1,0},{2,3},{3,2},{4,5},{5,4},{6,7},{7,6},{8,9},{9,8},{10,11... | collective-permute-start | bytes 4718600 | tf_op jit(solution)/shard_map/ppermute | solution.py:110
  13.9 21.9 %collective-permute-start.2 = (bf16[6144,128]{1,0:T(8,128)(2,1)}, bf16[6144,128]{1,0:T(8,128)(2,1)}, u32[]{:S(2)}, u32[]{:S(2)}) collective-permute-start(bf16[6144,128]{1,0:T(8,128)(2,1)} %bitcast.53), channel_id=1, source_target_pairs={{0,1},{1,0},{2,3},{3,2},{4,5},{5,4},{6,7},{7,6},{8,9},{9,8},{10,11... | collective-permute-start | bytes 4718600 | tf_op jit(solution)/shard_map/ppermute | solution.py:110
  15.9 37.9 %collective-permute-start.4 = (bf16[192,4096]{1,0:T(8,128)(2,1)}, bf16[192,4096]{1,0:T(8,128)(2,1)}, u32[]{:S(2)}, u32[]{:S(2)}) collective-permute-start(bf16[192,4096]{1,0:T(8,128)(2,1)} %bitcast.51), channel_id=1, source_target_pairs={{0,1},{1,0},{2,3},{3,2},{4,5},{5,4},{6,7},{7,6},{8,9},{9,8},{10,11... | collective-permute-start | bytes 4718600 | tf_op jit(solution)/shard_map/ppermute | solution.py:110
  29.8 14.6 %all-to-all-start = ((bf16[16,40,384]{2,1,0:T(8,128)(2,1)}), bf16[16,40,384]{2,1,0:T(8,128)(2,1)S(1)}, u32[]{:S(2)}, u32[]{:S(2)}) async-start(bf16[16,40,384]{2,1,0:T(8,128)(2,1)} %get-tuple-element.138), calls=%async_computation | async-start | bytes 983040 | tf_op jit(solution)/shard_map/all_to_all | solution.py:204
  33.6 2.4 copy-start.6
  44.4 2.8 copy-start
  50.0 7.5 %copy-start.5 = (bf16[1,4096,192]{2,1,0:T(8,128)(2,1)S(1)}, bf16[1,4096,192]{2,1,0:T(8,128)(2,1)}, u32[]{:S(2)}) copy-start(bf16[1,4096,192]{2,1,0:T(8,128)(2,1)} %copy.18) | copy-start | bytes 4718596
  50.0 12.3 %all-to-all-start.1 = ((bf16[16,40,256]{2,1,0:T(8,128)(2,1)}), bf16[16,40,256]{2,1,0:T(8,128)(2,1)S(1)}, u32[]{:S(2)}, u32[]{:S(2)}) async-start(bf16[16,40,256]{2,1,0:T(8,128)(2,1)} %get-tuple-element.140), calls=%async_computation.1 | async-start | bytes 655360 | tf_op jit(solution)/shard_map/all_to_all | solution.py:206
  59.4 55.2 %slice-start = ((s8[6291456]{0:T(1024)(128)(4,1)}), s8[2097152]{0:T(1024)(128)(4,1)S(1)}, s32[]{:S(2)}) async-start(s8[6291456]{0:T(1024)(128)(4,1)} %bitcast.30), calls=%async_computation.36 | async-start | bytes 4194304
  62.3 1.9 copy-start.2
  64.8 2.3 collective-permute-start.5
  82.5 2.8 copy-start.1
  85.3 12.7 %copy-start.3 = (bf16[4096,384]{1,0:T(8,128)(2,1)S(1)}, bf16[4096,384]{1,0:T(8,128)(2,1)}, u32[]{:S(2)}) copy-start(bf16[4096,384]{1,0:T(8,128)(2,1)} %maximum_bitcast_fusion.w_ref) | copy-start | bytes 9437188
  85.3 29.4 %slice-start.1 = ((s8[6291456]{0:T(1024)(128)(4,1)}), s8[4194304]{0:T(1024)(128)(4,1)S(1)}, s32[]{:S(2)}) async-start(s8[6291456]{0:T(1024)(128)(4,1)} %bitcast.30), calls=%async_computation.37 | async-start | bytes 8388608
  98.6 4.6 collective-permute-start.6
  127.8 4.6 collective-permute-start.7
  157.8 5.1 collective-permute-start.8
  188.9 5.8 collective-permute-start.9
  220.0 5.8 collective-permute-start.10
  251.5 6.2 collective-permute-start.11
  282.4 4.9 collective-permute-start.12
  312.2 5.8 collective-permute-start.13
  345.6 6.2 collective-permute-start.14
  376.7 6.1 collective-permute-start.15
  407.5 6.0 collective-permute-start.16
  438.2 5.9 collective-permute-start.17
  470.3 6.1 collective-permute-start.18
  501.7 5.5 collective-permute-start.19
  532.7 6.2 collective-permute-start.20
  550.4 6.4 copy-start.10
  553.2 11.4 %all-to-all-start.33 = ((bf16[16,40,256]{2,1,0:T(8,128)(2,1)}), bf16[16,40,256]{2,1,0:T(8,128)(2,1)S(1)}, u32[]{:S(2)}, u32[]{:S(2)}) async-start(bf16[16,40,256]{2,1,0:T(8,128)(2,1)} %get-tuple-element.269), calls=%async_computation.33 | async-start | bytes 655360 | tf_op jit(solution)/shard_map/all_to_all | solution.py:206
  564.6 1.9 copy-start.4
  568.5 72.6 %all-to-all-start.34 = ((f32[32,1,128]{2,1,0:T(1,128)}), f32[32,1,128]{2,1,0:T(1,128)S(1)}, u32[]{:S(2)}, u32[]{:S(2)}) async-start(f32[32,1,128]{2,1,0:T(1,128)} %broadcast_in_dim.107), calls=%async_computation.34 | async-start | bytes 32768 | tf_op jit(solution)/shard_map/all_to_all | solution.py:227
  634.2 27.7 %collective-permute-start.21 = (bf16[80,192]{1,0:T(8,128)(2,1)S(1)}, bf16[80,192]{1,0:T(8,128)(2,1)S(1)}, u32[]{:S(2)}, u32[]{:S(2)}) collective-permute-start(bf16[80,192]{1,0:T(8,128)(2,1)S(1)} %broadcast_select_fusion.10), channel_id=1, source_target_pairs={{0,1},{1,0},{2,3},{3,2},{4,5},{5,4},{6,7},{7,6},{8,9},{9,8},{10,11... | collective-permute-start | bytes 92168 | tf_op jit(solution)/shard_map/ppermute | solution.py:110
  641.7 31.4 %all-to-all-start.35 = ((f32[16,1,128]{2,1,0:T(1,128)}), f32[16,1,128]{2,1,0:T(1,128)S(1)}, u32[]{:S(2)}, u32[]{:S(2)}) async-start(f32[16,1,128]{2,1,0:T(1,128)} %broadcast_in_dim.108), calls=%async_computation.35 | async-start | bytes 16384 | tf_op jit(solution)/shard_map/all_to_all | solution.py:227

commit v3 on v1

v3 whole, which is shorter than its diff:
```python
import jax
import jax.numpy as jnp
from jax import lax
from jax.experimental import pallas as pl
from jax.experimental.pallas import tpu as pltpu
from jax.sharding import Mesh
from jax.sharding import PartitionSpec as P

D = 6144
HD = 64
DOCS = 8
MOST = 32
NEG = -1e30
PLANE = ("y", "x")
BF = jnp.bfloat16
F32 = jnp.float32


def iota(shape, axis):
    return lax.broadcasted_iota(jnp.int32, shape, axis)


def in_core_order(own, other):
    first = lax.axis_index("core") == 0
    return jnp.concatenate([jnp.where(first, own, other), jnp.where(first, other, own)], -1)


def dot(a, b, contract=((1,), (0,))):
    return lax.dot_general(a, b, (contract, ((), ())), preferred_element_type=F32)


def prepare(doc_ref, own_ref, other_ref, pick_ref, bias_ref, rows_ref, flag_ref):
    _, part, count = pick_ref.shape
    length = rows_ref.shape[1]
    doc_j = jnp.broadcast_to(doc_ref[...].astype(F32), (count, count))
    same = jnp.where(doc_j == jnp.transpose(doc_j), 1.0, 0.0)
    before = jnp.where(iota((count, count), 0) < iota((count, count), 1), same, 0.0)
    starts = jnp.sum(before, 0, keepdims=True) == 0.0
    lane = iota((1, count), 1)
    far = (jnp.abs(lane - count // 2) * count + lane).astype(F32)
    nearest = jnp.min(jnp.where(starts, far, float(count * count)), -1, keepdims=True)
    cut = nearest - count * jnp.floor(nearest / count)
    token = iota((part, count), 1).astype(F32)
    slot = iota((part, count), 0).astype(F32)
    picks = [
        jnp.where((token == slot) & (slot < cut), 1.0, 0.0),
        jnp.where(token == slot + cut, 1.0, 0.0),
    ]
    for core in range(2):
        pick_ref[core] = picks[core].astype(BF)
    pick = jnp.where(lax.axis_index("core") == 0, picks[0], picks[1])
    pick_bf = pick.astype(BF)
    rows = in_core_order(dot(pick_bf, own_ref[...]), dot(pick_bf, other_ref[...])).astype(F32)
    for number in range(part // length):
        rows_ref[number] = rows[number * length : (number + 1) * length].astype(BF)
    shifted = jnp.concatenate([jnp.zeros((length, count), F32), pick[: part - length]], 0)
    same_bf = same.astype(BF)
    for number, (queries, keys) in enumerate(((pick[:length], shifted), (pick[length:], pick))):
        alike = dot(dot(queries.astype(BF), same_bf).astype(BF), keys.astype(BF), ((1,), (1,)))
        query_at = iota((length, part), 0) + length
        key_at = iota((length, part), 1)
        allowed = ((alike > 0.5) & (key_at <= query_at)) | (key_at == query_at)
        bias_ref[number] = jnp.where(allowed, 0.0, NEG)
    section = lax.axis_index("section")
    row = iota(flag_ref.shape, 0)
    order = jnp.where(row == 0, -section, 0)
    flag_ref[...] = jnp.where((row == 1) & (section == 0), 1, order).astype(F32)


def qkv_attention(
    flag_ref,
    rows_ref,
    gain_ref,
    w_ref,
    bias_ref,
    kin_ref,
    vin_ref,
    send_ref,
    kout_ref,
    vout_ref,
    next_ref,
):
    chips, length, cols = rows_ref.shape
    width = kin_ref.shape[1]
    heads = width // HD
    total = jnp.zeros((length, cols), F32)
    for chip in range(chips):
        total += rows_ref[chip].astype(F32)
    mean = jnp.sum(total, -1, keepdims=True) / (chips * cols)
    total = jnp.zeros((length, cols), F32)
    for chip in range(chips):
        centered = rows_ref[chip].astype(F32) - mean
        total += centered * centered
    scale = lax.rsqrt(jnp.sum(total, -1, keepdims=True) / (chips * cols) + 1e-05)
    acc = jnp.zeros((length, 2 * width), F32)
    for chip in range(chips):
        span = slice(chip * cols, (chip + 1) * cols)
        centered = rows_ref[chip].astype(F32) - mean
        normed = (centered * scale * gain_ref[:, span]).astype(BF)
        acc += dot(normed, w_ref[span, :])
    rounded = acc.astype(BF).astype(F32)
    qk, val = rounded[:, :width], rounded[:, width:]
    head_of = iota((length, width), 1) // HD
    squares = qk * qk
    inverse = jnp.zeros((length, width), F32)
    stack = []
    for head in range(heads):
        mine = head_of == head
        square_mean = jnp.sum(jnp.where(mine, squares, 0.0), -1, keepdims=True) / HD
        inverse = jnp.where(mine, lax.rsqrt(square_mean + 1e-06), inverse)
        stack.append(jnp.where(mine, qk, 0.0))
    key = (qk * inverse).astype(BF).astype(F32)
    queries = jnp.concatenate(stack, 0).astype(BF)
    keys = jnp.concatenate([kin_ref[...], key], 0).astype(BF)
    vals = jnp.concatenate([vin_ref[...], val], 0).astype(BF)
    bias = jnp.where(flag_ref[0:1, 0:1] > 0.0, bias_ref[1], bias_ref[0])
    scores = dot(queries, keys, ((1,), (1,))) / HD + jnp.concatenate([bias] * heads, 0)
    peak = jnp.max(scores, -1, keepdims=True)
    expo = jnp.exp(scores - peak)
    weights = (expo / jnp.sum(expo, -1, keepdims=True)).astype(BF)
    mixed = dot(weights, vals)
    attended = jnp.zeros((length, width), F32)
    for head in range(heads):
        attended = jnp.where(head_of == head, mixed[head * length : (head + 1) * length], attended)
    half = width // 2
    attended = in_core_order(attended[:, :half], attended[:, half:]).astype(BF)
    for chip in range(chips):
        send_ref[chip] = attended
    kout_ref[...] = key
    vout_ref[...] = val
    next_ref[...] = flag_ref[...] + jnp.where(iota(flag_ref.shape, 0) == 0, 1.0, 0.0)


def pack(*refs):
    *parts, out_ref = refs
    begin = 0
    for ref in parts:
        out_ref[:, begin : begin + ref.shape[1]] = ref[...]
        begin += ref.shape[1]


def project_out(flag_ref, heads_ref, w_ref, rows_ref, kept_ref, out_ref, done_ref):
    chips, _, width = heads_ref.shape
    mixed = jnp.zeros(rows_ref.shape, F32)
    for chip in range(chips):
        mixed += dot(heads_ref[chip], w_ref[chip * width : (chip + 1) * width, :])
    rows = (rows_ref[...].astype(F32) + mixed).astype(BF)
    out_ref[...] = rows
    for number in range(kept_ref.shape[0]):
        mine = flag_ref[0:1, 0:1] == float(number)
        done_ref[number] = jnp.where(mine, rows.astype(F32), kept_ref[number].astype(F32)).astype(BF)


def spread(flag_ref, tokens_ref, received_ref, rows_ref, send_ref):
    first = flag_ref[1:2, 0:1] > 0.0
    rows = jnp.where(first, tokens_ref[...].astype(F32), received_ref[...].astype(F32)).astype(BF)
    rows_ref[...] = rows
    for chip in range(send_ref.shape[0]):
        send_ref[chip] = rows


def aim(pick_ref, own_ref, other_ref, goal_ref):
    pick = pick_ref[lax.axis_index("core")]
    goal_ref[...] = in_core_order(dot(pick, own_ref[...]), dot(pick, other_ref[...]))


def token_errors(pick_ref, done_ref, goal_ref, send_ref):
    slices, length, cols = done_ref.shape
    pick = pick_ref[lax.axis_index("core")].astype(F32)
    total = jnp.zeros((1, pick.shape[1]), F32)
    for number in range(slices):
        span = slice(number * length, (number + 1) * length)
        diff = done_ref[number].astype(F32) - goal_ref[span, :]
        sums = jnp.sum(diff * diff, -1, keepdims=True)
        total += jnp.sum(jnp.where(pick[span] > 0.0, sums, 0.0), 0, keepdims=True)
    last = lax.axis_index("section") == lax.axis_size("section") - 1
    total = jnp.where(last, total, 0.0)
    for number in range(send_ref.shape[0]):
        send_ref[number] = total


def add_up(pieces_ref, send_ref):
    total = pieces_ref[0]
    for number in range(1, pieces_ref.shape[0]):
        total += pieces_ref[number]
    for number in range(send_ref.shape[0]):
        send_ref[number] = total


def finish_losses(pieces_ref, doc_ref, loss_ref):
    total = pieces_ref[0]
    for number in range(1, pieces_ref.shape[0]):
        total += pieces_ref[number]
    count = doc_ref.shape[1]
    mine = doc_ref[...] == iota((DOCS, count), 0)
    sums = jnp.sum(jnp.where(mine, total, 0.0), -1, keepdims=True)
    tokens = jnp.sum(jnp.where(mine, 1.0, 0.0), -1, keepdims=True)
    loss_ref[...] = jnp.broadcast_to(sums / (tokens * D), (DOCS, count))


def place_back(pick_ref, parts_ref, out_ref):
    out_ref[...] = (
        dot(pick_ref[0], parts_ref[0], ((0,), (0,))) + dot(pick_ref[1], parts_ref[1], ((0,), (0,)))
    ).astype(BF)


VMEM = pl.BlockSpec(memory_space=pltpu.VMEM)


def run(kernel, outs, *args, flops=0, bytes_accessed=1 << 16):
    several = isinstance(outs, list)
    shapes = [jax.ShapeDtypeStruct(shape, kind) for shape, kind in (outs if several else [outs])]
    return pl.pallas_call(
        kernel,
        out_shape=shapes if several else shapes[0],
        in_specs=[VMEM] * len(args),
        out_specs=[VMEM] * len(shapes) if several else VMEM,
        compiler_params=pltpu.CompilerParams(vmem_limit_bytes=24 * 1024 * 1024),
        cost_estimate=pl.CostEstimate(flops=flops, bytes_accessed=bytes_accessed, transcendentals=0),
    )(*args)


def local(tokens, targets, doc_ids, norm_gains, w_qk, w_val, w_out):
    core = lax.axis_index("core")
    sections = lax.axis_size("section")
    chips = lax.axis_size("y") * lax.axis_size("x")
    row_count, cols_own = tokens.shape
    cols = 2 * cols_own
    width = 2 * w_qk.shape[2]
    slices = 2
    length = (row_count // 2 + MOST // 2) // slices
    part = slices * length

    def swap(value):
        return lax.ppermute(value, "core", [(0, 1), (1, 0)])

    docs = doc_ids.reshape(1, row_count)
    picks, bias, first_parts, flags = run(
        prepare,
        [
            ((2, part, row_count), BF),
            ((slices, length, part), F32),
            ((slices, length, cols), BF),
            ((8, 128), F32),
        ],
        docs,
        tokens,
        swap(tokens),
    )

    keys = jnp.zeros((length, width), F32)
    vals = jnp.zeros((length, width), F32)
    done = jnp.zeros((slices, length, cols), BF)
    received = jnp.zeros((length, cols), BF)
    goal = w_last = w_in = None
    for step in range(sections + slices - 1):
        rows, send = run(
            spread,
            [((length, cols), BF), ((chips, length, cols), BF)],
            flags,
            first_parts[min(step, slices - 1)],
            received,
        )
        if step == 0:
            w_qk, w_val, w_out, targets, send = lax.optimization_barrier((w_qk, w_val, w_out, targets, send))
            w_in = run(pack, ((D, 2 * width), BF), w_qk[0], swap(w_qk[0]), w_val[0], swap(w_val[0]))
            w_out_t = jnp.swapaxes(w_out[0], 0, 1)
            w_out_other = swap(w_out_t)
            targets_other = swap(targets)
        gathered = lax.all_to_all(send, PLANE, 0, 0, tiled=True)
        send, keys, vals, next_flags = run(
            qkv_attention,
            [((chips, length, width), BF), ((length, width), F32), ((length, width), F32), ((8, 128), F32)],
            flags,
            gathered,
            norm_gains,
            w_in,
            bias,
            keys,
            vals,
            flops=4 * length * D * width,
            bytes_accessed=4 * D * width,
        )
        if step == 0:
            w_out_t, send = lax.optimization_barrier((w_out_t, send))
            w_last = jnp.concatenate(
                [jnp.where(core == 0, w_out_t, w_out_other), jnp.where(core == 0, w_out_other, w_out_t)], 0
            )
            w_last = jnp.swapaxes(w_last, 0, 1)
            goal = run(aim, ((part, cols), F32), picks, targets, targets_other)
        attended = lax.all_to_all(send, PLANE, 0, 0, tiled=True)
        if step == 0:
            attended, goal, w_last, first_parts = lax.optimization_barrier((attended, goal, w_last, first_parts))
        rows, done = run(
            project_out,
            [((length, cols), BF), ((slices, length, cols), BF)],
            flags,
            attended,
            w_last,
            rows,
            done,
            flops=2 * length * chips * width * cols,
            bytes_accessed=2 * chips * width * cols,
        )
        flags = next_flags
        hops = [(z, z + 1) for z in range(sections - 1) if 0 <= step - z < slices]
        if hops:
            received = lax.ppermute(rows, "section", hops)

    send = run(token_errors, ((2 * chips, 1, row_count), F32), picks, done, goal)
    send = lax.all_to_all(send, PLANE + ("core",), 0, 0, tiled=True)
    send = run(add_up, ((sections, 1, row_count), F32), send)
    send = lax.all_to_all(send, "section", 0, 0, tiled=True)
    losses = run(finish_losses, ((DOCS, row_count), F32), send, docs)[:, 0]

    part_rows = done.reshape(part, cols)
    halves = [part_rows[:, :cols_own], part_rows[:, cols_own:]]
    keep = jnp.where(core == 0, halves[0], halves[1])
    other = swap(jnp.where(core == 0, halves[1], halves[0]))
    parts = jnp.stack([jnp.where(core == 0, keep, other), jnp.where(core == 0, other, keep)])
    section_rows = run(place_back, ((row_count, cols_own), BF), picks, parts)
    return (section_rows[None], losses)


def solution(mesh):
    names = ("section", "y", "x", "core")
    fine = Mesh(mesh.devices.reshape(mesh.devices.shape[0], 4, 4, 2), names)
    tensor = ("y", "x", "core")
    placed = (
        P(None, tensor),
        P(None, tensor),
        P(),
        P("section", None),
        P("section", None, tensor),
        P("section", None, tensor),
        P("section", None, tensor),
    )
    return jax.shard_map(
        local,
        mesh=fine,
        in_specs=placed,
        out_specs=(P("section", None, tensor), P()),
        check_vma=False,
    )
```

time: 793 us -> 638 us (0.80)
  blocking collectives: 164 us -> 380 us
  waiting for transfers between devices: 176 us -> 13.4 us
  starting transfers between devices: 261 us -> 151 us
  local copies, waits for them, and re-layouts: 90.6 us -> 23.1 us
  other arithmetic: 16.7 us -> 4.94 us
  Pallas kernels: 62.6 us -> 53.8 us
    all_to_all x0 -> x17, blocking collectives: none -> 205 us  [the longest x16 195 us: local(): gathered = lax.all_to_all(send, PLANE, 0, 0, tiled=True)]
    all_to_all x19 -> x2, waiting for transfers between devices: 154 us -> 10.2 us  [the longest x1 10.2 us: local(): send = lax.all_to_all(send, 'section', 0, 0, tiled=True)]
    unnamed x236 -> x28, local copies, waits for them, and re-layouts: 71.1 us -> 13.8 us
    ppermute x16, starting transfers between devices: 71.2 us -> 14.2 us  [local(): received = lax.ppermute(rows, 'section', hops)]
    all_to_all x19 -> x2, starting transfers between devices: 103 us -> 64.6 us  [the longest x1 61 us: local(): send = lax.all_to_all(send, 'section', 0, 0, tiled=True)]
    broadcast_in_dim x19 -> x2, local copies, waits for them, and re-layouts: 15.6 us -> 0.01 us  [the longest x1 0.01 us: local(): done = jnp.zeros((slices, length, cols), BF)]
    ppermute x16, waiting for transfers between devices: 15.8 us -> 1.99 us  [local(): received = lax.ppermute(rows, 'section', hops)]
    ppermute x6, starting transfers between devices: 75.5 us -> 64.9 us  [swap(): return lax.ppermute(value, 'core', [(0, 1), (1, 0)])]
  transfers between devices with their start and end apart: 43 -> 25, of which waited for: 36 -> 5; matrix products, arithmetic and copies ran while one was open for 3% -> 2% of each run, Pallas kernels for 1% -> 1%
where the time goes in v3:
time: 638 us; the launch traced here: 628 us
  blocking collectives  380 us (60%)
  starting transfers between devices  151 us (24%)
  Pallas kernels  53.8 us (8%)
  local copies, waits for them, and re-layouts  23.1 us (4%)
  waiting for transfers between devices  13.4 us (2%)
    all_to_all x16, blocking collectives, local(): gathered = lax.all_to_all(send, PLANE, 0, 0, tiled=True)  195 us
    all_to_all x16, blocking collectives, local(): attended = lax.all_to_all(send, PLANE, 0, 0, tiled=True)  175 us
    ppermute x6, starting transfers between devices, swap(): return lax.ppermute(value, 'core', [(0, 1), (1, 0)])  64.9 us
    all_to_all x1, starting transfers between devices, local(): send = lax.all_to_all(send, 'section', 0, 0, tiled=True)  61 us
    pallas_call x58, Pallas kernels, run(): pl.pallas_call(kernel, out_shape=shapes if several else shapes[0], in_spe...  53.8 us
    ppermute x16, starting transfers between devices, local(): received = lax.ppermute(rows, 'section', hops)  14.2 us
    unnamed x28, local copies, waits for them, and re-layouts  13.8 us
  transfers between devices with their start and end apart: 25, of which 5 were waited for; matrix products, arithmetic and copies ran while one was open for 2% of the time, Pallas kernels for 1%

profile of v3, /device:TPU:1, one launch (start us, length us, event | category | flops | bytes accessed | tf_op | source)
XLA Modules:
  0.0 627.6 jit_solution(926840050699466042)
XLA Ops:
  1.5 8.8 %collective-permute-start = (bf16[128,192]{1,0:T(8,128)(2,1)S(1)}, bf16[128,192]{1,0:T(8,128)(2,1)S(1)}, u32[]{:S(2)}, u32[]{:S(2)}) collective-permute-start(bf16[128,192]{1,0:T(8,128)(2,1)S(1)} %copy.22.own_ref), channel_id=1, source_target_pairs={{0,1},{1,0},{2,3},{3,2},{4,5},{5,4},{6,7},{7,6},{8,9},{9,8},{10,11... | collective-permute-start | bytes 147464 | tf_op jit(solution)/shard_map/ppermute | solution.py:235
  13.3 2.3 collective-permute-start.1
  15.5 2.1 collective-permute-start.2
  17.6 2.3 collective-permute-start.4
  19.9 3.6 all-to-all-start
  24.5 2.1 collective-permute-start.3
  26.6 3.8 copy.23
  32.1 3.0 shard_map.88.w_ref
  35.1 2.6 copy-done
  37.7 2.8 copy-done.1
  40.5 2.8 shard_map.89
  43.3 7.0 %all-to-all-start.1 = ((bf16[16,40,256]{2,1,0:T(8,128)(2,1)}), bf16[16,40,256]{2,1,0:T(8,128)(2,1)S(1)}, u32[]{:S(2)}, u32[]{:S(2)}) async-start(bf16[16,40,256]{2,1,0:T(8,128)(2,1)} %get-tuple-element.160), calls=%async_computation.1 | async-start | bytes 655360 | tf_op jit(solution)/shard_map/all_to_all | solution.py:291
  50.3 3.8 copy.27
  56.0 2.9 maximum_bitcast_fusion.w_ref
  64.5 15.7 %all_to_all.180.rows_ref = bf16[16,40,384]{2,1,0:T(8,128)(2,1)S(1)} all-to-all(bf16[16,40,384]{2,1,0:T(8,128)(2,1)S(1)} %get-tuple-element.168), channel_id=1, replica_groups=mesh['section'=16,'y'=4,'x'=4,'core'=2] {'y','x'}, dimensions={0} | all-to-all | bytes 983040 | tf_op jit(solution)/shard_map/all_to_all | solution.py:270
  80.3 2.8 copy-done.2
  83.1 2.1 shard_map.93
  85.1 10.7 %all_to_all.181.heads_ref = bf16[16,40,256]{2,1,0:T(8,128)(2,1)S(1)} all-to-all(bf16[16,40,256]{2,1,0:T(8,128)(2,1)S(1)} %get-tuple-element.172), channel_id=1, replica_groups=mesh['section'=16,'y'=4,'x'=4,'core'=2] {'y','x'}, dimensions={0} | all-to-all | bytes 655360 | tf_op jit(solution)/shard_map/all_to_all | solution.py:291
  96.5 3.2 collective-permute-start.6
  100.7 11.4 %all_to_all.182.rows_ref = bf16[16,40,384]{2,1,0:T(8,128)(2,1)S(1)} all-to-all(bf16[16,40,384]{2,1,0:T(8,128)(2,1)S(1)} %get-tuple-element.176), channel_id=1, replica_groups=mesh['section'=16,'y'=4,'x'=4,'core'=2] {'y','x'}, dimensions={0} | all-to-all | bytes 983040 | tf_op jit(solution)/shard_map/all_to_all | solution.py:270
  112.2 2.1 shard_map.96
  114.2 10.5 %all_to_all.183.heads_ref = bf16[16,40,256]{2,1,0:T(8,128)(2,1)S(1)} all-to-all(bf16[16,40,256]{2,1,0:T(8,128)(2,1)S(1)} %get-tuple-element.180), channel_id=1, replica_groups=mesh['section'=16,'y'=4,'x'=4,'core'=2] {'y','x'}, dimensions={0} | all-to-all | bytes 655360 | tf_op jit(solution)/shard_map/all_to_all | solution.py:291
  126.1 11.9 %all_to_all.184.rows_ref = bf16[16,40,384]{2,1,0:T(8,128)(2,1)S(1)} all-to-all(bf16[16,40,384]{2,1,0:T(8,128)(2,1)S(1)} %get-tuple-element.184), channel_id=1, replica_groups=mesh['section'=16,'y'=4,'x'=4,'core'=2] {'y','x'}, dimensions={0} | all-to-all | bytes 983040 | tf_op jit(solution)/shard_map/all_to_all | solution.py:270
  140.1 10.5 %all_to_all.185.heads_ref = bf16[16,40,256]{2,1,0:T(8,128)(2,1)S(1)} all-to-all(bf16[16,40,256]{2,1,0:T(8,128)(2,1)S(1)} %get-tuple-element.188), channel_id=1, replica_groups=mesh['section'=16,'y'=4,'x'=4,'core'=2] {'y','x'}, dimensions={0} | all-to-all | bytes 655360 | tf_op jit(solution)/shard_map/all_to_all | solution.py:291
  152.0 11.5 %all_to_all.186.rows_ref = bf16[16,40,384]{2,1,0:T(8,128)(2,1)S(1)} all-to-all(bf16[16,40,384]{2,1,0:T(8,128)(2,1)S(1)} %get-tuple-element.192), channel_id=1, replica_groups=mesh['section'=16,'y'=4,'x'=4,'core'=2] {'y','x'}, dimensions={0} | all-to-all | bytes 983040 | tf_op jit(solution)/shard_map/all_to_all | solution.py:270
  163.4 2.1 shard_map.102
  165.5 11.3 %all_to_all.187.heads_ref = bf16[16,40,256]{2,1,0:T(8,128)(2,1)S(1)} all-to-all(bf16[16,40,256]{2,1,0:T(8,128)(2,1)S(1)} %get-tuple-element.196), channel_id=1, replica_groups=mesh['section'=16,'y'=4,'x'=4,'core'=2] {'y','x'}, dimensions={0} | all-to-all | bytes 655360 | tf_op jit(solution)/shard_map/all_to_all | solution.py:291
  178.2 13.5 %all_to_all.188.rows_ref = bf16[16,40,384]{2,1,0:T(8,128)(2,1)S(1)} all-to-all(bf16[16,40,384]{2,1,0:T(8,128)(2,1)S(1)} %get-tuple-element.200), channel_id=1, replica_groups=mesh['section'=16,'y'=4,'x'=4,'core'=2] {'y','x'}, dimensions={0} | all-to-all | bytes 983040 | tf_op jit(solution)/shard_map/all_to_all | solution.py:270
  191.7 2.1 shard_map.105
  193.7 12.1 %all_to_all.189.heads_ref = bf16[16,40,256]{2,1,0:T(8,128)(2,1)S(1)} all-to-all(bf16[16,40,256]{2,1,0:T(8,128)(2,1)S(1)} %get-tuple-element.204), channel_id=1, replica_groups=mesh['section'=16,'y'=4,'x'=4,'core'=2] {'y','x'}, dimensions={0} | all-to-all | bytes 655360 | tf_op jit(solution)/shard_map/all_to_all | solution.py:291
  207.2 11.7 %all_to_all.190.rows_ref = bf16[16,40,384]{2,1,0:T(8,128)(2,1)S(1)} all-to-all(bf16[16,40,384]{2,1,0:T(8,128)(2,1)S(1)} %get-tuple-element.208), channel_id=1, replica_groups=mesh['section'=16,'y'=4,'x'=4,'core'=2] {'y','x'}, dimensions={0} | all-to-all | bytes 983040 | tf_op jit(solution)/shard_map/all_to_all | solution.py:270
  218.9 2.1 shard_map.108
  220.9 10.5 %all_to_all.191.heads_ref = bf16[16,40,256]{2,1,0:T(8,128)(2,1)S(1)} all-to-all(bf16[16,40,256]{2,1,0:T(8,128)(2,1)S(1)} %get-tuple-element.212), channel_id=1, replica_groups=mesh['section'=16,'y'=4,'x'=4,'core'=2] {'y','x'}, dimensions={0} | all-to-all | bytes 655360 | tf_op jit(solution)/shard_map/all_to_all | solution.py:291
  232.8 11.6 %all_to_all.192.rows_ref = bf16[16,40,384]{2,1,0:T(8,128)(2,1)S(1)} all-to-all(bf16[16,40,384]{2,1,0:T(8,128)(2,1)S(1)} %get-tuple-element.216), channel_id=1, replica_groups=mesh['section'=16,'y'=4,'x'=4,'core'=2] {'y','x'}, dimensions={0} | all-to-all | bytes 983040 | tf_op jit(solution)/shard_map/all_to_all | solution.py:270
  244.5 2.1 shard_map.111
  246.5 10.5 %all_to_all.193.heads_ref = bf16[16,40,256]{2,1,0:T(8,128)(2,1)S(1)} all-to-all(bf16[16,40,256]{2,1,0:T(8,128)(2,1)S(1)} %get-tuple-element.220), channel_id=1, replica_groups=mesh['section'=16,'y'=4,'x'=4,'core'=2] {'y','x'}, dimensions={0} | all-to-all | bytes 655360 | tf_op jit(solution)/shard_map/all_to_all | solution.py:291
  258.4 11.6 %all_to_all.194.rows_ref = bf16[16,40,384]{2,1,0:T(8,128)(2,1)S(1)} all-to-all(bf16[16,40,384]{2,1,0:T(8,128)(2,1)S(1)} %get-tuple-element.224), channel_id=1, replica_groups=mesh['section'=16,'y'=4,'x'=4,'core'=2] {'y','x'}, dimensions={0} | all-to-all | bytes 983040 | tf_op jit(solution)/shard_map/all_to_all | solution.py:270
  270.0 2.1 shard_map.114
  272.1 10.5 %all_to_all.195.heads_ref = bf16[16,40,256]{2,1,0:T(8,128)(2,1)S(1)} all-to-all(bf16[16,40,256]{2,1,0:T(8,128)(2,1)S(1)} %get-tuple-element.228), channel_id=1, replica_groups=mesh['section'=16,'y'=4,'x'=4,'core'=2] {'y','x'}, dimensions={0} | all-to-all | bytes 655360 | tf_op jit(solution)/shard_map/all_to_all | solution.py:291
  284.0 11.4 %all_to_all.196.rows_ref = bf16[16,40,384]{2,1,0:T(8,128)(2,1)S(1)} all-to-all(bf16[16,40,384]{2,1,0:T(8,128)(2,1)S(1)} %get-tuple-element.232), channel_id=1, replica_groups=mesh['section'=16,'y'=4,'x'=4,'core'=2] {'y','x'}, dimensions={0} | all-to-all | bytes 983040 | tf_op jit(solution)/shard_map/all_to_all | solution.py:270
  297.5 10.5 %all_to_all.197.heads_ref = bf16[16,40,256]{2,1,0:T(8,128)(2,1)S(1)} all-to-all(bf16[16,40,256]{2,1,0:T(8,128)(2,1)S(1)} %get-tuple-element.236), channel_id=1, replica_groups=mesh['section'=16,'y'=4,'x'=4,'core'=2] {'y','x'}, dimensions={0} | all-to-all | bytes 655360 | tf_op jit(solution)/shard_map/all_to_all | solution.py:291
  309.4 13.3 %all_to_all.198.rows_ref = bf16[16,40,384]{2,1,0:T(8,128)(2,1)S(1)} all-to-all(bf16[16,40,384]{2,1,0:T(8,128)(2,1)S(1)} %get-tuple-element.240), channel_id=1, replica_groups=mesh['section'=16,'y'=4,'x'=4,'core'=2] {'y','x'}, dimensions={0} | all-to-all | bytes 983040 | tf_op jit(solution)/shard_map/all_to_all | solution.py:270
  322.7 2.1 shard_map.120
  324.7 11.5 %all_to_all.199.heads_ref = bf16[16,40,256]{2,1,0:T(8,128)(2,1)S(1)} all-to-all(bf16[16,40,256]{2,1,0:T(8,128)(2,1)S(1)} %get-tuple-element.244), channel_id=1, replica_groups=mesh['section'=16,'y'=4,'x'=4,'core'=2] {'y','x'}, dimensions={0} | all-to-all | bytes 655360 | tf_op jit(solution)/shard_map/all_to_all | solution.py:291
  337.6 12.6 %all_to_all.200.rows_ref = bf16[16,40,384]{2,1,0:T(8,128)(2,1)S(1)} all-to-all(bf16[16,40,384]{2,1,0:T(8,128)(2,1)S(1)} %get-tuple-element.248), channel_id=1, replica_groups=mesh['section'=16,'y'=4,'x'=4,'core'=2] {'y','x'}, dimensions={0} | all-to-all | bytes 983040 | tf_op jit(solution)/shard_map/all_to_all | solution.py:270
  352.3 10.7 %all_to_all.201.heads_ref = bf16[16,40,256]{2,1,0:T(8,128)(2,1)S(1)} all-to-all(bf16[16,40,256]{2,1,0:T(8,128)(2,1)S(1)} %get-tuple-element.252), channel_id=1, replica_groups=mesh['section'=16,'y'=4,'x'=4,'core'=2] {'y','x'}, dimensions={0} | all-to-all | bytes 655360 | tf_op jit(solution)/shard_map/all_to_all | solution.py:291
  364.4 11.9 %all_to_all.202.rows_ref = bf16[16,40,384]{2,1,0:T(8,128)(2,1)S(1)} all-to-all(bf16[16,40,384]{2,1,0:T(8,128)(2,1)S(1)} %get-tuple-element.256), channel_id=1, replica_groups=mesh['section'=16,'y'=4,'x'=4,'core'=2] {'y','x'}, dimensions={0} | all-to-all | bytes 983040 | tf_op jit(solution)/shard_map/all_to_all | solution.py:270
  376.3 2.1 shard_map.126
  378.3 10.5 %all_to_all.203.heads_ref = bf16[16,40,256]{2,1,0:T(8,128)(2,1)S(1)} all-to-all(bf16[16,40,256]{2,1,0:T(8,128)(2,1)S(1)} %get-tuple-element.260), channel_id=1, replica_groups=mesh['section'=16,'y'=4,'x'=4,'core'=2] {'y','x'}, dimensions={0} | all-to-all | bytes 655360 | tf_op jit(solution)/shard_map/all_to_all | solution.py:291
  390.2 11.6 %all_to_all.204.rows_ref = bf16[16,40,384]{2,1,0:T(8,128)(2,1)S(1)} all-to-all(bf16[16,40,384]{2,1,0:T(8,128)(2,1)S(1)} %get-tuple-element.264), channel_id=1, replica_groups=mesh['section'=16,'y'=4,'x'=4,'core'=2] {'y','x'}, dimensions={0} | all-to-all | bytes 983040 | tf_op jit(solution)/shard_map/all_to_all | solution.py:270
  403.9 10.5 %all_to_all.205.heads_ref = bf16[16,40,256]{2,1,0:T(8,128)(2,1)S(1)} all-to-all(bf16[16,40,256]{2,1,0:T(8,128)(2,1)S(1)} %get-tuple-element.268), channel_id=1, replica_groups=mesh['section'=16,'y'=4,'x'=4,'core'=2] {'y','x'}, dimensions={0} | all-to-all | bytes 655360 | tf_op jit(solution)/shard_map/all_to_all | solution.py:291
  415.8 11.4 %all_to_all.206.rows_ref = bf16[16,40,384]{2,1,0:T(8,128)(2,1)S(1)} all-to-all(bf16[16,40,384]{2,1,0:T(8,128)(2,1)S(1)} %get-tuple-element.272), channel_id=1, replica_groups=mesh['section'=16,'y'=4,'x'=4,'core'=2] {'y','x'}, dimensions={0} | all-to-all | bytes 983040 | tf_op jit(solution)/shard_map/all_to_all | solution.py:270
  427.2 2.1 shard_map.132
  429.3 10.5 %all_to_all.207.heads_ref = bf16[16,40,256]{2,1,0:T(8,128)(2,1)S(1)} all-to-all(bf16[16,40,256]{2,1,0:T(8,128)(2,1)S(1)} %get-tuple-element.276), channel_id=1, replica_groups=mesh['section'=16,'y'=4,'x'=4,'core'=2] {'y','x'}, dimensions={0} | all-to-all | bytes 655360 | tf_op jit(solution)/shard_map/all_to_all | solution.py:291
  441.2 12.2 %all_to_all.208.rows_ref = bf16[16,40,384]{2,1,0:T(8,128)(2,1)S(1)} all-to-all(bf16[16,40,384]{2,1,0:T(8,128)(2,1)S(1)} %get-tuple-element.280), channel_id=1, replica_groups=mesh['section'=16,'y'=4,'x'=4,'core'=2] {'y','x'}, dimensions={0} | all-to-all | bytes 983040 | tf_op jit(solution)/shard_map/all_to_all | solution.py:270
  453.4 2.1 shard_map.135
  455.5 12.6 %all_to_all.209.heads_ref = bf16[16,40,256]{2,1,0:T(8,128)(2,1)S(1)} all-to-all(bf16[16,40,256]{2,1,0:T(8,128)(2,1)S(1)} %get-tuple-element.284), channel_id=1, replica_groups=mesh['section'=16,'y'=4,'x'=4,'core'=2] {'y','x'}, dimensions={0} | all-to-all | bytes 655360 | tf_op jit(solution)/shard_map/all_to_all | solution.py:291
  469.5 12.0 %all_to_all.210.rows_ref = bf16[16,40,384]{2,1,0:T(8,128)(2,1)S(1)} all-to-all(bf16[16,40,384]{2,1,0:T(8,128)(2,1)S(1)} %get-tuple-element.288), channel_id=1, replica_groups=mesh['section'=16,'y'=4,'x'=4,'core'=2] {'y','x'}, dimensions={0} | all-to-all | bytes 983040 | tf_op jit(solution)/shard_map/all_to_all | solution.py:270
  481.5 2.5 shard_map.138
  484.0 11.0 %all_to_all.211.heads_ref = bf16[16,40,256]{2,1,0:T(8,128)(2,1)S(1)} all-to-all(bf16[16,40,256]{2,1,0:T(8,128)(2,1)S(1)} %get-tuple-element.291), channel_id=1, replica_groups=mesh['section'=16,'y'=4,'x'=4,'core'=2] {'y','x'}, dimensions={0} | all-to-all | bytes 655360 | tf_op jit(solution)/shard_map/all_to_all | solution.py:291
  496.3 47.5 %collective-permute-start.21 = (bf16[80,192]{1,0:T(8,128)(2,1)S(1)}, bf16[80,192]{1,0:T(8,128)(2,1)S(1)}, u32[]{:S(2)}, u32[]{:S(2)}) collective-permute-start(bf16[80,192]{1,0:T(8,128)(2,1)S(1)} %broadcast_select_fusion.2), channel_id=1, source_target_pairs={{0,1},{1,0},{2,3},{3,2},{4,5},{5,4},{6,7},{7,6},{8,9},{9,8},{10,11... | collective-permute-start | bytes 92168 | tf_op jit(solution)/shard_map/ppermute | solution.py:235
  543.9 10.0 %all_to_all.212.pieces_ref = f32[32,1,128]{2,1,0:T(1,128)S(1)} all-to-all(f32[32,1,128]{2,1,0:T(1,128)S(1)} %shard_map.141), channel_id=1, replica_groups=mesh['section'=16,'y'=4,'x'=4,'core'=2] {'y','x','core'}, dimensions={0} | all-to-all | bytes 32768 | tf_op jit(solution)/shard_map/all_to_all | solution.py:311
  554.5 61.0 %all-to-all-start.35 = ((f32[16,1,128]{2,1,0:T(1,128)}), f32[16,1,128]{2,1,0:T(1,128)S(1)}, u32[]{:S(2)}, u32[]{:S(2)}) async-start(f32[16,1,128]{2,1,0:T(1,128)} %shard_map.142), calls=%async_computation.35 | async-start | bytes 16384 | tf_op jit(solution)/shard_map/all_to_all | solution.py:313
  616.5 10.2 %all-to-all-done.35.pieces_ref = f32[16,1,128]{2,1,0:T(1,128)S(1)} async-done(((f32[16,1,128]{2,1,0:T(1,128)}), f32[16,1,128]{2,1,0:T(1,128)S(1)}, u32[]{:S(2)}, u32[]{:S(2)}) %all-to-all-start.35) | async-done | bytes 8224 | tf_op jit(solution)/shard_map/all_to_all | solution.py:313
  (120 shorter events, 46.5 us)
Async XLA Ops:
  1.5 9.7 %collective-permute-start = (bf16[128,192]{1,0:T(8,128)(2,1)S(1)}, bf16[128,192]{1,0:T(8,128)(2,1)S(1)}, u32[]{:S(2)}, u32[]{:S(2)}) collective-permute-start(bf16[128,192]{1,0:T(8,128)(2,1)S(1)} %copy.22.own_ref), channel_id=1, source_target_pairs={{0,1},{1,0},{2,3},{3,2},{4,5},{5,4},{6,7},{7,6},{8,9},{9,8},{10,11... | collective-permute-start | bytes 147464 | tf_op jit(solution)/shard_map/ppermute | solution.py:235
  11.2 0.7 copy-start.8
  13.3 17.4 %collective-permute-start.1 = (bf16[6144,128]{1,0:T(8,128)(2,1)}, bf16[6144,128]{1,0:T(8,128)(2,1)}, u32[]{:S(2)}, u32[]{:S(2)}) collective-permute-start(bf16[6144,128]{1,0:T(8,128)(2,1)} %bitcast.21), channel_id=1, source_target_pairs={{0,1},{1,0},{2,3},{3,2},{4,5},{5,4},{6,7},{7,6},{8,9},{9,8},{10,11... | collective-permute-start | bytes 4718600 | tf_op jit(solution)/shard_map/ppermute | solution.py:235
  15.5 15.2 %collective-permute-start.2 = (bf16[6144,128]{1,0:T(8,128)(2,1)}, bf16[6144,128]{1,0:T(8,128)(2,1)}, u32[]{:S(2)}, u32[]{:S(2)}) collective-permute-start(bf16[6144,128]{1,0:T(8,128)(2,1)} %bitcast.23), channel_id=1, source_target_pairs={{0,1},{1,0},{2,3},{3,2},{4,5},{5,4},{6,7},{7,6},{8,9},{9,8},{10,11... | collective-permute-start | bytes 4718600 | tf_op jit(solution)/shard_map/ppermute | solution.py:235
  17.6 32.7 %collective-permute-start.4 = (bf16[192,4096]{1,0:T(8,128)(2,1)}, bf16[192,4096]{1,0:T(8,128)(2,1)}, u32[]{:S(2)}, u32[]{:S(2)}) collective-permute-start(bf16[192,4096]{1,0:T(8,128)(2,1)} %bitcast.31), channel_id=1, source_target_pairs={{0,1},{1,0},{2,3},{3,2},{4,5},{5,4},{6,7},{7,6},{8,9},{9,8},{10,11... | collective-permute-start | bytes 4718600 | tf_op jit(solution)/shard_map/ppermute | solution.py:235
  19.9 17.8 %all-to-all-start = ((bf16[16,40,384]{2,1,0:T(8,128)(2,1)}), bf16[16,40,384]{2,1,0:T(8,128)(2,1)S(1)}, u32[]{:S(2)}, u32[]{:S(2)}) async-start(bf16[16,40,384]{2,1,0:T(8,128)(2,1)} %get-tuple-element.153), calls=%async_computation | async-start | bytes 983040 | tf_op jit(solution)/shard_map/all_to_all | solution.py:270
  23.4 7.2 %copy-start.6 = (bf16[1,6144,128]{2,1,0:T(8,128)(2,1)S(1)}, bf16[1,6144,128]{2,1,0:T(8,128)(2,1)}, u32[]{:S(2)}) copy-start(bf16[1,6144,128]{2,1,0:T(8,128)(2,1)} %param.11) | copy-start | bytes 4718596
  24.5 5.9 collective-permute-start.3
  30.6 7.0 %copy-start.5 = (f32[1,6144]{1,0:T(1,128)S(1)}, f32[1,6144]{1,0:T(1,128)}, u32[]{:S(2)}) copy-start(f32[1,6144]{1,0:T(1,128)} %gain_ref.33) | copy-start | bytes 73732
  30.7 1.4 copy-start.7
  35.1 2.6 copy-start
  37.7 2.8 copy-start.1
  43.3 10.9 %copy-start.10 = (bf16[1,4096,192]{2,1,0:T(8,128)(2,1)S(1)}, bf16[1,4096,192]{2,1,0:T(8,128)(2,1)}, u32[]{:S(2)}) copy-start(bf16[1,4096,192]{2,1,0:T(8,128)(2,1)} %copy.23) | copy-start | bytes 4718596
  43.3 16.0 %all-to-all-start.1 = ((bf16[16,40,256]{2,1,0:T(8,128)(2,1)}), bf16[16,40,256]{2,1,0:T(8,128)(2,1)S(1)}, u32[]{:S(2)}, u32[]{:S(2)}) async-start(bf16[16,40,256]{2,1,0:T(8,128)(2,1)} %get-tuple-element.160), calls=%async_computation.1 | async-start | bytes 655360 | tf_op jit(solution)/shard_map/all_to_all | solution.py:291
  56.0 56.1 %slice-start = ((s8[6291456]{0:T(1024)(128)(4,1)}), s8[2097152]{0:T(1024)(128)(4,1)S(1)}, s32[]{:S(2)}) async-start(s8[6291456]{0:T(1024)(128)(4,1)} %bitcast.19), calls=%async_computation.36 | async-start | bytes 4194304
  59.3 1.9 copy-start.3
  61.8 2.7 collective-permute-start.5
  80.3 2.8 copy-start.2
  83.1 12.8 %copy-start.4 = (bf16[4096,384]{1,0:T(8,128)(2,1)S(1)}, bf16[4096,384]{1,0:T(8,128)(2,1)}, u32[]{:S(2)}) copy-start(bf16[4096,384]{1,0:T(8,128)(2,1)} %maximum_bitcast_fusion.w_ref) | copy-start | bytes 9437188
  83.1 29.1 %slice-start.1 = ((s8[6291456]{0:T(1024)(128)(4,1)}), s8[4194304]{0:T(1024)(128)(4,1)S(1)}, s32[]{:S(2)}) async-start(s8[6291456]{0:T(1024)(128)(4,1)} %bitcast.19), calls=%async_computation.37 | async-start | bytes 8388608
  96.5 4.2 collective-permute-start.6
  125.4 0.7 collective-permute-start.7
  151.2 0.7 collective-permute-start.8
  177.4 0.7 collective-permute-start.9
  206.4 0.7 collective-permute-start.10
  232.0 0.7 collective-permute-start.11
  257.7 0.7 collective-permute-start.12
  283.2 0.7 collective-permute-start.13
  308.6 0.7 collective-permute-start.14
  336.8 0.7 collective-permute-start.15
  363.6 0.7 collective-permute-start.16
  389.4 0.7 collective-permute-start.17
  415.0 0.7 collective-permute-start.18
  440.4 0.7 collective-permute-start.19
  468.7 0.7 collective-permute-start.20
  495.0 131.7 %copy-start.9 = (s32[128]{0:T(128)S(1)}, s32[128]{0:T(128)}, u32[]{:S(2)}) copy-start(s32[128]{0:T(128)} %param.9) | copy-start | bytes 1540
  496.3 119.2 %collective-permute-start.21 = (bf16[80,192]{1,0:T(8,128)(2,1)S(1)}, bf16[80,192]{1,0:T(8,128)(2,1)S(1)}, u32[]{:S(2)}, u32[]{:S(2)}) collective-permute-start(bf16[80,192]{1,0:T(8,128)(2,1)S(1)} %broadcast_select_fusion.2), channel_id=1, source_target_pairs={{0,1},{1,0},{2,3},{3,2},{4,5},{5,4},{6,7},{7,6},{8,9},{9,8},{10,11... | collective-permute-start | bytes 92168 | tf_op jit(solution)/shard_map/ppermute | solution.py:235
  554.5 72.2 %all-to-all-start.35 = ((f32[16,1,128]{2,1,0:T(1,128)}), f32[16,1,128]{2,1,0:T(1,128)S(1)}, u32[]{:S(2)}, u32[]{:S(2)}) async-start(f32[16,1,128]{2,1,0:T(1,128)} %shard_map.142), calls=%async_computation.35 | async-start | bytes 16384 | tf_op jit(solution)/shard_map/all_to_all | solution.py:313

commit v4 on v3

--- a/solution.py
+++ b/solution.py
@@ -50,7 +50,7 @@
         pick_ref[core] = picks[core].astype(BF)
     pick = jnp.where(lax.axis_index("core") == 0, picks[0], picks[1])
     pick_bf = pick.astype(BF)
-    rows = in_core_order(dot(pick_bf, own_ref[...]), dot(pick_bf, other_ref[...])).astype(F32)
+    rows = in_core_order(*[dot(pick_bf, ref[...], ((1,), (1,))) for ref in (own_ref, other_ref)])
     for number in range(part // length):
         rows_ref[number] = rows[number * length : (number + 1) * length].astype(BF)
     shifted = jnp.concatenate([jnp.zeros((length, count), F32), pick[: part - length]], 0)
@@ -131,12 +131,29 @@
     next_ref[...] = flag_ref[...] + jnp.where(iota(flag_ref.shape, 0) == 0, 1.0, 0.0)
 
 
-def pack(*refs):
-    *parts, out_ref = refs
-    begin = 0
-    for ref in parts:
-        out_ref[:, begin : begin + ref.shape[1]] = ref[...]
-        begin += ref.shape[1]
+def stage(qk_ref, qk_other_ref, val_ref, val_other_ref, out_ref, out_other_ref, in_ref, last_ref, *scratch):
+    own, other, packed, turned, sems = scratch
+    width = qk_ref.shape[1]
+    copies = [(out_ref, own), (out_other_ref, other)]
+    for number, ref in enumerate((qk_ref, qk_other_ref, val_ref, val_other_ref)):
+        copies.append((ref, packed.at[:, pl.ds(number * width, width)]))
+    copies += [(packed, in_ref), (turned, last_ref)]
+    copies = [pltpu.make_async_copy(*pair, sems.at[number]) for number, pair in enumerate(copies)]
+    for copy in copies[:6]:
+        copy.start()
+    for copy in copies[:6]:
+        copy.wait()
+    copies[6].start()
+    block = 256
+    first = lax.axis_index("core") == 0
+    for begin in range(0, own.shape[1], block):
+        span = slice(begin, begin + block)
+        here, there = own[:, span], other[:, span]
+        here, there = jnp.where(first, here, there), jnp.where(first, there, here)
+        turned[span, :] = jnp.transpose(jnp.concatenate([here, there], 0))
+    copies[7].start()
+    copies[6].wait()
+    copies[7].wait()
 
 
 def project_out(flag_ref, heads_ref, w_ref, rows_ref, kept_ref, out_ref, done_ref):
@@ -151,9 +168,13 @@
         done_ref[number] = jnp.where(mine, rows.astype(F32), kept_ref[number].astype(F32)).astype(BF)
 
 
-def spread(flag_ref, tokens_ref, received_ref, rows_ref, send_ref):
-    first = flag_ref[1:2, 0:1] > 0.0
-    rows = jnp.where(first, tokens_ref[...].astype(F32), received_ref[...].astype(F32)).astype(BF)
+def spread(flag_ref, tokens_ref, *refs):
+    *received_refs, rows_ref, send_ref = refs
+    rows = tokens_ref[...].astype(F32)
+    for number, received_ref in enumerate(received_refs):
+        here = (flag_ref[0:1, 0:1] == float(number)) & (flag_ref[1:2, 0:1] == 0.0)
+        rows = jnp.where(here, received_ref[...].astype(F32), rows)
+    rows = rows.astype(BF)
     rows_ref[...] = rows
     for chip in range(send_ref.shape[0]):
         send_ref[chip] = rows
@@ -161,7 +182,7 @@
 
 def aim(pick_ref, own_ref, other_ref, goal_ref):
     pick = pick_ref[lax.axis_index("core")]
-    goal_ref[...] = in_core_order(dot(pick, own_ref[...]), dot(pick, other_ref[...]))
+    goal_ref[...] = in_core_order(*[dot(pick, ref[...], ((1,), (1,))) for ref in (own_ref, other_ref)])
 
 
 def token_errors(pick_ref, done_ref, goal_ref, send_ref):
@@ -235,6 +256,7 @@
         return lax.ppermute(value, "core", [(0, 1), (1, 0)])
 
     docs = doc_ids.reshape(1, row_count)
+    tokens_t = jnp.swapaxes(tokens, 0, 1)
     picks, bias, first_parts, flags = run(
         prepare,
         [
@@ -244,14 +266,14 @@
             ((8, 128), F32),
         ],
         docs,
-        tokens,
-        swap(tokens),
+        tokens_t,
+        swap(tokens_t),
     )
 
     keys = jnp.zeros((length, width), F32)
     vals = jnp.zeros((length, width), F32)
     done = jnp.zeros((slices, length, cols), BF)
-    received = jnp.zeros((length, cols), BF)
+    received = []
     goal = w_last = w_in = None
     for step in range(sections + slices - 1):
         rows, send = run(
@@ -259,15 +281,38 @@
             [((length, cols), BF), ((chips, length, cols), BF)],
             flags,
             first_parts[min(step, slices - 1)],
-            received,
+            *received,
         )
         if step == 0:
             w_qk, w_val, w_out, targets, send = lax.optimization_barrier((w_qk, w_val, w_out, targets, send))
-            w_in = run(pack, ((D, 2 * width), BF), w_qk[0], swap(w_qk[0]), w_val[0], swap(w_val[0]))
-            w_out_t = jnp.swapaxes(w_out[0], 0, 1)
-            w_out_other = swap(w_out_t)
-            targets_other = swap(targets)
+            targets_t = jnp.swapaxes(targets, 0, 1)
+            targets_other = swap(targets_t)
+            targets_other, w_out = lax.optimization_barrier((targets_other, jnp.swapaxes(w_out[0], 0, 1)))
+            goal = run(aim, ((part, cols), F32), picks, targets_t, targets_other)
+            weights = [w_qk[0], swap(w_qk[0]), w_val[0], swap(w_val[0]), w_out, swap(w_out)]
         gathered = lax.all_to_all(send, PLANE, 0, 0, tiled=True)
+        if step == 0:
+            w_in, w_last = pl.pallas_call(
+                stage,
+                out_shape=[
+                    jax.ShapeDtypeStruct((D, 2 * width), BF),
+                    jax.ShapeDtypeStruct((chips * width, cols), BF),
+                ],
+                in_specs=[pl.BlockSpec(memory_space=pltpu.HBM)] * 6,
+                out_specs=[pl.BlockSpec(memory_space=pltpu.HBM)] * 2,
+                scratch_shapes=[
+                    pltpu.VMEM(w_out.shape, BF),
+                    pltpu.VMEM(w_out.shape, BF),
+                    pltpu.VMEM((D, 2 * width), BF),
+                    pltpu.VMEM((chips * width, cols), BF),
+                    pltpu.SemaphoreType.DMA((8,)),
+                ],
+                compiler_params=pltpu.CompilerParams(vmem_limit_bytes=60 * 1024 * 1024),
+                cost_estimate=pl.CostEstimate(flops=0, bytes_accessed=12 * D * width, transcendentals=0),
+            )(*weights)
+            gathered, goal, first_parts, w_in, w_last = lax.optimization_barrier(
+                (gathered, goal, first_parts, w_in, w_last)
+            )
         send, keys, vals, next_flags = run(
             qkv_attention,
             [((chips, length, width), BF), ((length, width), F32), ((length, width), F32), ((8, 128), F32)],
@@ -281,16 +326,7 @@
             flops=4 * length * D * width,
             bytes_accessed=4 * D * width,
         )
-        if step == 0:
-            w_out_t, send = lax.optimization_barrier((w_out_t, send))
-            w_last = jnp.concatenate(
-                [jnp.where(core == 0, w_out_t, w_out_other), jnp.where(core == 0, w_out_other, w_out_t)], 0
-            )
-            w_last = jnp.swapaxes(w_last, 0, 1)
-            goal = run(aim, ((part, cols), F32), picks, targets, targets_other)
         attended = lax.all_to_all(send, PLANE, 0, 0, tiled=True)
-        if step == 0:
-            attended, goal, w_last, first_parts = lax.optimization_barrier((attended, goal, w_last, first_parts))
         rows, done = run(
             project_out,
             [((length, cols), BF), ((slices, length, cols), BF)],
@@ -303,9 +339,10 @@
             bytes_accessed=2 * chips * width * cols,
         )
         flags = next_flags
-        hops = [(z, z + 1) for z in range(sections - 1) if 0 <= step - z < slices]
-        if hops:
-            received = lax.ppermute(rows, "section", hops)
+        hops = [step - number for number in range(slices)]
+        received = [
+            lax.ppermute(rows, "section", [(z, z + 1)]) if 0 <= z < sections - 1 else jnp.zeros_like(rows) for z in hops
+        ]
 
     send = run(token_errors, ((2 * chips, 1, row_count), F32), picks, done, goal)
     send = lax.all_to_all(send, PLANE + ("core",), 0, 0, tiled=True)

time: 638 us -> 634 us (level)
  local copies, waits for them, and re-layouts: 23.1 us -> 12.5 us
  waiting for transfers between devices: 13.4 us -> 21.8 us
    ppermute x16 -> x30, starting transfers between devices: 14.2 us -> 24.1 us  [local(): lax.ppermute(rows, 'section', [(z, z + 1)])]
    all_to_all x1, waiting for transfers between devices: 0.36 us -> 8.48 us  [local(): attended = lax.all_to_all(send, PLANE, 0, 0, tiled=True)]
    pallas_call x0 -> x1, Pallas kernels: none -> 7.56 us  [local(): pl.pallas_call(stage, out_shape=[jax.ShapeDtypeStruct((D, 2 * width), BF)...]
    pallas_call x58 -> x57, Pallas kernels: 53.8 us -> 49.5 us  [run(): pl.pallas_call(kernel, out_shape=shapes if several else shapes[0], in_spe...]
    unnamed x28 -> x41, local copies, waits for them, and re-layouts: 13.8 us -> 11.9 us
  transfers between devices with their start and end apart: 25 -> 39, of which waited for: 5 -> 6; matrix products, arithmetic and copies ran while one was open for 2% -> 0% of each run, Pallas kernels for 1% -> 1%
where the time goes in v4:
time: 634 us; the launch traced here: 624 us
  blocking collectives  377 us (59%)
  starting transfers between devices  153 us (24%)
  Pallas kernels  57.1 us (9%)
  waiting for transfers between devices  21.8 us (3%)
  local copies, waits for them, and re-layouts  12.5 us (2%)
    all_to_all x16, blocking collectives, local(): gathered = lax.all_to_all(send, PLANE, 0, 0, tiled=True)  190 us
    all_to_all x16, blocking collectives, local(): attended = lax.all_to_all(send, PLANE, 0, 0, tiled=True)  177 us
    ppermute x6, starting transfers between devices, swap(): return lax.ppermute(value, 'core', [(0, 1), (1, 0)])  66.1 us
    all_to_all x1, starting transfers between devices, local(): send = lax.all_to_all(send, 'section', 0, 0, tiled=True)  55.5 us
    pallas_call x57, Pallas kernels, run(): pl.pallas_call(kernel, out_shape=shapes if several else shapes[0], in_spe...  49.5 us
    ppermute x30, starting transfers between devices, local(): lax.ppermute(rows, 'section', [(z, z + 1)])  24.1 us
  transfers between devices with their start and end apart: 39, of which 6 were waited for; matrix products, arithmetic and copies ran while one was open for 0% of the time, Pallas kernels for 1%

profile of v4, /device:TPU:1, one launch (start us, length us, event | category | flops | bytes accessed | tf_op | source)
XLA Modules:
  0.0 623.5 jit_solution(6736496049789552907)
XLA Ops:
  0.6 8.8 %collective-permute-start = (bf16[192,128]{1,0:T(8,128)(2,1)}, bf16[192,128]{1,0:T(8,128)(2,1)S(1)}, u32[]{:S(2)}, u32[]{:S(2)}) collective-permute-start(bf16[192,128]{1,0:T(8,128)(2,1)} %bitcast.23), channel_id=1, source_target_pairs={{0,1},{1,0},{2,3},{3,2},{4,5},{5,4},{6,7},{7,6},{8,9},{9,8},{10,11... | collective-permute-start | bytes 147464 | tf_op jit(solution)/shard_map/ppermute | solution.py:256
  13.3 2.2 collective-permute-start.1
  15.6 2.1 collective-permute-start.2
  17.7 2.3 collective-permute-start.3
  19.9 2.1 collective-permute-start.4
  22.0 3.6 all-to-all-start
  27.9 7.6 %shard_map.89 = (bf16[6144,512]{1,0:T(8,128)(2,1)}, bf16[4096,384]{1,0:T(8,128)(2,1)}) custom-call(bf16[6144,128]{1,0:T(8,128)(2,1)} %bitcast.28, bf16[6144,128]{1,0:T(8,128)(2,1)} %copy-done.19, bf16[6144,128]{1,0:T(8,128)(2,1)} %bitcast.30, bf16[6144,128]{1,0:T(8,128)(2,1)} %collective-permute-done.3.val_other_ref, bf16[192,4096]{1,0:T(8,128)(2,1)} %bitcast.32, ...), custom_call_target="tpu_custom_call" | custom-call | bytes 18874368 | tf_op jit(solution)/shard_map/pallas_call | solution.py:295
  36.2 2.8 copy-done
  39.0 2.1 shard_map.90
  41.1 14.2 %all_to_all.180.heads_ref = bf16[16,40,256]{2,1,0:T(8,128)(2,1)S(1)} all-to-all(bf16[16,40,256]{2,1,0:T(8,128)(2,1)S(1)} %get-tuple-element.170), channel_id=1, replica_groups=mesh['section'=16,'y'=4,'x'=4,'core'=2] {'y','x'}, dimensions={0} | all-to-all | bytes 655360 | tf_op jit(solution)/shard_map/all_to_all | solution.py:329
  60.1 11.6 %all_to_all.181.rows_ref = bf16[16,40,384]{2,1,0:T(8,128)(2,1)S(1)} all-to-all(bf16[16,40,384]{2,1,0:T(8,128)(2,1)S(1)} %get-tuple-element.174), channel_id=1, replica_groups=mesh['section'=16,'y'=4,'x'=4,'core'=2] {'y','x'}, dimensions={0} | all-to-all | bytes 983040 | tf_op jit(solution)/shard_map/all_to_all | solution.py:293
  71.7 2.0 shard_map.93
  73.8 10.5 %all_to_all.182.heads_ref = bf16[16,40,256]{2,1,0:T(8,128)(2,1)S(1)} all-to-all(bf16[16,40,256]{2,1,0:T(8,128)(2,1)S(1)} %get-tuple-element.178), channel_id=1, replica_groups=mesh['section'=16,'y'=4,'x'=4,'core'=2] {'y','x'}, dimensions={0} | all-to-all | bytes 655360 | tf_op jit(solution)/shard_map/all_to_all | solution.py:329
  85.6 4.3 collective-permute-start.7
  90.9 11.4 %all_to_all.183.rows_ref = bf16[16,40,384]{2,1,0:T(8,128)(2,1)S(1)} all-to-all(bf16[16,40,384]{2,1,0:T(8,128)(2,1)S(1)} %get-tuple-element.182), channel_id=1, replica_groups=mesh['section'=16,'y'=4,'x'=4,'core'=2] {'y','x'}, dimensions={0} | all-to-all | bytes 983040 | tf_op jit(solution)/shard_map/all_to_all | solution.py:293
  102.4 2.0 shard_map.96
  104.4 10.5 %all_to_all.184.heads_ref = bf16[16,40,256]{2,1,0:T(8,128)(2,1)S(1)} all-to-all(bf16[16,40,256]{2,1,0:T(8,128)(2,1)S(1)} %get-tuple-element.186), channel_id=1, replica_groups=mesh['section'=16,'y'=4,'x'=4,'core'=2] {'y','x'}, dimensions={0} | all-to-all | bytes 655360 | tf_op jit(solution)/shard_map/all_to_all | solution.py:329
  117.0 11.4 %all_to_all.185.rows_ref = bf16[16,40,384]{2,1,0:T(8,128)(2,1)S(1)} all-to-all(bf16[16,40,384]{2,1,0:T(8,128)(2,1)S(1)} %get-tuple-element.190), channel_id=1, replica_groups=mesh['section'=16,'y'=4,'x'=4,'core'=2] {'y','x'}, dimensions={0} | all-to-all | bytes 983040 | tf_op jit(solution)/shard_map/all_to_all | solution.py:293
  128.4 2.0 shard_map.99
  130.5 10.5 %all_to_all.186.heads_ref = bf16[16,40,256]{2,1,0:T(8,128)(2,1)S(1)} all-to-all(bf16[16,40,256]{2,1,0:T(8,128)(2,1)S(1)} %get-tuple-element.194), channel_id=1, replica_groups=mesh['section'=16,'y'=4,'x'=4,'core'=2] {'y','x'}, dimensions={0} | all-to-all | bytes 655360 | tf_op jit(solution)/shard_map/all_to_all | solution.py:329
  143.0 12.2 %all_to_all.187.rows_ref = bf16[16,40,384]{2,1,0:T(8,128)(2,1)S(1)} all-to-all(bf16[16,40,384]{2,1,0:T(8,128)(2,1)S(1)} %get-tuple-element.198), channel_id=1, replica_groups=mesh['section'=16,'y'=4,'x'=4,'core'=2] {'y','x'}, dimensions={0} | all-to-all | bytes 983040 | tf_op jit(solution)/shard_map/all_to_all | solution.py:293
  155.2 2.1 shard_map.102
  157.3 12.3 %all_to_all.188.heads_ref = bf16[16,40,256]{2,1,0:T(8,128)(2,1)S(1)} all-to-all(bf16[16,40,256]{2,1,0:T(8,128)(2,1)S(1)} %get-tuple-element.202), channel_id=1, replica_groups=mesh['section'=16,'y'=4,'x'=4,'core'=2] {'y','x'}, dimensions={0} | all-to-all | bytes 655360 | tf_op jit(solution)/shard_map/all_to_all | solution.py:329
  171.6 12.7 %all_to_all.189.rows_ref = bf16[16,40,384]{2,1,0:T(8,128)(2,1)S(1)} all-to-all(bf16[16,40,384]{2,1,0:T(8,128)(2,1)S(1)} %get-tuple-element.206), channel_id=1, replica_groups=mesh['section'=16,'y'=4,'x'=4,'core'=2] {'y','x'}, dimensions={0} | all-to-all | bytes 983040 | tf_op jit(solution)/shard_map/all_to_all | solution.py:293
  184.4 2.1 shard_map.105
  186.4 10.6 %all_to_all.190.heads_ref = bf16[16,40,256]{2,1,0:T(8,128)(2,1)S(1)} all-to-all(bf16[16,40,256]{2,1,0:T(8,128)(2,1)S(1)} %get-tuple-element.210), channel_id=1, replica_groups=mesh['section'=16,'y'=4,'x'=4,'core'=2] {'y','x'}, dimensions={0} | all-to-all | bytes 655360 | tf_op jit(solution)/shard_map/all_to_all | solution.py:329
  199.1 11.6 %all_to_all.191.rows_ref = bf16[16,40,384]{2,1,0:T(8,128)(2,1)S(1)} all-to-all(bf16[16,40,384]{2,1,0:T(8,128)(2,1)S(1)} %get-tuple-element.214), channel_id=1, replica_groups=mesh['section'=16,'y'=4,'x'=4,'core'=2] {'y','x'}, dimensions={0} | all-to-all | bytes 983040 | tf_op jit(solution)/shard_map/all_to_all | solution.py:293
  210.7 2.0 shard_map.108
  212.7 10.5 %all_to_all.192.heads_ref = bf16[16,40,256]{2,1,0:T(8,128)(2,1)S(1)} all-to-all(bf16[16,40,256]{2,1,0:T(8,128)(2,1)S(1)} %get-tuple-element.218), channel_id=1, replica_groups=mesh['section'=16,'y'=4,'x'=4,'core'=2] {'y','x'}, dimensions={0} | all-to-all | bytes 655360 | tf_op jit(solution)/shard_map/all_to_all | solution.py:329
  225.3 11.4 %all_to_all.193.rows_ref = bf16[16,40,384]{2,1,0:T(8,128)(2,1)S(1)} all-to-all(bf16[16,40,384]{2,1,0:T(8,128)(2,1)S(1)} %get-tuple-element.222), channel_id=1, replica_groups=mesh['section'=16,'y'=4,'x'=4,'core'=2] {'y','x'}, dimensions={0} | all-to-all | bytes 983040 | tf_op jit(solution)/shard_map/all_to_all | solution.py:293
  236.7 2.0 shard_map.111
  238.8 10.5 %all_to_all.194.heads_ref = bf16[16,40,256]{2,1,0:T(8,128)(2,1)S(1)} all-to-all(bf16[16,40,256]{2,1,0:T(8,128)(2,1)S(1)} %get-tuple-element.226), channel_id=1, replica_groups=mesh['section'=16,'y'=4,'x'=4,'core'=2] {'y','x'}, dimensions={0} | all-to-all | bytes 655360 | tf_op jit(solution)/shard_map/all_to_all | solution.py:329
  251.3 11.4 %all_to_all.195.rows_ref = bf16[16,40,384]{2,1,0:T(8,128)(2,1)S(1)} all-to-all(bf16[16,40,384]{2,1,0:T(8,128)(2,1)S(1)} %get-tuple-element.230), channel_id=1, replica_groups=mesh['section'=16,'y'=4,'x'=4,'core'=2] {'y','x'}, dimensions={0} | all-to-all | bytes 983040 | tf_op jit(solution)/shard_map/all_to_all | solution.py:293
  262.7 2.0 shard_map.114
  264.8 10.5 %all_to_all.196.heads_ref = bf16[16,40,256]{2,1,0:T(8,128)(2,1)S(1)} all-to-all(bf16[16,40,256]{2,1,0:T(8,128)(2,1)S(1)} %get-tuple-element.234), channel_id=1, replica_groups=mesh['section'=16,'y'=4,'x'=4,'core'=2] {'y','x'}, dimensions={0} | all-to-all | bytes 655360 | tf_op jit(solution)/shard_map/all_to_all | solution.py:329
  277.4 11.9 %all_to_all.197.rows_ref = bf16[16,40,384]{2,1,0:T(8,128)(2,1)S(1)} all-to-all(bf16[16,40,384]{2,1,0:T(8,128)(2,1)S(1)} %get-tuple-element.238), channel_id=1, replica_groups=mesh['section'=16,'y'=4,'x'=4,'core'=2] {'y','x'}, dimensions={0} | all-to-all | bytes 983040 | tf_op jit(solution)/shard_map/all_to_all | solution.py:293
  289.3 2.1 shard_map.117
  291.4 11.3 %all_to_all.198.heads_ref = bf16[16,40,256]{2,1,0:T(8,128)(2,1)S(1)} all-to-all(bf16[16,40,256]{2,1,0:T(8,128)(2,1)S(1)} %get-tuple-element.242), channel_id=1, replica_groups=mesh['section'=16,'y'=4,'x'=4,'core'=2] {'y','x'}, dimensions={0} | all-to-all | bytes 655360 | tf_op jit(solution)/shard_map/all_to_all | solution.py:329
  304.7 13.3 %all_to_all.199.rows_ref = bf16[16,40,384]{2,1,0:T(8,128)(2,1)S(1)} all-to-all(bf16[16,40,384]{2,1,0:T(8,128)(2,1)S(1)} %get-tuple-element.246), channel_id=1, replica_groups=mesh['section'=16,'y'=4,'x'=4,'core'=2] {'y','x'}, dimensions={0} | all-to-all | bytes 983040 | tf_op jit(solution)/shard_map/all_to_all | solution.py:293
  317.9 2.1 shard_map.120
  320.0 11.1 %all_to_all.200.heads_ref = bf16[16,40,256]{2,1,0:T(8,128)(2,1)S(1)} all-to-all(bf16[16,40,256]{2,1,0:T(8,128)(2,1)S(1)} %get-tuple-element.250), channel_id=1, replica_groups=mesh['section'=16,'y'=4,'x'=4,'core'=2] {'y','x'}, dimensions={0} | all-to-all | bytes 655360 | tf_op jit(solution)/shard_map/all_to_all | solution.py:329
  333.1 11.7 %all_to_all.201.rows_ref = bf16[16,40,384]{2,1,0:T(8,128)(2,1)S(1)} all-to-all(bf16[16,40,384]{2,1,0:T(8,128)(2,1)S(1)} %get-tuple-element.254), channel_id=1, replica_groups=mesh['section'=16,'y'=4,'x'=4,'core'=2] {'y','x'}, dimensions={0} | all-to-all | bytes 983040 | tf_op jit(solution)/shard_map/all_to_all | solution.py:293
  344.8 2.1 shard_map.123
  346.8 10.5 %all_to_all.202.heads_ref = bf16[16,40,256]{2,1,0:T(8,128)(2,1)S(1)} all-to-all(bf16[16,40,256]{2,1,0:T(8,128)(2,1)S(1)} %get-tuple-element.258), channel_id=1, replica_groups=mesh['section'=16,'y'=4,'x'=4,'core'=2] {'y','x'}, dimensions={0} | all-to-all | bytes 655360 | tf_op jit(solution)/shard_map/all_to_all | solution.py:329
  359.4 11.4 %all_to_all.203.rows_ref = bf16[16,40,384]{2,1,0:T(8,128)(2,1)S(1)} all-to-all(bf16[16,40,384]{2,1,0:T(8,128)(2,1)S(1)} %get-tuple-element.262), channel_id=1, replica_groups=mesh['section'=16,'y'=4,'x'=4,'core'=2] {'y','x'}, dimensions={0} | all-to-all | bytes 983040 | tf_op jit(solution)/shard_map/all_to_all | solution.py:293
  370.8 2.0 shard_map.126
  372.9 10.5 %all_to_all.204.heads_ref = bf16[16,40,256]{2,1,0:T(8,128)(2,1)S(1)} all-to-all(bf16[16,40,256]{2,1,0:T(8,128)(2,1)S(1)} %get-tuple-element.266), channel_id=1, replica_groups=mesh['section'=16,'y'=4,'x'=4,'core'=2] {'y','x'}, dimensions={0} | all-to-all | bytes 655360 | tf_op jit(solution)/shard_map/all_to_all | solution.py:329
  385.4 11.4 %all_to_all.205.rows_ref = bf16[16,40,384]{2,1,0:T(8,128)(2,1)S(1)} all-to-all(bf16[16,40,384]{2,1,0:T(8,128)(2,1)S(1)} %get-tuple-element.270), channel_id=1, replica_groups=mesh['section'=16,'y'=4,'x'=4,'core'=2] {'y','x'}, dimensions={0} | all-to-all | bytes 983040 | tf_op jit(solution)/shard_map/all_to_all | solution.py:293
  396.9 2.0 shard_map.129
  398.9 10.5 %all_to_all.206.heads_ref = bf16[16,40,256]{2,1,0:T(8,128)(2,1)S(1)} all-to-all(bf16[16,40,256]{2,1,0:T(8,128)(2,1)S(1)} %get-tuple-element.274), channel_id=1, replica_groups=mesh['section'=16,'y'=4,'x'=4,'core'=2] {'y','x'}, dimensions={0} | all-to-all | bytes 655360 | tf_op jit(solution)/shard_map/all_to_all | solution.py:329
  411.5 11.6 %all_to_all.207.rows_ref = bf16[16,40,384]{2,1,0:T(8,128)(2,1)S(1)} all-to-all(bf16[16,40,384]{2,1,0:T(8,128)(2,1)S(1)} %get-tuple-element.278), channel_id=1, replica_groups=mesh['section'=16,'y'=4,'x'=4,'core'=2] {'y','x'}, dimensions={0} | all-to-all | bytes 983040 | tf_op jit(solution)/shard_map/all_to_all | solution.py:293
  423.1 2.0 shard_map.132
  425.2 10.8 %all_to_all.208.heads_ref = bf16[16,40,256]{2,1,0:T(8,128)(2,1)S(1)} all-to-all(bf16[16,40,256]{2,1,0:T(8,128)(2,1)S(1)} %get-tuple-element.282), channel_id=1, replica_groups=mesh['section'=16,'y'=4,'x'=4,'core'=2] {'y','x'}, dimensions={0} | all-to-all | bytes 655360 | tf_op jit(solution)/shard_map/all_to_all | solution.py:329
  438.0 12.9 %all_to_all.209.rows_ref = bf16[16,40,384]{2,1,0:T(8,128)(2,1)S(1)} all-to-all(bf16[16,40,384]{2,1,0:T(8,128)(2,1)S(1)} %get-tuple-element.286), channel_id=1, replica_groups=mesh['section'=16,'y'=4,'x'=4,'core'=2] {'y','x'}, dimensions={0} | all-to-all | bytes 983040 | tf_op jit(solution)/shard_map/all_to_all | solution.py:293
  451.0 2.1 shard_map.135
  453.0 12.1 %all_to_all.210.heads_ref = bf16[16,40,256]{2,1,0:T(8,128)(2,1)S(1)} all-to-all(bf16[16,40,256]{2,1,0:T(8,128)(2,1)S(1)} %get-tuple-element.290), channel_id=1, replica_groups=mesh['section'=16,'y'=4,'x'=4,'core'=2] {'y','x'}, dimensions={0} | all-to-all | bytes 655360 | tf_op jit(solution)/shard_map/all_to_all | solution.py:329
  466.5 11.7 %all_to_all.211.rows_ref = bf16[16,40,384]{2,1,0:T(8,128)(2,1)S(1)} all-to-all(bf16[16,40,384]{2,1,0:T(8,128)(2,1)S(1)} %get-tuple-element.294), channel_id=1, replica_groups=mesh['section'=16,'y'=4,'x'=4,'core'=2] {'y','x'}, dimensions={0} | all-to-all | bytes 983040 | tf_op jit(solution)/shard_map/all_to_all | solution.py:293
  478.2 2.5 shard_map.138
  481.5 3.5 all-to-all-start.33
  485.0 8.5 %all-to-all-done.33.heads_ref = bf16[16,40,256]{2,1,0:T(8,128)(2,1)S(1)} async-done(((bf16[16,40,256]{2,1,0:T(8,128)(2,1)}), bf16[16,40,256]{2,1,0:T(8,128)(2,1)S(1)}, u32[]{:S(2)}, u32[]{:S(2)}) %all-to-all-start.33) | async-done | bytes 327712 | tf_op jit(solution)/shard_map/all_to_all | solution.py:329
  496.4 48.7 %collective-permute-start.35 = (bf16[80,192]{1,0:T(8,128)(2,1)S(1)}, bf16[80,192]{1,0:T(8,128)(2,1)S(1)}, u32[]{:S(2)}, u32[]{:S(2)}) collective-permute-start(bf16[80,192]{1,0:T(8,128)(2,1)S(1)} %broadcast_select_fusion), channel_id=1, source_target_pairs={{0,1},{1,0},{2,3},{3,2},{4,5},{5,4},{6,7},{7,6},{8,9},{9,8},{10,11... | collective-permute-start | bytes 92168 | tf_op jit(solution)/shard_map/ppermute | solution.py:256
  545.2 9.9 %all_to_all.212.pieces_ref = f32[32,1,128]{2,1,0:T(1,128)S(1)} all-to-all(f32[32,1,128]{2,1,0:T(1,128)S(1)} %shard_map.141), channel_id=1, replica_groups=mesh['section'=16,'y'=4,'x'=4,'core'=2] {'y','x','core'}, dimensions={0} | all-to-all | bytes 32768 | tf_op jit(solution)/shard_map/all_to_all | solution.py:348
  555.7 55.5 %all-to-all-start.35 = ((f32[16,1,128]{2,1,0:T(1,128)}), f32[16,1,128]{2,1,0:T(1,128)S(1)}, u32[]{:S(2)}, u32[]{:S(2)}) async-start(f32[16,1,128]{2,1,0:T(1,128)} %shard_map.142), calls=%async_computation.35 | async-start | bytes 16384 | tf_op jit(solution)/shard_map/all_to_all | solution.py:350
  613.1 9.5 %all-to-all-done.35.pieces_ref = f32[16,1,128]{2,1,0:T(1,128)S(1)} async-done(((f32[16,1,128]{2,1,0:T(1,128)}), f32[16,1,128]{2,1,0:T(1,128)S(1)}, u32[]{:S(2)}, u32[]{:S(2)}) %all-to-all-start.35) | async-done | bytes 8224 | tf_op jit(solution)/shard_map/all_to_all | solution.py:350
  (155 shorter events, 47.9 us)
Async XLA Ops:
  0.6 9.9 %collective-permute-start = (bf16[192,128]{1,0:T(8,128)(2,1)}, bf16[192,128]{1,0:T(8,128)(2,1)S(1)}, u32[]{:S(2)}, u32[]{:S(2)}) collective-permute-start(bf16[192,128]{1,0:T(8,128)(2,1)} %bitcast.23), channel_id=1, source_target_pairs={{0,1},{1,0},{2,3},{3,2},{4,5},{5,4},{6,7},{7,6},{8,9},{9,8},{10,11... | collective-permute-start | bytes 147464 | tf_op jit(solution)/shard_map/ppermute | solution.py:256
  10.5 0.8 copy-start.14
  11.3 0.7 copy-start.17
  12.4 23.0 %copy-start.7 = (bf16[2,80,128]{2,1,0:T(8,128)(2,1)}, bf16[2,80,128]{2,1,0:T(8,128)(2,1)S(1)}, u32[]{:S(2)}) copy-start(bf16[2,80,128]{2,1,0:T(8,128)(2,1)S(1)} %get-tuple-element.152.pick_ref) | copy-start | bytes 122884
  13.3 6.6 %collective-permute-start.1 = (bf16[192,128]{1,0:T(8,128)(2,1)}, bf16[192,128]{1,0:T(8,128)(2,1)S(1)}, u32[]{:S(2)}, u32[]{:S(2)}) collective-permute-start(bf16[192,128]{1,0:T(8,128)(2,1)} %bitcast.21), channel_id=1, source_target_pairs={{0,1},{1,0},{2,3},{3,2},{4,5},{5,4},{6,7},{7,6},{8,9},{9,8},{10,11... | collective-permute-start | bytes 147464 | tf_op jit(solution)/shard_map/ppermute | solution.py:256
  15.6 11.1 %collective-permute-start.2 = (bf16[6144,128]{1,0:T(8,128)(2,1)}, bf16[6144,128]{1,0:T(8,128)(2,1)S(1)}, u32[]{:S(2)}, u32[]{:S(2)}) collective-permute-start(bf16[6144,128]{1,0:T(8,128)(2,1)} %bitcast.27), channel_id=1, source_target_pairs={{0,1},{1,0},{2,3},{3,2},{4,5},{5,4},{6,7},{7,6},{8,9},{9,8},{10,11... | collective-permute-start | bytes 4718600 | tf_op jit(solution)/shard_map/ppermute | solution.py:256
  17.7 9.1 %collective-permute-start.3 = (bf16[6144,128]{1,0:T(8,128)(2,1)}, bf16[6144,128]{1,0:T(8,128)(2,1)}, u32[]{:S(2)}, u32[]{:S(2)}) collective-permute-start(bf16[6144,128]{1,0:T(8,128)(2,1)} %bitcast.29), channel_id=1, source_target_pairs={{0,1},{1,0},{2,3},{3,2},{4,5},{5,4},{6,7},{7,6},{8,9},{9,8},{10,11... | collective-permute-start | bytes 4718600 | tf_op jit(solution)/shard_map/ppermute | solution.py:256
  19.9 6.8 %collective-permute-start.4 = (bf16[192,4096]{1,0:T(8,128)(2,1)}, bf16[192,4096]{1,0:T(8,128)(2,1)}, u32[]{:S(2)}, u32[]{:S(2)}) collective-permute-start(bf16[192,4096]{1,0:T(8,128)(2,1)} %bitcast.31), channel_id=1, source_target_pairs={{0,1},{1,0},{2,3},{3,2},{4,5},{5,4},{6,7},{7,6},{8,9},{9,8},{10,11... | collective-permute-start | bytes 4718600 | tf_op jit(solution)/shard_map/ppermute | solution.py:256
  22.0 14.2 %all-to-all-start = ((bf16[16,40,384]{2,1,0:T(8,128)(2,1)}), bf16[16,40,384]{2,1,0:T(8,128)(2,1)S(1)}, u32[]{:S(2)}, u32[]{:S(2)}) async-start(bf16[16,40,384]{2,1,0:T(8,128)(2,1)} %get-tuple-element.156), calls=%async_computation | async-start | bytes 983040 | tf_op jit(solution)/shard_map/all_to_all | solution.py:293
  25.6 0.8 copy-start.13
  26.7 8.8 %copy-start.5 = (f32[80,384]{1,0:T(8,128)}, f32[80,384]{1,0:T(8,128)S(1)}, u32[]{:S(2)}) copy-start(f32[80,384]{1,0:T(8,128)S(1)} %shard_map.88.goal_ref) | copy-start | bytes 368644
  26.7 9.6 %copy-start.4 = (f32[1,6144]{1,0:T(1,128)S(1)}, f32[1,6144]{1,0:T(1,128)}, u32[]{:S(2)}) copy-start(f32[1,6144]{1,0:T(1,128)} %gain_ref.33) | copy-start | bytes 73732
  26.7 1.2 copy-start.19
  36.2 2.8 copy-start
  39.0 32.7 %copy-start.1 = (bf16[6144,512]{1,0:T(8,128)(2,1)S(1)}, bf16[6144,512]{1,0:T(8,128)(2,1)}, u32[]{:S(2)}) copy-start(bf16[6144,512]{1,0:T(8,128)(2,1)} %get-tuple-element.166.w_ref) | copy-start | bytes 18874372
  55.3 1.9 copy-start.2
  57.7 2.3 collective-permute-start.5
  71.7 12.6 %copy-start.3 = (bf16[4096,384]{1,0:T(8,128)(2,1)S(1)}, bf16[4096,384]{1,0:T(8,128)(2,1)}, u32[]{:S(2)}) copy-start(bf16[4096,384]{1,0:T(8,128)(2,1)} %get-tuple-element.171.w_ref) | copy-start | bytes 9437188
  84.9 5.0 collective-permute-start.6
  85.6 5.3 collective-permute-start.7
  115.5 1.3 collective-permute-start.8
  116.2 0.7 collective-permute-start.9
  141.6 1.3 collective-permute-start.10
  142.2 0.7 collective-permute-start.11
  170.2 1.3 collective-permute-start.12
  170.8 0.7 collective-permute-start.13
  197.6 1.3 collective-permute-start.14
  198.3 0.7 collective-permute-start.15
  223.8 1.3 collective-permute-start.16
  224.5 0.7 collective-permute-start.17
  249.8 1.3 collective-permute-start.18
  250.5 0.7 collective-permute-start.19
  275.9 1.3 collective-permute-start.20
  276.6 0.7 collective-permute-start.21
  303.2 1.3 collective-permute-start.22
  303.9 0.7 collective-permute-start.23
  331.6 1.3 collective-permute-start.24
  332.3 0.7 collective-permute-start.25
  357.9 1.3 collective-permute-start.26
  358.6 0.7 collective-permute-start.27
  384.0 1.3 collective-permute-start.28
  384.6 0.7 collective-permute-start.29
  410.0 1.3 collective-permute-start.30
  410.7 0.7 collective-permute-start.31
  436.6 1.3 collective-permute-start.32
  437.2 0.7 collective-permute-start.33
  465.7 15.0 %copy-start.11 = (bf16[2,40,384]{2,1,0:T(8,128)(2,1)}, bf16[2,40,384]{2,1,0:T(8,128)(2,1)S(1)}, u32[]{:S(2)}) copy-start(bf16[2,40,384]{2,1,0:T(8,128)(2,1)S(1)} %get-tuple-element.299.kept_ref) | copy-start | bytes 184324
  465.8 0.7 collective-permute-start.34
  466.5 14.2 %copy-start.15 = (bf16[40,384]{1,0:T(8,128)(2,1)}, bf16[40,384]{1,0:T(8,128)(2,1)S(1)}, u32[]{:S(2)}) copy-start(bf16[40,384]{1,0:T(8,128)(2,1)S(1)} %get-tuple-element.298.rows_ref) | copy-start | bytes 92164
  480.8 0.7 copy-start.10
  481.5 12.0 %all-to-all-start.33 = ((bf16[16,40,256]{2,1,0:T(8,128)(2,1)}), bf16[16,40,256]{2,1,0:T(8,128)(2,1)S(1)}, u32[]{:S(2)}, u32[]{:S(2)}) async-start(bf16[16,40,256]{2,1,0:T(8,128)(2,1)} %copy-done.10), calls=%async_computation.33 | async-start | bytes 655360 | tf_op jit(solution)/shard_map/all_to_all | solution.py:329
  493.5 0.8 copy-start.12
  494.4 0.8 copy-start.16
  495.1 49.9 %copy-start.6 = (f32[80,384]{1,0:T(8,128)S(1)}, f32[80,384]{1,0:T(8,128)}, u32[]{:S(2)}) copy-start(f32[80,384]{1,0:T(8,128)} %copy-done.5) | copy-start | bytes 368644
  495.1 49.9 %copy-start.8 = (bf16[2,80,128]{2,1,0:T(8,128)(2,1)S(1)}, bf16[2,80,128]{2,1,0:T(8,128)(2,1)}, u32[]{:S(2)}) copy-start(bf16[2,80,128]{2,1,0:T(8,128)(2,1)} %copy-done.7) | copy-start | bytes 122884
  495.1 127.4 %copy-start.18 = (s32[128]{0:T(128)S(1)}, s32[128]{0:T(128)}, u32[]{:S(2)}) copy-start(s32[128]{0:T(128)} %param.9) | copy-start | bytes 1540
  496.4 114.9 %collective-permute-start.35 = (bf16[80,192]{1,0:T(8,128)(2,1)S(1)}, bf16[80,192]{1,0:T(8,128)(2,1)S(1)}, u32[]{:S(2)}, u32[]{:S(2)}) collective-permute-start(bf16[80,192]{1,0:T(8,128)(2,1)S(1)} %broadcast_select_fusion), channel_id=1, source_target_pairs={{0,1},{1,0},{2,3},{3,2},{4,5},{5,4},{6,7},{7,6},{8,9},{9,8},{10,11... | collective-permute-start | bytes 92168 | tf_op jit(solution)/shard_map/ppermute | solution.py:256
  555.7 66.8 %all-to-all-start.35 = ((f32[16,1,128]{2,1,0:T(1,128)}), f32[16,1,128]{2,1,0:T(1,128)S(1)}, u32[]{:S(2)}, u32[]{:S(2)}) async-start(f32[16,1,128]{2,1,0:T(1,128)} %shard_map.142), calls=%async_computation.35 | async-start | bytes 16384 | tf_op jit(solution)/shard_map/all_to_all | solution.py:350
  611.4 0.8 copy-start.9

commit v5 on v4

--- a/solution.py
+++ b/solution.py
@@ -171,7 +171,7 @@
 def spread(flag_ref, tokens_ref, *refs):
     *received_refs, rows_ref, send_ref = refs
     rows = tokens_ref[...].astype(F32)
-    for number, received_ref in enumerate(received_refs):
+    for number, received_ref in enumerate(reversed(received_refs)):
         here = (flag_ref[0:1, 0:1] == float(number)) & (flag_ref[1:2, 0:1] == 0.0)
         rows = jnp.where(here, received_ref[...].astype(F32), rows)
     rows = rows.astype(BF)
@@ -281,14 +281,11 @@
             [((length, cols), BF), ((chips, length, cols), BF)],
             flags,
             first_parts[min(step, slices - 1)],
-            *received,
+            *reversed(received),
         )
         if step == 0:
-            w_qk, w_val, w_out, targets, send = lax.optimization_barrier((w_qk, w_val, w_out, targets, send))
-            targets_t = jnp.swapaxes(targets, 0, 1)
-            targets_other = swap(targets_t)
-            targets_other, w_out = lax.optimization_barrier((targets_other, jnp.swapaxes(w_out[0], 0, 1)))
-            goal = run(aim, ((part, cols), F32), picks, targets_t, targets_other)
+            w_qk, w_val, w_out, send = lax.optimization_barrier((w_qk, w_val, w_out, send))
+            w_out = jnp.swapaxes(w_out[0], 0, 1)
             weights = [w_qk[0], swap(w_qk[0]), w_val[0], swap(w_val[0]), w_out, swap(w_out)]
         gathered = lax.all_to_all(send, PLANE, 0, 0, tiled=True)
         if step == 0:
@@ -310,9 +307,7 @@
                 compiler_params=pltpu.CompilerParams(vmem_limit_bytes=60 * 1024 * 1024),
                 cost_estimate=pl.CostEstimate(flops=0, bytes_accessed=12 * D * width, transcendentals=0),
             )(*weights)
-            gathered, goal, first_parts, w_in, w_last = lax.optimization_barrier(
-                (gathered, goal, first_parts, w_in, w_last)
-            )
+            gathered, first_parts, w_in, w_last = lax.optimization_barrier((gathered, first_parts, w_in, w_last))
         send, keys, vals, next_flags = run(
             qkv_attention,
             [((chips, length, width), BF), ((length, width), F32), ((length, width), F32), ((8, 128), F32)],
@@ -327,6 +322,8 @@
             bytes_accessed=4 * D * width,
         )
         attended = lax.all_to_all(send, PLANE, 0, 0, tiled=True)
+        if step == sections + slices - 2:
+            attended, picks, goal = lax.optimization_barrier((attended, picks, goal))
         rows, done = run(
             project_out,
             [((length, cols), BF), ((slices, length, cols), BF)],
@@ -339,13 +336,23 @@
             bytes_accessed=2 * chips * width * cols,
         )
         flags = next_flags
-        hops = [step - number for number in range(slices)]
-        received = [
-            lax.ppermute(rows, "section", [(z, z + 1)]) if 0 <= z < sections - 1 else jnp.zeros_like(rows) for z in hops
-        ]
+        received = {}
+        for number in reversed(range(slices)):
+            z = step - number
+            if 0 <= z < sections - 1:
+                received[number] = lax.ppermute(rows, "section", [(z, z + 1)])
+            else:
+                received[number] = jnp.zeros_like(rows)
+        received = [received[number] for number in range(slices)]
+        if step == sections // 2:
+            targets, rows = lax.optimization_barrier((targets, rows))
+            targets_t = jnp.swapaxes(targets, 0, 1)
+            goal = run(aim, ((part, cols), F32), picks, targets_t, swap(targets_t))
+            goal, picks, received = lax.optimization_barrier((goal, picks, received))
 
     send = run(token_errors, ((2 * chips, 1, row_count), F32), picks, done, goal)
     send = lax.all_to_all(send, PLANE + ("core",), 0, 0, tiled=True)
+    send, done = lax.optimization_barrier((send, done))
     send = run(add_up, ((sections, 1, row_count), F32), send)
     send = lax.all_to_all(send, "section", 0, 0, tiled=True)
     losses = run(finish_losses, ((DOCS, row_count), F32), send, docs)[:, 0]

time: 634 us -> 633 us (level)
    ppermute x6, starting transfers between devices: 66.1 us -> 44.4 us  [swap(): return lax.ppermute(value, 'core', [(0, 1), (1, 0)])]
    all_to_all x1, starting transfers between devices: 3.54 us -> 24.3 us  [local(): send = lax.all_to_all(send, PLANE + ('core',), 0, 0, tiled=True)]
    all_to_all x1 -> x0, blocking collectives: 9.95 us -> none  [local(): send = lax.all_to_all(send, PLANE + ('core',), 0, 0, tiled=True)]
    all_to_all x16 -> x17, blocking collectives: 177 us -> 187 us  [local(): attended = lax.all_to_all(send, PLANE, 0, 0, tiled=True)]
where the time goes in v5:
time: 633 us; the launch traced here: 623 us
  blocking collectives  378 us (60%)
  starting transfers between devices  154 us (24%)
  Pallas kernels  58.3 us (9%)
  waiting for transfers between devices  21.7 us (3%)
  local copies, waits for them, and re-layouts  8.85 us (1%)
    all_to_all x16, blocking collectives, local(): gathered = lax.all_to_all(send, PLANE, 0, 0, tiled=True)  191 us
    all_to_all x17, blocking collectives, local(): attended = lax.all_to_all(send, PLANE, 0, 0, tiled=True)  187 us
    all_to_all x1, starting transfers between devices, local(): send = lax.all_to_all(send, 'section', 0, 0, tiled=True)  57.7 us
    pallas_call x57, Pallas kernels, run(): pl.pallas_call(kernel, out_shape=shapes if several else shapes[0], in_spe...  50.7 us
    ppermute x6, starting transfers between devices, swap(): return lax.ppermute(value, 'core', [(0, 1), (1, 0)])  44.4 us
    all_to_all x1, starting transfers between devices, local(): send = lax.all_to_all(send, PLANE + ('core',), 0, 0, tiled=True)  24.3 us
    ppermute x30, starting transfers between devices, local(): received[number] = lax.ppermute(rows, 'section', [(z, z + 1)])  23.5 us
  transfers between devices with their start and end apart: 39, of which 6 were waited for; matrix products, arithmetic and copies ran while one was open for 0% of the time, Pallas kernels for 1%

profile of v5, /device:TPU:1, one launch (start us, length us, event | category | flops | bytes accessed | tf_op | source)
XLA Modules:
  0.0 622.5 jit_solution(255667958488870856)
XLA Ops:
  0.6 8.8 %collective-permute-start = (bf16[192,128]{1,0:T(8,128)(2,1)}, bf16[192,128]{1,0:T(8,128)(2,1)S(1)}, u32[]{:S(2)}, u32[]{:S(2)}) collective-permute-start(bf16[192,128]{1,0:T(8,128)(2,1)} %bitcast.23), channel_id=1, source_target_pairs={{0,1},{1,0},{2,3},{3,2},{4,5},{5,4},{6,7},{7,6},{8,9},{9,8},{10,11... | collective-permute-start | bytes 147464 | tf_op jit(solution)/shard_map/ppermute | solution.py:256
  13.3 2.2 collective-permute-start.1
  15.5 2.1 collective-permute-start.2
  17.6 2.3 collective-permute-start.3
  19.9 3.6 all-to-all-start
  24.7 7.5 %shard_map.88 = (bf16[6144,512]{1,0:T(8,128)(2,1)}, bf16[4096,384]{1,0:T(8,128)(2,1)}) custom-call(bf16[6144,128]{1,0:T(8,128)(2,1)} %bitcast.28, bf16[6144,128]{1,0:T(8,128)(2,1)} %copy-done.9, bf16[6144,128]{1,0:T(8,128)(2,1)} %bitcast.30, bf16[6144,128]{1,0:T(8,128)(2,1)} %collective-permute-done.2.val_other_ref, bf16[192,4096]{1,0:T(8,128)(2,1)} %bitcast.32, ...), custom_call_target="tpu_custom_call" | custom-call | bytes 18874368 | tf_op jit(solution)/shard_map/pallas_call | solution.py:292
  32.2 2.1 all-to-all-done.rows_ref
  34.3 2.8 copy-done
  37.1 2.1 shard_map.89
  39.2 13.0 %all_to_all.180.heads_ref = bf16[16,40,256]{2,1,0:T(8,128)(2,1)S(1)} all-to-all(bf16[16,40,256]{2,1,0:T(8,128)(2,1)S(1)} %get-tuple-element.172), channel_id=1, replica_groups=mesh['section'=16,'y'=4,'x'=4,'core'=2] {'y','x'}, dimensions={0} | all-to-all | bytes 655360 | tf_op jit(solution)/shard_map/all_to_all | solution.py:324
  57.1 11.7 %all_to_all.181.rows_ref = bf16[16,40,384]{2,1,0:T(8,128)(2,1)S(1)} all-to-all(bf16[16,40,384]{2,1,0:T(8,128)(2,1)S(1)} %get-tuple-element.176), channel_id=1, replica_groups=mesh['section'=16,'y'=4,'x'=4,'core'=2] {'y','x'}, dimensions={0} | all-to-all | bytes 983040 | tf_op jit(solution)/shard_map/all_to_all | solution.py:290
  68.8 2.1 shard_map.92
  70.8 10.5 %all_to_all.182.heads_ref = bf16[16,40,256]{2,1,0:T(8,128)(2,1)S(1)} all-to-all(bf16[16,40,256]{2,1,0:T(8,128)(2,1)S(1)} %get-tuple-element.180), channel_id=1, replica_groups=mesh['section'=16,'y'=4,'x'=4,'core'=2] {'y','x'}, dimensions={0} | all-to-all | bytes 655360 | tf_op jit(solution)/shard_map/all_to_all | solution.py:324
  81.9 3.6 collective-permute-start.5
  86.6 11.4 %all_to_all.183.rows_ref = bf16[16,40,384]{2,1,0:T(8,128)(2,1)S(1)} all-to-all(bf16[16,40,384]{2,1,0:T(8,128)(2,1)S(1)} %get-tuple-element.184), channel_id=1, replica_groups=mesh['section'=16,'y'=4,'x'=4,'core'=2] {'y','x'}, dimensions={0} | all-to-all | bytes 983040 | tf_op jit(solution)/shard_map/all_to_all | solution.py:290
  98.1 2.1 shard_map.95
  100.1 10.5 %all_to_all.184.heads_ref = bf16[16,40,256]{2,1,0:T(8,128)(2,1)S(1)} all-to-all(bf16[16,40,256]{2,1,0:T(8,128)(2,1)S(1)} %get-tuple-element.188), channel_id=1, replica_groups=mesh['section'=16,'y'=4,'x'=4,'core'=2] {'y','x'}, dimensions={0} | all-to-all | bytes 655360 | tf_op jit(solution)/shard_map/all_to_all | solution.py:324
  112.7 11.4 %all_to_all.185.rows_ref = bf16[16,40,384]{2,1,0:T(8,128)(2,1)S(1)} all-to-all(bf16[16,40,384]{2,1,0:T(8,128)(2,1)S(1)} %get-tuple-element.192), channel_id=1, replica_groups=mesh['section'=16,'y'=4,'x'=4,'core'=2] {'y','x'}, dimensions={0} | all-to-all | bytes 983040 | tf_op jit(solution)/shard_map/all_to_all | solution.py:290
  124.2 2.1 shard_map.98
  126.2 10.5 %all_to_all.186.heads_ref = bf16[16,40,256]{2,1,0:T(8,128)(2,1)S(1)} all-to-all(bf16[16,40,256]{2,1,0:T(8,128)(2,1)S(1)} %get-tuple-element.196), channel_id=1, replica_groups=mesh['section'=16,'y'=4,'x'=4,'core'=2] {'y','x'}, dimensions={0} | all-to-all | bytes 655360 | tf_op jit(solution)/shard_map/all_to_all | solution.py:324
  138.8 11.9 %all_to_all.187.rows_ref = bf16[16,40,384]{2,1,0:T(8,128)(2,1)S(1)} all-to-all(bf16[16,40,384]{2,1,0:T(8,128)(2,1)S(1)} %get-tuple-element.200), channel_id=1, replica_groups=mesh['section'=16,'y'=4,'x'=4,'core'=2] {'y','x'}, dimensions={0} | all-to-all | bytes 983040 | tf_op jit(solution)/shard_map/all_to_all | solution.py:290
  150.8 2.1 shard_map.101
  152.8 12.7 %all_to_all.188.heads_ref = bf16[16,40,256]{2,1,0:T(8,128)(2,1)S(1)} all-to-all(bf16[16,40,256]{2,1,0:T(8,128)(2,1)S(1)} %get-tuple-element.204), channel_id=1, replica_groups=mesh['section'=16,'y'=4,'x'=4,'core'=2] {'y','x'}, dimensions={0} | all-to-all | bytes 655360 | tf_op jit(solution)/shard_map/all_to_all | solution.py:324
  167.5 13.3 %all_to_all.189.rows_ref = bf16[16,40,384]{2,1,0:T(8,128)(2,1)S(1)} all-to-all(bf16[16,40,384]{2,1,0:T(8,128)(2,1)S(1)} %get-tuple-element.208), channel_id=1, replica_groups=mesh['section'=16,'y'=4,'x'=4,'core'=2] {'y','x'}, dimensions={0} | all-to-all | bytes 983040 | tf_op jit(solution)/shard_map/all_to_all | solution.py:290
  180.8 2.0 shard_map.104
  182.9 11.2 %all_to_all.190.heads_ref = bf16[16,40,256]{2,1,0:T(8,128)(2,1)S(1)} all-to-all(bf16[16,40,256]{2,1,0:T(8,128)(2,1)S(1)} %get-tuple-element.212), channel_id=1, replica_groups=mesh['section'=16,'y'=4,'x'=4,'core'=2] {'y','x'}, dimensions={0} | all-to-all | bytes 655360 | tf_op jit(solution)/shard_map/all_to_all | solution.py:324
  196.1 12.0 %all_to_all.191.rows_ref = bf16[16,40,384]{2,1,0:T(8,128)(2,1)S(1)} all-to-all(bf16[16,40,384]{2,1,0:T(8,128)(2,1)S(1)} %get-tuple-element.216), channel_id=1, replica_groups=mesh['section'=16,'y'=4,'x'=4,'core'=2] {'y','x'}, dimensions={0} | all-to-all | bytes 983040 | tf_op jit(solution)/shard_map/all_to_all | solution.py:290
  208.1 2.1 shard_map.107
  210.1 10.6 %all_to_all.192.heads_ref = bf16[16,40,256]{2,1,0:T(8,128)(2,1)S(1)} all-to-all(bf16[16,40,256]{2,1,0:T(8,128)(2,1)S(1)} %get-tuple-element.220), channel_id=1, replica_groups=mesh['section'=16,'y'=4,'x'=4,'core'=2] {'y','x'}, dimensions={0} | all-to-all | bytes 655360 | tf_op jit(solution)/shard_map/all_to_all | solution.py:324
  222.8 11.4 %all_to_all.193.rows_ref = bf16[16,40,384]{2,1,0:T(8,128)(2,1)S(1)} all-to-all(bf16[16,40,384]{2,1,0:T(8,128)(2,1)S(1)} %get-tuple-element.224), channel_id=1, replica_groups=mesh['section'=16,'y'=4,'x'=4,'core'=2] {'y','x'}, dimensions={0} | all-to-all | bytes 983040 | tf_op jit(solution)/shard_map/all_to_all | solution.py:290
  234.3 2.1 shard_map.110
  236.3 10.5 %all_to_all.194.heads_ref = bf16[16,40,256]{2,1,0:T(8,128)(2,1)S(1)} all-to-all(bf16[16,40,256]{2,1,0:T(8,128)(2,1)S(1)} %get-tuple-element.228), channel_id=1, replica_groups=mesh['section'=16,'y'=4,'x'=4,'core'=2] {'y','x'}, dimensions={0} | all-to-all | bytes 655360 | tf_op jit(solution)/shard_map/all_to_all | solution.py:324
  248.9 11.4 %all_to_all.195.rows_ref = bf16[16,40,384]{2,1,0:T(8,128)(2,1)S(1)} all-to-all(bf16[16,40,384]{2,1,0:T(8,128)(2,1)S(1)} %get-tuple-element.232), channel_id=1, replica_groups=mesh['section'=16,'y'=4,'x'=4,'core'=2] {'y','x'}, dimensions={0} | all-to-all | bytes 983040 | tf_op jit(solution)/shard_map/all_to_all | solution.py:290
  260.3 2.1 shard_map.113
  262.4 10.5 %all_to_all.196.heads_ref = bf16[16,40,256]{2,1,0:T(8,128)(2,1)S(1)} all-to-all(bf16[16,40,256]{2,1,0:T(8,128)(2,1)S(1)} %get-tuple-element.237), channel_id=1, replica_groups=mesh['section'=16,'y'=4,'x'=4,'core'=2] {'y','x'}, dimensions={0} | all-to-all | bytes 655360 | tf_op jit(solution)/shard_map/all_to_all | solution.py:324
  273.7 26.5 %collective-permute-start.19 = (bf16[192,128]{1,0:T(8,128)(2,1)S(1)}, bf16[192,128]{1,0:T(8,128)(2,1)S(1)}, u32[]{:S(2)}, u32[]{:S(2)}) collective-permute-start(bf16[192,128]{1,0:T(8,128)(2,1)S(1)} %bitcast.21), channel_id=1, source_target_pairs={{0,1},{1,0},{2,3},{3,2},{4,5},{5,4},{6,7},{7,6},{8,9},{9,8},{10,11... | collective-permute-start | bytes 147464 | tf_op jit(solution)/shard_map/ppermute | solution.py:256
  302.0 13.8 %all_to_all.197.rows_ref = bf16[16,40,384]{2,1,0:T(8,128)(2,1)S(1)} all-to-all(bf16[16,40,384]{2,1,0:T(8,128)(2,1)S(1)} %get-tuple-element.244), channel_id=1, replica_groups=mesh['section'=16,'y'=4,'x'=4,'core'=2] {'y','x'}, dimensions={0} | all-to-all | bytes 983040 | tf_op jit(solution)/shard_map/all_to_all | solution.py:290
  315.8 2.1 shard_map.117
  317.8 11.4 %all_to_all.198.heads_ref = bf16[16,40,256]{2,1,0:T(8,128)(2,1)S(1)} all-to-all(bf16[16,40,256]{2,1,0:T(8,128)(2,1)S(1)} %get-tuple-element.248), channel_id=1, replica_groups=mesh['section'=16,'y'=4,'x'=4,'core'=2] {'y','x'}, dimensions={0} | all-to-all | bytes 655360 | tf_op jit(solution)/shard_map/all_to_all | solution.py:324
  331.3 11.6 %all_to_all.199.rows_ref = bf16[16,40,384]{2,1,0:T(8,128)(2,1)S(1)} all-to-all(bf16[16,40,384]{2,1,0:T(8,128)(2,1)S(1)} %get-tuple-element.252), channel_id=1, replica_groups=mesh['section'=16,'y'=4,'x'=4,'core'=2] {'y','x'}, dimensions={0} | all-to-all | bytes 983040 | tf_op jit(solution)/shard_map/all_to_all | solution.py:290
  342.9 2.1 shard_map.120
  345.0 10.5 %all_to_all.200.heads_ref = bf16[16,40,256]{2,1,0:T(8,128)(2,1)S(1)} all-to-all(bf16[16,40,256]{2,1,0:T(8,128)(2,1)S(1)} %get-tuple-element.256), channel_id=1, replica_groups=mesh['section'=16,'y'=4,'x'=4,'core'=2] {'y','x'}, dimensions={0} | all-to-all | bytes 655360 | tf_op jit(solution)/shard_map/all_to_all | solution.py:324
  357.5 11.4 %all_to_all.201.rows_ref = bf16[16,40,384]{2,1,0:T(8,128)(2,1)S(1)} all-to-all(bf16[16,40,384]{2,1,0:T(8,128)(2,1)S(1)} %get-tuple-element.260), channel_id=1, replica_groups=mesh['section'=16,'y'=4,'x'=4,'core'=2] {'y','x'}, dimensions={0} | all-to-all | bytes 983040 | tf_op jit(solution)/shard_map/all_to_all | solution.py:290
  369.0 2.1 shard_map.123
  371.0 10.5 %all_to_all.202.heads_ref = bf16[16,40,256]{2,1,0:T(8,128)(2,1)S(1)} all-to-all(bf16[16,40,256]{2,1,0:T(8,128)(2,1)S(1)} %get-tuple-element.264), channel_id=1, replica_groups=mesh['section'=16,'y'=4,'x'=4,'core'=2] {'y','x'}, dimensions={0} | all-to-all | bytes 655360 | tf_op jit(solution)/shard_map/all_to_all | solution.py:324
  383.6 11.4 %all_to_all.203.rows_ref = bf16[16,40,384]{2,1,0:T(8,128)(2,1)S(1)} all-to-all(bf16[16,40,384]{2,1,0:T(8,128)(2,1)S(1)} %get-tuple-element.268), channel_id=1, replica_groups=mesh['section'=16,'y'=4,'x'=4,'core'=2] {'y','x'}, dimensions={0} | all-to-all | bytes 983040 | tf_op jit(solution)/shard_map/all_to_all | solution.py:290
  395.1 2.1 shard_map.126
  397.1 10.5 %all_to_all.204.heads_ref = bf16[16,40,256]{2,1,0:T(8,128)(2,1)S(1)} all-to-all(bf16[16,40,256]{2,1,0:T(8,128)(2,1)S(1)} %get-tuple-element.272), channel_id=1, replica_groups=mesh['section'=16,'y'=4,'x'=4,'core'=2] {'y','x'}, dimensions={0} | all-to-all | bytes 655360 | tf_op jit(solution)/shard_map/all_to_all | solution.py:324
  409.7 11.4 %all_to_all.205.rows_ref = bf16[16,40,384]{2,1,0:T(8,128)(2,1)S(1)} all-to-all(bf16[16,40,384]{2,1,0:T(8,128)(2,1)S(1)} %get-tuple-element.276), channel_id=1, replica_groups=mesh['section'=16,'y'=4,'x'=4,'core'=2] {'y','x'}, dimensions={0} | all-to-all | bytes 983040 | tf_op jit(solution)/shard_map/all_to_all | solution.py:290
  421.1 2.1 shard_map.129
  423.2 10.8 %all_to_all.206.heads_ref = bf16[16,40,256]{2,1,0:T(8,128)(2,1)S(1)} all-to-all(bf16[16,40,256]{2,1,0:T(8,128)(2,1)S(1)} %get-tuple-element.280), channel_id=1, replica_groups=mesh['section'=16,'y'=4,'x'=4,'core'=2] {'y','x'}, dimensions={0} | all-to-all | bytes 655360 | tf_op jit(solution)/shard_map/all_to_all | solution.py:324
  436.0 12.8 %all_to_all.207.rows_ref = bf16[16,40,384]{2,1,0:T(8,128)(2,1)S(1)} all-to-all(bf16[16,40,384]{2,1,0:T(8,128)(2,1)S(1)} %get-tuple-element.284), channel_id=1, replica_groups=mesh['section'=16,'y'=4,'x'=4,'core'=2] {'y','x'}, dimensions={0} | all-to-all | bytes 983040 | tf_op jit(solution)/shard_map/all_to_all | solution.py:290
  448.9 2.1 shard_map.132
  451.0 12.2 %all_to_all.208.heads_ref = bf16[16,40,256]{2,1,0:T(8,128)(2,1)S(1)} all-to-all(bf16[16,40,256]{2,1,0:T(8,128)(2,1)S(1)} %get-tuple-element.288), channel_id=1, replica_groups=mesh['section'=16,'y'=4,'x'=4,'core'=2] {'y','x'}, dimensions={0} | all-to-all | bytes 655360 | tf_op jit(solution)/shard_map/all_to_all | solution.py:324
  465.2 12.3 %all_to_all.209.rows_ref = bf16[16,40,384]{2,1,0:T(8,128)(2,1)S(1)} all-to-all(bf16[16,40,384]{2,1,0:T(8,128)(2,1)S(1)} %get-tuple-element.292), channel_id=1, replica_groups=mesh['section'=16,'y'=4,'x'=4,'core'=2] {'y','x'}, dimensions={0} | all-to-all | bytes 983040 | tf_op jit(solution)/shard_map/all_to_all | solution.py:290
  479.6 10.5 %all_to_all.210.heads_ref = bf16[16,40,256]{2,1,0:T(8,128)(2,1)S(1)} all-to-all(bf16[16,40,256]{2,1,0:T(8,128)(2,1)S(1)} %get-tuple-element.296), channel_id=1, replica_groups=mesh['section'=16,'y'=4,'x'=4,'core'=2] {'y','x'}, dimensions={0} | all-to-all | bytes 655360 | tf_op jit(solution)/shard_map/all_to_all | solution.py:324
  491.5 11.7 %all_to_all.211.rows_ref = bf16[16,40,384]{2,1,0:T(8,128)(2,1)S(1)} all-to-all(bf16[16,40,384]{2,1,0:T(8,128)(2,1)S(1)} %get-tuple-element.300), channel_id=1, replica_groups=mesh['section'=16,'y'=4,'x'=4,'core'=2] {'y','x'}, dimensions={0} | all-to-all | bytes 983040 | tf_op jit(solution)/shard_map/all_to_all | solution.py:290
  503.1 2.5 shard_map.138
  505.6 10.5 %all_to_all.212.heads_ref = bf16[16,40,256]{2,1,0:T(8,128)(2,1)S(1)} all-to-all(bf16[16,40,256]{2,1,0:T(8,128)(2,1)S(1)} %get-tuple-element.303), channel_id=1, replica_groups=mesh['section'=16,'y'=4,'x'=4,'core'=2] {'y','x'}, dimensions={0} | all-to-all | bytes 655360 | tf_op jit(solution)/shard_map/all_to_all | solution.py:324
  518.1 24.3 %all-to-all-start.34 = ((f32[32,1,128]{2,1,0:T(1,128)}), f32[32,1,128]{2,1,0:T(1,128)S(1)}, u32[]{:S(2)}, u32[]{:S(2)}) async-start(f32[32,1,128]{2,1,0:T(1,128)} %shard_map.140), calls=%async_computation.34 | async-start | bytes 32768 | tf_op jit(solution)/shard_map/all_to_all | solution.py:354
  542.4 7.0 %all-to-all-done.34.pieces_ref = f32[32,1,128]{2,1,0:T(1,128)S(1)} async-done(((f32[32,1,128]{2,1,0:T(1,128)}), f32[32,1,128]{2,1,0:T(1,128)S(1)}, u32[]{:S(2)}, u32[]{:S(2)}) %all-to-all-start.34) | async-done | bytes 16416 | tf_op jit(solution)/shard_map/all_to_all | solution.py:354
  549.5 2.6 collective-permute-start.35
  552.7 57.7 %all-to-all-start.35 = ((f32[16,1,128]{2,1,0:T(1,128)}), f32[16,1,128]{2,1,0:T(1,128)S(1)}, u32[]{:S(2)}, u32[]{:S(2)}) async-start(f32[16,1,128]{2,1,0:T(1,128)} %shard_map.142), calls=%async_computation.35 | async-start | bytes 16384 | tf_op jit(solution)/shard_map/all_to_all | solution.py:357
  611.4 10.2 %all-to-all-done.35.pieces_ref = f32[16,1,128]{2,1,0:T(1,128)S(1)} async-done(((f32[16,1,128]{2,1,0:T(1,128)}), f32[16,1,128]{2,1,0:T(1,128)S(1)}, u32[]{:S(2)}, u32[]{:S(2)}) %all-to-all-start.35) | async-done | bytes 8224 | tf_op jit(solution)/shard_map/all_to_all | solution.py:357
  (135 shorter events, 46.0 us)
Async XLA Ops:
  0.6 9.9 %collective-permute-start = (bf16[192,128]{1,0:T(8,128)(2,1)}, bf16[192,128]{1,0:T(8,128)(2,1)S(1)}, u32[]{:S(2)}, u32[]{:S(2)}) collective-permute-start(bf16[192,128]{1,0:T(8,128)(2,1)} %bitcast.23), channel_id=1, source_target_pairs={{0,1},{1,0},{2,3},{3,2},{4,5},{5,4},{6,7},{7,6},{8,9},{9,8},{10,11... | collective-permute-start | bytes 147464 | tf_op jit(solution)/shard_map/ppermute | solution.py:256
  10.5 0.8 copy-start.6
  11.3 0.7 copy-start.7
  13.3 10.2 %collective-permute-start.1 = (bf16[6144,128]{1,0:T(8,128)(2,1)}, bf16[6144,128]{1,0:T(8,128)(2,1)S(1)}, u32[]{:S(2)}, u32[]{:S(2)}) collective-permute-start(bf16[6144,128]{1,0:T(8,128)(2,1)} %bitcast.27), channel_id=1, source_target_pairs={{0,1},{1,0},{2,3},{3,2},{4,5},{5,4},{6,7},{7,6},{8,9},{9,8},{10,11... | collective-permute-start | bytes 4718600 | tf_op jit(solution)/shard_map/ppermute | solution.py:256
  15.5 8.0 %collective-permute-start.2 = (bf16[6144,128]{1,0:T(8,128)(2,1)}, bf16[6144,128]{1,0:T(8,128)(2,1)}, u32[]{:S(2)}, u32[]{:S(2)}) collective-permute-start(bf16[6144,128]{1,0:T(8,128)(2,1)} %bitcast.29), channel_id=1, source_target_pairs={{0,1},{1,0},{2,3},{3,2},{4,5},{5,4},{6,7},{7,6},{8,9},{9,8},{10,11... | collective-permute-start | bytes 4718600 | tf_op jit(solution)/shard_map/ppermute | solution.py:256
  17.6 5.9 collective-permute-start.3
  19.9 14.4 %all-to-all-start = ((bf16[16,40,384]{2,1,0:T(8,128)(2,1)}), bf16[16,40,384]{2,1,0:T(8,128)(2,1)S(1)}, u32[]{:S(2)}, u32[]{:S(2)}) async-start(bf16[16,40,384]{2,1,0:T(8,128)(2,1)} %get-tuple-element.161), calls=%async_computation | async-start | bytes 983040 | tf_op jit(solution)/shard_map/all_to_all | solution.py:290
  23.5 10.8 %copy-start.4 = (f32[1,6144]{1,0:T(1,128)S(1)}, f32[1,6144]{1,0:T(1,128)}, u32[]{:S(2)}) copy-start(f32[1,6144]{1,0:T(1,128)} %gain_ref.33) | copy-start | bytes 73732
  23.5 1.2 copy-start.9
  34.3 2.8 copy-start
  37.1 31.7 %copy-start.1 = (bf16[6144,512]{1,0:T(8,128)(2,1)S(1)}, bf16[6144,512]{1,0:T(8,128)(2,1)}, u32[]{:S(2)}) copy-start(bf16[6144,512]{1,0:T(8,128)(2,1)} %get-tuple-element.168.w_ref) | copy-start | bytes 18874372
  52.2 1.9 copy-start.2
  54.7 2.3 collective-permute-start.4
  68.8 12.6 %copy-start.3 = (bf16[4096,384]{1,0:T(8,128)(2,1)S(1)}, bf16[4096,384]{1,0:T(8,128)(2,1)}, u32[]{:S(2)}) copy-start(bf16[4096,384]{1,0:T(8,128)(2,1)} %get-tuple-element.173.w_ref) | copy-start | bytes 9437188
  81.9 4.6 collective-permute-start.5
  85.6 1.0 collective-permute-start.6
  111.3 1.3 collective-permute-start.7
  111.9 0.7 collective-permute-start.8
  137.3 1.3 collective-permute-start.9
  138.0 0.7 collective-permute-start.10
  166.1 1.3 collective-permute-start.11
  166.7 0.7 collective-permute-start.12
  194.7 1.3 collective-permute-start.13
  195.3 0.7 collective-permute-start.14
  221.4 1.3 collective-permute-start.15
  222.0 0.7 collective-permute-start.16
  247.4 1.3 collective-permute-start.17
  248.1 0.7 collective-permute-start.18
  272.9 0.8 copy-start.5
  273.7 27.9 %collective-permute-start.19 = (bf16[192,128]{1,0:T(8,128)(2,1)S(1)}, bf16[192,128]{1,0:T(8,128)(2,1)S(1)}, u32[]{:S(2)}, u32[]{:S(2)}) collective-permute-start(bf16[192,128]{1,0:T(8,128)(2,1)S(1)} %bitcast.21), channel_id=1, source_target_pairs={{0,1},{1,0},{2,3},{3,2},{4,5},{5,4},{6,7},{7,6},{8,9},{9,8},{10,11... | collective-permute-start | bytes 147464 | tf_op jit(solution)/shard_map/ppermute | solution.py:256
  300.3 1.6 collective-permute-start.20
  300.9 1.0 collective-permute-start.21
  329.8 1.3 collective-permute-start.22
  330.5 0.7 collective-permute-start.23
  356.1 1.3 collective-permute-start.24
  356.8 0.7 collective-permute-start.25
  382.2 1.3 collective-permute-start.26
  382.8 0.7 collective-permute-start.27
  408.3 1.3 collective-permute-start.28
  408.9 0.7 collective-permute-start.29
  434.6 1.3 collective-permute-start.30
  435.3 0.7 collective-permute-start.31
  463.8 1.3 collective-permute-start.32
  464.4 0.7 collective-permute-start.33
  490.7 0.7 collective-permute-start.34
  516.2 105.4 %copy-start.8 = (s32[128]{0:T(128)S(1)}, s32[128]{0:T(128)}, u32[]{:S(2)}) copy-start(s32[128]{0:T(128)} %param.9) | copy-start | bytes 1540
  518.1 31.3 %all-to-all-start.34 = ((f32[32,1,128]{2,1,0:T(1,128)}), f32[32,1,128]{2,1,0:T(1,128)S(1)}, u32[]{:S(2)}, u32[]{:S(2)}) async-start(f32[32,1,128]{2,1,0:T(1,128)} %shard_map.140), calls=%async_computation.34 | async-start | bytes 32768 | tf_op jit(solution)/shard_map/all_to_all | solution.py:354
  549.5 60.9 %collective-permute-start.35 = (bf16[80,192]{1,0:T(8,128)(2,1)S(1)}, bf16[80,192]{1,0:T(8,128)(2,1)S(1)}, u32[]{:S(2)}, u32[]{:S(2)}) collective-permute-start(bf16[80,192]{1,0:T(8,128)(2,1)S(1)} %broadcast_select_fusion), channel_id=1, source_target_pairs={{0,1},{1,0},{2,3},{3,2},{4,5},{5,4},{6,7},{7,6},{8,9},{9,8},{10,11... | collective-permute-start | bytes 92168 | tf_op jit(solution)/shard_map/ppermute | solution.py:256
  552.7 68.9 %all-to-all-start.35 = ((f32[16,1,128]{2,1,0:T(1,128)}), f32[16,1,128]{2,1,0:T(1,128)S(1)}, u32[]{:S(2)}, u32[]{:S(2)}) async-start(f32[16,1,128]{2,1,0:T(1,128)} %shard_map.142), calls=%async_computation.35 | async-start | bytes 16384 | tf_op jit(solution)/shard_map/all_to_all | solution.py:357

commit v6 on v5

--- a/solution.py
+++ b/solution.py
@@ -1,3 +1,5 @@
+import functools
+
 import jax
 import jax.numpy as jnp
 from jax import lax
@@ -93,11 +95,12 @@
         total += centered * centered
     scale = lax.rsqrt(jnp.sum(total, -1, keepdims=True) / (chips * cols) + 1e-05)
     acc = jnp.zeros((length, 2 * width), F32)
-    for chip in range(chips):
-        span = slice(chip * cols, (chip + 1) * cols)
-        centered = rows_ref[chip].astype(F32) - mean
-        normed = (centered * scale * gain_ref[:, span]).astype(BF)
-        acc += dot(normed, w_ref[span, :])
+    for pair in range(0, chips, 2):
+        normed = []
+        for chip in (pair, pair + 1):
+            centered = rows_ref[chip].astype(F32) - mean
+            normed.append((centered * scale * gain_ref[:, chip * cols : (chip + 1) * cols]).astype(BF))
+        acc += dot(jnp.concatenate(normed, 1), w_ref[pair * cols : (pair + 2) * cols, :])
     rounded = acc.astype(BF).astype(F32)
     qk, val = rounded[:, :width], rounded[:, width:]
     head_of = iota((length, width), 1) // HD
@@ -168,10 +171,11 @@
         done_ref[number] = jnp.where(mine, rows.astype(F32), kept_ref[number].astype(F32)).astype(BF)
 
 
-def spread(flag_ref, tokens_ref, *refs):
+def spread(backward, flag_ref, tokens_ref, *refs):
     *received_refs, rows_ref, send_ref = refs
+    received_refs = list(enumerate(reversed(received_refs) if backward else received_refs))
     rows = tokens_ref[...].astype(F32)
-    for number, received_ref in enumerate(reversed(received_refs)):
+    for number, received_ref in received_refs:
         here = (flag_ref[0:1, 0:1] == float(number)) & (flag_ref[1:2, 0:1] == 0.0)
         rows = jnp.where(here, received_ref[...].astype(F32), rows)
     rows = rows.astype(BF)
@@ -180,20 +184,17 @@
         send_ref[chip] = rows
 
 
-def aim(pick_ref, own_ref, other_ref, goal_ref):
-    pick = pick_ref[lax.axis_index("core")]
-    goal_ref[...] = in_core_order(*[dot(pick, ref[...], ((1,), (1,))) for ref in (own_ref, other_ref)])
-
-
-def token_errors(pick_ref, done_ref, goal_ref, send_ref):
-    slices, length, cols = done_ref.shape
-    pick = pick_ref[lax.axis_index("core")].astype(F32)
-    total = jnp.zeros((1, pick.shape[1]), F32)
-    for number in range(slices):
-        span = slice(number * length, (number + 1) * length)
-        diff = done_ref[number].astype(F32) - goal_ref[span, :]
-        sums = jnp.sum(diff * diff, -1, keepdims=True)
-        total += jnp.sum(jnp.where(pick[span] > 0.0, sums, 0.0), 0, keepdims=True)
+def row_parts(keep_ref, other_ref):
+    first = lax.axis_index("core") == 0
+    keep, other = keep_ref[...], other_ref[...]
+    return jnp.where(first, keep, other), jnp.where(first, other, keep)
+
+
+def token_errors(pick_ref, keep_ref, other_ref, targets_ref, send_ref):
+    parts = row_parts(keep_ref, other_ref)
+    rows = dot(parts[0], pick_ref[0], ((0,), (0,))) + dot(parts[1], pick_ref[1], ((0,), (0,)))
+    diff = rows - targets_ref[...].astype(F32)
+    total = jnp.sum(diff * diff, 0, keepdims=True)
     last = lax.axis_index("section") == lax.axis_size("section") - 1
     total = jnp.where(last, total, 0.0)
     for number in range(send_ref.shape[0]):
@@ -219,9 +220,10 @@
     loss_ref[...] = jnp.broadcast_to(sums / (tokens * D), (DOCS, count))
 
 
-def place_back(pick_ref, parts_ref, out_ref):
+def place_back(pick_ref, keep_ref, other_ref, out_ref):
+    parts = row_parts(keep_ref, other_ref)
     out_ref[...] = (
-        dot(pick_ref[0], parts_ref[0], ((0,), (0,))) + dot(pick_ref[1], parts_ref[1], ((0,), (0,)))
+        dot(pick_ref[0], parts[0], ((0,), (0,))) + dot(pick_ref[1], parts[1], ((0,), (0,)))
     ).astype(BF)
 
 
@@ -274,14 +276,15 @@
     vals = jnp.zeros((length, width), F32)
     done = jnp.zeros((slices, length, cols), BF)
     received = []
-    goal = w_last = w_in = None
+    w_last = w_in = None
     for step in range(sections + slices - 1):
+        backward = step % 2 == 1
         rows, send = run(
-            spread,
+            functools.partial(spread, backward),
             [((length, cols), BF), ((chips, length, cols), BF)],
             flags,
             first_parts[min(step, slices - 1)],
-            *reversed(received),
+            *(reversed(received) if backward else received),
         )
         if step == 0:
             w_qk, w_val, w_out, send = lax.optimization_barrier((w_qk, w_val, w_out, send))
@@ -323,7 +326,7 @@
         )
         attended = lax.all_to_all(send, PLANE, 0, 0, tiled=True)
         if step == sections + slices - 2:
-            attended, picks, goal = lax.optimization_barrier((attended, picks, goal))
+            attended, picks, targets = lax.optimization_barrier((attended, picks, targets))
         rows, done = run(
             project_out,
             [((length, cols), BF), ((slices, length, cols), BF)],
@@ -344,25 +347,19 @@
             else:
                 received[number] = jnp.zeros_like(rows)
         received = [received[number] for number in range(slices)]
-        if step == sections // 2:
-            targets, rows = lax.optimization_barrier((targets, rows))
-            targets_t = jnp.swapaxes(targets, 0, 1)
-            goal = run(aim, ((part, cols), F32), picks, targets_t, swap(targets_t))
-            goal, picks, received = lax.optimization_barrier((goal, picks, received))
-
-    send = run(token_errors, ((2 * chips, 1, row_count), F32), picks, done, goal)
-    send = lax.all_to_all(send, PLANE + ("core",), 0, 0, tiled=True)
-    send, done = lax.optimization_barrier((send, done))
-    send = run(add_up, ((sections, 1, row_count), F32), send)
-    send = lax.all_to_all(send, "section", 0, 0, tiled=True)
-    losses = run(finish_losses, ((DOCS, row_count), F32), send, docs)[:, 0]
 
     part_rows = done.reshape(part, cols)
     halves = [part_rows[:, :cols_own], part_rows[:, cols_own:]]
     keep = jnp.where(core == 0, halves[0], halves[1])
     other = swap(jnp.where(core == 0, halves[1], halves[0]))
-    parts = jnp.stack([jnp.where(core == 0, keep, other), jnp.where(core == 0, other, keep)])
-    section_rows = run(place_back, ((row_count, cols_own), BF), picks, parts)
+    targets_t = jnp.swapaxes(targets, 0, 1)
+    send = run(token_errors, ((2 * chips, 1, row_count), F32), picks, keep, other, targets_t)
+    send = lax.all_to_all(send, PLANE + ("core",), 0, 0, tiled=True)
+    send = run(add_up, ((sections, 1, row_count), F32), send)
+    send = lax.all_to_all(send, "section", 0, 0, tiled=True)
+    losses = run(finish_losses, ((DOCS, row_count), F32), send, docs)[:, 0]
+
+    section_rows = run(place_back, ((row_count, cols_own), BF), picks, keep, other)
     return (section_rows[None], losses)
 
 

time: 633 us -> 626 us (0.989)
  starting transfers between devices: 154 us -> 143 us
    all_to_all x1, starting transfers between devices: 24.3 us -> 3.54 us  [local(): attended = lax.all_to_all(send, PLANE, 0, 0, tiled=True)]
    ppermute x6 -> x5, starting transfers between devices: 44.4 us -> 62.9 us  [swap(): return lax.ppermute(value, 'core', [(0, 1), (1, 0)])]
    all_to_all x17 -> x16, blocking collectives: 187 us -> 177 us  [local(): attended = lax.all_to_all(send, PLANE, 0, 0, tiled=True)]
    all_to_all x0 -> x1, blocking collectives: none -> 10.2 us  [local(): send = lax.all_to_all(send, PLANE + ('core',), 0, 0, tiled=True)]
    all_to_all x1, starting transfers between devices: 57.7 us -> 48.8 us  [local(): send = lax.all_to_all(send, 'section', 0, 0, tiled=True)]
    pallas_call x57 -> x56, Pallas kernels: 50.7 us -> 48.9 us  [run(): pl.pallas_call(kernel, out_shape=shapes if several else shapes[0], in_spe...]
  transfers between devices with their start and end apart: 39 -> 38, of which waited for: 6 -> 7; matrix products, arithmetic and copies ran while one was open for 0% -> 0% of each run, Pallas kernels for 1% -> 1%
where the time goes in v6:
time: 626 us; the launch traced here: 615 us
  blocking collectives  378 us (60%)
  starting transfers between devices  143 us (23%)
  Pallas kernels  56.5 us (9%)
  waiting for transfers between devices  26 us (4%)
  local copies, waits for them, and re-layouts  10.2 us (2%)
    all_to_all x16, blocking collectives, local(): gathered = lax.all_to_all(send, PLANE, 0, 0, tiled=True)  191 us
    all_to_all x16, blocking collectives, local(): attended = lax.all_to_all(send, PLANE, 0, 0, tiled=True)  177 us
    ppermute x5, starting transfers between devices, swap(): return lax.ppermute(value, 'core', [(0, 1), (1, 0)])  62.9 us
    pallas_call x56, Pallas kernels, run(): pl.pallas_call(kernel, out_shape=shapes if several else shapes[0], in_spe...  48.9 us
    all_to_all x1, starting transfers between devices, local(): send = lax.all_to_all(send, 'section', 0, 0, tiled=True)  48.8 us
    ppermute x30, starting transfers between devices, local(): received[number] = lax.ppermute(rows, 'section', [(z, z + 1)])  24.1 us
  transfers between devices with their start and end apart: 38, of which 7 were waited for; matrix products, arithmetic and copies ran while one was open for 0% of the time, Pallas kernels for 1%

profile of v6, /device:TPU:1, one launch (start us, length us, event | category | flops | bytes accessed | tf_op | source)
XLA Modules:
  0.0 615.4 jit_solution(475709767409893870)
XLA Ops:
  0.6 8.8 %collective-permute-start = (bf16[192,128]{1,0:T(8,128)(2,1)}, bf16[192,128]{1,0:T(8,128)(2,1)S(1)}, u32[]{:S(2)}, u32[]{:S(2)}) collective-permute-start(bf16[192,128]{1,0:T(8,128)(2,1)} %bitcast.16), channel_id=1, source_target_pairs={{0,1},{1,0},{2,3},{3,2},{4,5},{5,4},{6,7},{7,6},{8,9},{9,8},{10,11... | collective-permute-start | bytes 147464 | tf_op jit(solution)/shard_map/ppermute | solution.py:258
  13.3 2.2 collective-permute-start.1
  15.5 2.1 collective-permute-start.2
  17.6 2.3 collective-permute-start.3
  19.9 3.6 all-to-all-start
  24.7 7.5 %shard_map.88 = (bf16[6144,512]{1,0:T(8,128)(2,1)}, bf16[4096,384]{1,0:T(8,128)(2,1)}) custom-call(bf16[6144,128]{1,0:T(8,128)(2,1)} %bitcast.22, bf16[6144,128]{1,0:T(8,128)(2,1)} %copy-done.12, bf16[6144,128]{1,0:T(8,128)(2,1)} %bitcast.24, bf16[6144,128]{1,0:T(8,128)(2,1)} %collective-permute-done.2.val_other_ref, bf16[192,4096]{1,0:T(8,128)(2,1)} %bitcast.26, ...), custom_call_target="tpu_custom_call" | custom-call | bytes 18874368 | tf_op jit(solution)/shard_map/pallas_call | solution.py:295
  32.2 2.1 all-to-all-done.rows_ref
  34.3 2.8 copy-done
  37.1 2.0 shard_map.89
  39.2 13.1 %all_to_all.180.heads_ref = bf16[16,40,256]{2,1,0:T(8,128)(2,1)S(1)} all-to-all(bf16[16,40,256]{2,1,0:T(8,128)(2,1)S(1)} %get-tuple-element.165), channel_id=1, replica_groups=mesh['section'=16,'y'=4,'x'=4,'core'=2] {'y','x'}, dimensions={0} | all-to-all | bytes 655360 | tf_op jit(solution)/shard_map/all_to_all | solution.py:327
  57.1 11.7 %all_to_all.181.rows_ref = bf16[16,40,384]{2,1,0:T(8,128)(2,1)S(1)} all-to-all(bf16[16,40,384]{2,1,0:T(8,128)(2,1)S(1)} %get-tuple-element.169), channel_id=1, replica_groups=mesh['section'=16,'y'=4,'x'=4,'core'=2] {'y','x'}, dimensions={0} | all-to-all | bytes 983040 | tf_op jit(solution)/shard_map/all_to_all | solution.py:293
  68.8 2.0 shard_map.92
  70.8 10.5 %all_to_all.182.heads_ref = bf16[16,40,256]{2,1,0:T(8,128)(2,1)S(1)} all-to-all(bf16[16,40,256]{2,1,0:T(8,128)(2,1)S(1)} %get-tuple-element.173), channel_id=1, replica_groups=mesh['section'=16,'y'=4,'x'=4,'core'=2] {'y','x'}, dimensions={0} | all-to-all | bytes 655360 | tf_op jit(solution)/shard_map/all_to_all | solution.py:327
  82.6 4.2 collective-permute-start.6
  87.9 11.4 %all_to_all.183.rows_ref = bf16[16,40,384]{2,1,0:T(8,128)(2,1)S(1)} all-to-all(bf16[16,40,384]{2,1,0:T(8,128)(2,1)S(1)} %get-tuple-element.177), channel_id=1, replica_groups=mesh['section'=16,'y'=4,'x'=4,'core'=2] {'y','x'}, dimensions={0} | all-to-all | bytes 983040 | tf_op jit(solution)/shard_map/all_to_all | solution.py:293
  99.3 2.0 shard_map.95
  101.4 10.5 %all_to_all.184.heads_ref = bf16[16,40,256]{2,1,0:T(8,128)(2,1)S(1)} all-to-all(bf16[16,40,256]{2,1,0:T(8,128)(2,1)S(1)} %get-tuple-element.181), channel_id=1, replica_groups=mesh['section'=16,'y'=4,'x'=4,'core'=2] {'y','x'}, dimensions={0} | all-to-all | bytes 655360 | tf_op jit(solution)/shard_map/all_to_all | solution.py:327
  113.9 11.4 %all_to_all.185.rows_ref = bf16[16,40,384]{2,1,0:T(8,128)(2,1)S(1)} all-to-all(bf16[16,40,384]{2,1,0:T(8,128)(2,1)S(1)} %get-tuple-element.185), channel_id=1, replica_groups=mesh['section'=16,'y'=4,'x'=4,'core'=2] {'y','x'}, dimensions={0} | all-to-all | bytes 983040 | tf_op jit(solution)/shard_map/all_to_all | solution.py:293
  125.3 2.0 shard_map.98
  127.4 10.5 %all_to_all.186.heads_ref = bf16[16,40,256]{2,1,0:T(8,128)(2,1)S(1)} all-to-all(bf16[16,40,256]{2,1,0:T(8,128)(2,1)S(1)} %get-tuple-element.189), channel_id=1, replica_groups=mesh['section'=16,'y'=4,'x'=4,'core'=2] {'y','x'}, dimensions={0} | all-to-all | bytes 655360 | tf_op jit(solution)/shard_map/all_to_all | solution.py:327
  139.9 12.0 %all_to_all.187.rows_ref = bf16[16,40,384]{2,1,0:T(8,128)(2,1)S(1)} all-to-all(bf16[16,40,384]{2,1,0:T(8,128)(2,1)S(1)} %get-tuple-element.193), channel_id=1, replica_groups=mesh['section'=16,'y'=4,'x'=4,'core'=2] {'y','x'}, dimensions={0} | all-to-all | bytes 983040 | tf_op jit(solution)/shard_map/all_to_all | solution.py:293
  151.9 2.0 shard_map.101
  153.9 12.7 %all_to_all.188.heads_ref = bf16[16,40,256]{2,1,0:T(8,128)(2,1)S(1)} all-to-all(bf16[16,40,256]{2,1,0:T(8,128)(2,1)S(1)} %get-tuple-element.197), channel_id=1, replica_groups=mesh['section'=16,'y'=4,'x'=4,'core'=2] {'y','x'}, dimensions={0} | all-to-all | bytes 655360 | tf_op jit(solution)/shard_map/all_to_all | solution.py:327
  168.6 13.3 %all_to_all.189.rows_ref = bf16[16,40,384]{2,1,0:T(8,128)(2,1)S(1)} all-to-all(bf16[16,40,384]{2,1,0:T(8,128)(2,1)S(1)} %get-tuple-element.201), channel_id=1, replica_groups=mesh['section'=16,'y'=4,'x'=4,'core'=2] {'y','x'}, dimensions={0} | all-to-all | bytes 983040 | tf_op jit(solution)/shard_map/all_to_all | solution.py:293
  181.9 2.0 shard_map.104
  183.9 11.2 %all_to_all.190.heads_ref = bf16[16,40,256]{2,1,0:T(8,128)(2,1)S(1)} all-to-all(bf16[16,40,256]{2,1,0:T(8,128)(2,1)S(1)} %get-tuple-element.205), channel_id=1, replica_groups=mesh['section'=16,'y'=4,'x'=4,'core'=2] {'y','x'}, dimensions={0} | all-to-all | bytes 655360 | tf_op jit(solution)/shard_map/all_to_all | solution.py:327
  197.2 12.0 %all_to_all.191.rows_ref = bf16[16,40,384]{2,1,0:T(8,128)(2,1)S(1)} all-to-all(bf16[16,40,384]{2,1,0:T(8,128)(2,1)S(1)} %get-tuple-element.209), channel_id=1, replica_groups=mesh['section'=16,'y'=4,'x'=4,'core'=2] {'y','x'}, dimensions={0} | all-to-all | bytes 983040 | tf_op jit(solution)/shard_map/all_to_all | solution.py:293
  209.2 2.0 shard_map.107
  211.2 10.7 %all_to_all.192.heads_ref = bf16[16,40,256]{2,1,0:T(8,128)(2,1)S(1)} all-to-all(bf16[16,40,256]{2,1,0:T(8,128)(2,1)S(1)} %get-tuple-element.213), channel_id=1, replica_groups=mesh['section'=16,'y'=4,'x'=4,'core'=2] {'y','x'}, dimensions={0} | all-to-all | bytes 655360 | tf_op jit(solution)/shard_map/all_to_all | solution.py:327
  223.9 11.4 %all_to_all.193.rows_ref = bf16[16,40,384]{2,1,0:T(8,128)(2,1)S(1)} all-to-all(bf16[16,40,384]{2,1,0:T(8,128)(2,1)S(1)} %get-tuple-element.217), channel_id=1, replica_groups=mesh['section'=16,'y'=4,'x'=4,'core'=2] {'y','x'}, dimensions={0} | all-to-all | bytes 983040 | tf_op jit(solution)/shard_map/all_to_all | solution.py:293
  235.4 2.0 shard_map.110
  237.4 10.5 %all_to_all.194.heads_ref = bf16[16,40,256]{2,1,0:T(8,128)(2,1)S(1)} all-to-all(bf16[16,40,256]{2,1,0:T(8,128)(2,1)S(1)} %get-tuple-element.221), channel_id=1, replica_groups=mesh['section'=16,'y'=4,'x'=4,'core'=2] {'y','x'}, dimensions={0} | all-to-all | bytes 655360 | tf_op jit(solution)/shard_map/all_to_all | solution.py:327
  249.9 11.4 %all_to_all.195.rows_ref = bf16[16,40,384]{2,1,0:T(8,128)(2,1)S(1)} all-to-all(bf16[16,40,384]{2,1,0:T(8,128)(2,1)S(1)} %get-tuple-element.225), channel_id=1, replica_groups=mesh['section'=16,'y'=4,'x'=4,'core'=2] {'y','x'}, dimensions={0} | all-to-all | bytes 983040 | tf_op jit(solution)/shard_map/all_to_all | solution.py:293
  261.4 2.0 shard_map.113
  263.4 10.5 %all_to_all.196.heads_ref = bf16[16,40,256]{2,1,0:T(8,128)(2,1)S(1)} all-to-all(bf16[16,40,256]{2,1,0:T(8,128)(2,1)S(1)} %get-tuple-element.229), channel_id=1, replica_groups=mesh['section'=16,'y'=4,'x'=4,'core'=2] {'y','x'}, dimensions={0} | all-to-all | bytes 655360 | tf_op jit(solution)/shard_map/all_to_all | solution.py:327
  276.0 11.6 %all_to_all.197.rows_ref = bf16[16,40,384]{2,1,0:T(8,128)(2,1)S(1)} all-to-all(bf16[16,40,384]{2,1,0:T(8,128)(2,1)S(1)} %get-tuple-element.233), channel_id=1, replica_groups=mesh['section'=16,'y'=4,'x'=4,'core'=2] {'y','x'}, dimensions={0} | all-to-all | bytes 983040 | tf_op jit(solution)/shard_map/all_to_all | solution.py:293
  287.6 2.0 shard_map.116
  289.6 10.5 %all_to_all.198.heads_ref = bf16[16,40,256]{2,1,0:T(8,128)(2,1)S(1)} all-to-all(bf16[16,40,256]{2,1,0:T(8,128)(2,1)S(1)} %get-tuple-element.237), channel_id=1, replica_groups=mesh['section'=16,'y'=4,'x'=4,'core'=2] {'y','x'}, dimensions={0} | all-to-all | bytes 655360 | tf_op jit(solution)/shard_map/all_to_all | solution.py:327
  302.2 13.2 %all_to_all.199.rows_ref = bf16[16,40,384]{2,1,0:T(8,128)(2,1)S(1)} all-to-all(bf16[16,40,384]{2,1,0:T(8,128)(2,1)S(1)} %get-tuple-element.241), channel_id=1, replica_groups=mesh['section'=16,'y'=4,'x'=4,'core'=2] {'y','x'}, dimensions={0} | all-to-all | bytes 983040 | tf_op jit(solution)/shard_map/all_to_all | solution.py:293
  315.4 2.0 shard_map.119
  317.4 11.6 %all_to_all.200.heads_ref = bf16[16,40,256]{2,1,0:T(8,128)(2,1)S(1)} all-to-all(bf16[16,40,256]{2,1,0:T(8,128)(2,1)S(1)} %get-tuple-element.245), channel_id=1, replica_groups=mesh['section'=16,'y'=4,'x'=4,'core'=2] {'y','x'}, dimensions={0} | all-to-all | bytes 655360 | tf_op jit(solution)/shard_map/all_to_all | solution.py:327
  331.0 12.5 %all_to_all.201.rows_ref = bf16[16,40,384]{2,1,0:T(8,128)(2,1)S(1)} all-to-all(bf16[16,40,384]{2,1,0:T(8,128)(2,1)S(1)} %get-tuple-element.249), channel_id=1, replica_groups=mesh['section'=16,'y'=4,'x'=4,'core'=2] {'y','x'}, dimensions={0} | all-to-all | bytes 983040 | tf_op jit(solution)/shard_map/all_to_all | solution.py:293
  343.5 2.0 shard_map.122
  345.6 10.7 %all_to_all.202.heads_ref = bf16[16,40,256]{2,1,0:T(8,128)(2,1)S(1)} all-to-all(bf16[16,40,256]{2,1,0:T(8,128)(2,1)S(1)} %get-tuple-element.253), channel_id=1, replica_groups=mesh['section'=16,'y'=4,'x'=4,'core'=2] {'y','x'}, dimensions={0} | all-to-all | bytes 655360 | tf_op jit(solution)/shard_map/all_to_all | solution.py:327
  358.3 11.9 %all_to_all.203.rows_ref = bf16[16,40,384]{2,1,0:T(8,128)(2,1)S(1)} all-to-all(bf16[16,40,384]{2,1,0:T(8,128)(2,1)S(1)} %get-tuple-element.257), channel_id=1, replica_groups=mesh['section'=16,'y'=4,'x'=4,'core'=2] {'y','x'}, dimensions={0} | all-to-all | bytes 983040 | tf_op jit(solution)/shard_map/all_to_all | solution.py:293
  370.2 2.0 shard_map.125
  372.2 10.5 %all_to_all.204.heads_ref = bf16[16,40,256]{2,1,0:T(8,128)(2,1)S(1)} all-to-all(bf16[16,40,256]{2,1,0:T(8,128)(2,1)S(1)} %get-tuple-element.261), channel_id=1, replica_groups=mesh['section'=16,'y'=4,'x'=4,'core'=2] {'y','x'}, dimensions={0} | all-to-all | bytes 655360 | tf_op jit(solution)/shard_map/all_to_all | solution.py:327
  384.7 11.4 %all_to_all.205.rows_ref = bf16[16,40,384]{2,1,0:T(8,128)(2,1)S(1)} all-to-all(bf16[16,40,384]{2,1,0:T(8,128)(2,1)S(1)} %get-tuple-element.265), channel_id=1, replica_groups=mesh['section'=16,'y'=4,'x'=4,'core'=2] {'y','x'}, dimensions={0} | all-to-all | bytes 983040 | tf_op jit(solution)/shard_map/all_to_all | solution.py:293
  396.2 2.0 shard_map.128
  398.2 10.5 %all_to_all.206.heads_ref = bf16[16,40,256]{2,1,0:T(8,128)(2,1)S(1)} all-to-all(bf16[16,40,256]{2,1,0:T(8,128)(2,1)S(1)} %get-tuple-element.269), channel_id=1, replica_groups=mesh['section'=16,'y'=4,'x'=4,'core'=2] {'y','x'}, dimensions={0} | all-to-all | bytes 655360 | tf_op jit(solution)/shard_map/all_to_all | solution.py:327
  410.8 11.6 %all_to_all.207.rows_ref = bf16[16,40,384]{2,1,0:T(8,128)(2,1)S(1)} all-to-all(bf16[16,40,384]{2,1,0:T(8,128)(2,1)S(1)} %get-tuple-element.273), channel_id=1, replica_groups=mesh['section'=16,'y'=4,'x'=4,'core'=2] {'y','x'}, dimensions={0} | all-to-all | bytes 983040 | tf_op jit(solution)/shard_map/all_to_all | solution.py:293
  422.4 2.0 shard_map.131
  424.4 10.5 %all_to_all.208.heads_ref = bf16[16,40,256]{2,1,0:T(8,128)(2,1)S(1)} all-to-all(bf16[16,40,256]{2,1,0:T(8,128)(2,1)S(1)} %get-tuple-element.277), channel_id=1, replica_groups=mesh['section'=16,'y'=4,'x'=4,'core'=2] {'y','x'}, dimensions={0} | all-to-all | bytes 655360 | tf_op jit(solution)/shard_map/all_to_all | solution.py:327
  437.0 11.4 %all_to_all.209.rows_ref = bf16[16,40,384]{2,1,0:T(8,128)(2,1)S(1)} all-to-all(bf16[16,40,384]{2,1,0:T(8,128)(2,1)S(1)} %get-tuple-element.281), channel_id=1, replica_groups=mesh['section'=16,'y'=4,'x'=4,'core'=2] {'y','x'}, dimensions={0} | all-to-all | bytes 983040 | tf_op jit(solution)/shard_map/all_to_all | solution.py:293
  448.4 2.0 shard_map.134
  450.4 12.2 %all_to_all.210.heads_ref = bf16[16,40,256]{2,1,0:T(8,128)(2,1)S(1)} all-to-all(bf16[16,40,256]{2,1,0:T(8,128)(2,1)S(1)} %get-tuple-element.285), channel_id=1, replica_groups=mesh['section'=16,'y'=4,'x'=4,'core'=2] {'y','x'}, dimensions={0} | all-to-all | bytes 655360 | tf_op jit(solution)/shard_map/all_to_all | solution.py:327
  464.0 12.5 %all_to_all.211.rows_ref = bf16[16,40,384]{2,1,0:T(8,128)(2,1)S(1)} all-to-all(bf16[16,40,384]{2,1,0:T(8,128)(2,1)S(1)} %get-tuple-element.289), channel_id=1, replica_groups=mesh['section'=16,'y'=4,'x'=4,'core'=2] {'y','x'}, dimensions={0} | all-to-all | bytes 983040 | tf_op jit(solution)/shard_map/all_to_all | solution.py:293
  476.4 2.5 shard_map.137
  479.6 3.5 all-to-all-start.33
  483.2 9.6 %all-to-all-done.33.heads_ref = bf16[16,40,256]{2,1,0:T(8,128)(2,1)S(1)} async-done(((bf16[16,40,256]{2,1,0:T(8,128)(2,1)}), bf16[16,40,256]{2,1,0:T(8,128)(2,1)S(1)}, u32[]{:S(2)}, u32[]{:S(2)}) %all-to-all-start.33) | async-done | bytes 327712 | tf_op jit(solution)/shard_map/all_to_all | solution.py:327
  494.8 47.5 %collective-permute-start.34 = (bf16[80,192]{1,0:T(8,128)(2,1)S(1)}, bf16[80,192]{1,0:T(8,128)(2,1)S(1)}, u32[]{:S(2)}, u32[]{:S(2)}) collective-permute-start(bf16[80,192]{1,0:T(8,128)(2,1)S(1)} %get-tuple-element.304), channel_id=1, source_target_pairs={{0,1},{1,0},{2,3},{3,2},{4,5},{5,4},{6,7},{7,6},{8,9},{9,8},{10,11... | collective-permute-start | bytes 92168 | tf_op jit(solution)/shard_map/ppermute | solution.py:258
  543.4 10.2 %all_to_all.212.pieces_ref = f32[32,1,128]{2,1,0:T(1,128)S(1)} all-to-all(f32[32,1,128]{2,1,0:T(1,128)S(1)} %shard_map.140), channel_id=1, replica_groups=mesh['section'=16,'y'=4,'x'=4,'core'=2] {'y','x','core'}, dimensions={0} | all-to-all | bytes 32768 | tf_op jit(solution)/shard_map/all_to_all | solution.py:357
  554.3 48.8 %all-to-all-start.35 = ((f32[16,1,128]{2,1,0:T(1,128)}), f32[16,1,128]{2,1,0:T(1,128)S(1)}, u32[]{:S(2)}, u32[]{:S(2)}) async-start(f32[16,1,128]{2,1,0:T(1,128)} %shard_map.141), calls=%async_computation.35 | async-start | bytes 16384 | tf_op jit(solution)/shard_map/all_to_all | solution.py:359
  604.0 10.4 %all-to-all-done.35.pieces_ref = f32[16,1,128]{2,1,0:T(1,128)S(1)} async-done(((f32[16,1,128]{2,1,0:T(1,128)}), f32[16,1,128]{2,1,0:T(1,128)S(1)}, u32[]{:S(2)}, u32[]{:S(2)}) %all-to-all-start.35) | async-done | bytes 8224 | tf_op jit(solution)/shard_map/all_to_all | solution.py:359
  (136 shorter events, 45.4 us)
Async XLA Ops:
  0.6 9.9 %collective-permute-start = (bf16[192,128]{1,0:T(8,128)(2,1)}, bf16[192,128]{1,0:T(8,128)(2,1)S(1)}, u32[]{:S(2)}, u32[]{:S(2)}) collective-permute-start(bf16[192,128]{1,0:T(8,128)(2,1)} %bitcast.16), channel_id=1, source_target_pairs={{0,1},{1,0},{2,3},{3,2},{4,5},{5,4},{6,7},{7,6},{8,9},{9,8},{10,11... | collective-permute-start | bytes 147464 | tf_op jit(solution)/shard_map/ppermute | solution.py:258
  10.5 0.8 copy-start.8
  11.3 0.7 copy-start.10
  13.3 10.2 %collective-permute-start.1 = (bf16[6144,128]{1,0:T(8,128)(2,1)}, bf16[6144,128]{1,0:T(8,128)(2,1)S(1)}, u32[]{:S(2)}, u32[]{:S(2)}) collective-permute-start(bf16[6144,128]{1,0:T(8,128)(2,1)} %bitcast.21), channel_id=1, source_target_pairs={{0,1},{1,0},{2,3},{3,2},{4,5},{5,4},{6,7},{7,6},{8,9},{9,8},{10,11... | collective-permute-start | bytes 4718600 | tf_op jit(solution)/shard_map/ppermute | solution.py:258
  15.5 8.0 %collective-permute-start.2 = (bf16[6144,128]{1,0:T(8,128)(2,1)}, bf16[6144,128]{1,0:T(8,128)(2,1)}, u32[]{:S(2)}, u32[]{:S(2)}) collective-permute-start(bf16[6144,128]{1,0:T(8,128)(2,1)} %bitcast.23), channel_id=1, source_target_pairs={{0,1},{1,0},{2,3},{3,2},{4,5},{5,4},{6,7},{7,6},{8,9},{9,8},{10,11... | collective-permute-start | bytes 4718600 | tf_op jit(solution)/shard_map/ppermute | solution.py:258
  17.6 5.9 collective-permute-start.3
  19.9 14.4 %all-to-all-start = ((bf16[16,40,384]{2,1,0:T(8,128)(2,1)}), bf16[16,40,384]{2,1,0:T(8,128)(2,1)S(1)}, u32[]{:S(2)}, u32[]{:S(2)}) async-start(bf16[16,40,384]{2,1,0:T(8,128)(2,1)} %get-tuple-element.154), calls=%async_computation | async-start | bytes 983040 | tf_op jit(solution)/shard_map/all_to_all | solution.py:293
  23.5 10.8 %copy-start.4 = (f32[1,6144]{1,0:T(1,128)S(1)}, f32[1,6144]{1,0:T(1,128)}, u32[]{:S(2)}) copy-start(f32[1,6144]{1,0:T(1,128)} %gain_ref.33) | copy-start | bytes 73732
  23.5 1.2 copy-start.12
  34.3 2.8 copy-start
  37.1 31.7 %copy-start.1 = (bf16[6144,512]{1,0:T(8,128)(2,1)S(1)}, bf16[6144,512]{1,0:T(8,128)(2,1)}, u32[]{:S(2)}) copy-start(bf16[6144,512]{1,0:T(8,128)(2,1)} %get-tuple-element.161.w_ref) | copy-start | bytes 18874372
  52.3 1.9 copy-start.2
  54.7 2.3 collective-permute-start.4
  68.8 12.5 %copy-start.3 = (bf16[4096,384]{1,0:T(8,128)(2,1)S(1)}, bf16[4096,384]{1,0:T(8,128)(2,1)}, u32[]{:S(2)}) copy-start(bf16[4096,384]{1,0:T(8,128)(2,1)} %get-tuple-element.166.w_ref) | copy-start | bytes 9437188
  81.9 4.9 collective-permute-start.5
  82.6 5.2 collective-permute-start.6
  112.4 1.3 collective-permute-start.7
  113.1 0.7 collective-permute-start.8
  138.5 1.3 collective-permute-start.9
  139.1 0.7 collective-permute-start.10
  167.2 1.3 collective-permute-start.11
  167.8 0.7 collective-permute-start.12
  195.7 1.3 collective-permute-start.13
  196.4 0.7 collective-permute-start.14
  222.5 1.3 collective-permute-start.15
  223.1 0.7 collective-permute-start.16
  248.5 1.3 collective-permute-start.17
  249.2 0.7 collective-permute-start.18
  274.5 1.3 collective-permute-start.19
  275.2 0.7 collective-permute-start.20
  300.7 1.3 collective-permute-start.21
  301.4 0.7 collective-permute-start.22
  329.5 1.3 collective-permute-start.23
  330.2 0.7 collective-permute-start.24
  356.8 1.3 collective-permute-start.25
  357.5 0.7 collective-permute-start.26
  383.3 1.3 collective-permute-start.27
  384.0 0.7 collective-permute-start.28
  409.3 1.3 collective-permute-start.29
  410.0 0.7 collective-permute-start.30
  435.5 1.3 collective-permute-start.31
  436.2 0.7 collective-permute-start.32
  463.2 15.7 %copy-start.6 = (bf16[2,40,384]{2,1,0:T(8,128)(2,1)}, bf16[2,40,384]{2,1,0:T(8,128)(2,1)S(1)}, u32[]{:S(2)}) copy-start(bf16[2,40,384]{2,1,0:T(8,128)(2,1)S(1)} %get-tuple-element.297.kept_ref) | copy-start | bytes 184324
  463.2 0.7 collective-permute-start.33
  478.9 0.7 copy-start.5
  479.6 13.1 %all-to-all-start.33 = ((bf16[16,40,256]{2,1,0:T(8,128)(2,1)}), bf16[16,40,256]{2,1,0:T(8,128)(2,1)S(1)}, u32[]{:S(2)}, u32[]{:S(2)}) async-start(bf16[16,40,256]{2,1,0:T(8,128)(2,1)} %copy-done.5), calls=%async_computation.33 | async-start | bytes 655360 | tf_op jit(solution)/shard_map/all_to_all | solution.py:327
  492.8 0.8 copy-start.7
  493.6 49.6 %copy-start.9 = (bf16[128,192]{0,1:T(8,128)(2,1)S(1)}, bf16[128,192]{0,1:T(8,128)(2,1)}, u32[]{:S(2)}) copy-start(bf16[128,192]{0,1:T(8,128)(2,1)} %param.8) | copy-start | bytes 147460
  493.6 120.8 %copy-start.11 = (s32[128]{0:T(128)S(1)}, s32[128]{0:T(128)}, u32[]{:S(2)}) copy-start(s32[128]{0:T(128)} %param.9) | copy-start | bytes 1540
  494.8 48.3 %collective-permute-start.34 = (bf16[80,192]{1,0:T(8,128)(2,1)S(1)}, bf16[80,192]{1,0:T(8,128)(2,1)S(1)}, u32[]{:S(2)}, u32[]{:S(2)}) collective-permute-start(bf16[80,192]{1,0:T(8,128)(2,1)S(1)} %get-tuple-element.304), channel_id=1, source_target_pairs={{0,1},{1,0},{2,3},{3,2},{4,5},{5,4},{6,7},{7,6},{8,9},{9,8},{10,11... | collective-permute-start | bytes 92168 | tf_op jit(solution)/shard_map/ppermute | solution.py:258
  554.3 60.1 %all-to-all-start.35 = ((f32[16,1,128]{2,1,0:T(1,128)}), f32[16,1,128]{2,1,0:T(1,128)S(1)}, u32[]{:S(2)}, u32[]{:S(2)}) async-start(f32[16,1,128]{2,1,0:T(1,128)} %shard_map.141), calls=%async_computation.35 | async-start | bytes 16384 | tf_op jit(solution)/shard_map/all_to_all | solution.py:359

commit v7 on v6

--- a/solution.py
+++ b/solution.py
@@ -66,7 +66,8 @@
     section = lax.axis_index("section")
     row = iota(flag_ref.shape, 0)
     order = jnp.where(row == 0, -section, 0)
-    flag_ref[...] = jnp.where((row == 1) & (section == 0), 1, order).astype(F32)
+    order = jnp.where((row == 1) & (section == 0), 1, order)
+    flag_ref[...] = jnp.where(row == 2, lax.axis_index("core"), order).astype(F32)
 
 
 def qkv_attention(
@@ -78,9 +79,9 @@
     kin_ref,
     vin_ref,
     send_ref,
-    kout_ref,
-    vout_ref,
-    next_ref,
+    kout_ref=None,
+    vout_ref=None,
+    next_ref=None,
 ):
     chips, length, cols = rows_ref.shape
     width = kin_ref.shape[1]
@@ -129,6 +130,8 @@
     attended = in_core_order(attended[:, :half], attended[:, half:]).astype(BF)
     for chip in range(chips):
         send_ref[chip] = attended
+    if kout_ref is None:
+        return
     kout_ref[...] = key
     vout_ref[...] = val
     next_ref[...] = flag_ref[...] + jnp.where(iota(flag_ref.shape, 0) == 0, 1.0, 0.0)
@@ -159,13 +162,14 @@
     copies[7].wait()
 
 
-def project_out(flag_ref, heads_ref, w_ref, rows_ref, kept_ref, out_ref, done_ref):
+def project_out(flag_ref, heads_ref, w_ref, rows_ref, kept_ref, done_ref, out_ref=None):
     chips, _, width = heads_ref.shape
     mixed = jnp.zeros(rows_ref.shape, F32)
     for chip in range(chips):
         mixed += dot(heads_ref[chip], w_ref[chip * width : (chip + 1) * width, :])
     rows = (rows_ref[...].astype(F32) + mixed).astype(BF)
-    out_ref[...] = rows
+    if out_ref is not None:
+        out_ref[...] = rows
     for number in range(kept_ref.shape[0]):
         mine = flag_ref[0:1, 0:1] == float(number)
         done_ref[number] = jnp.where(mine, rows.astype(F32), kept_ref[number].astype(F32)).astype(BF)
@@ -244,7 +248,6 @@
 
 
 def local(tokens, targets, doc_ids, norm_gains, w_qk, w_val, w_out):
-    core = lax.axis_index("core")
     sections = lax.axis_size("section")
     chips = lax.axis_size("y") * lax.axis_size("x")
     row_count, cols_own = tokens.shape
@@ -272,6 +275,7 @@
         swap(tokens_t),
     )
 
+    first_flags = flags
     keys = jnp.zeros((length, width), F32)
     vals = jnp.zeros((length, width), F32)
     done = jnp.zeros((slices, length, cols), BF)
@@ -311,9 +315,11 @@
                 cost_estimate=pl.CostEstimate(flops=0, bytes_accessed=12 * D * width, transcendentals=0),
             )(*weights)
             gathered, first_parts, w_in, w_last = lax.optimization_barrier((gathered, first_parts, w_in, w_last))
-        send, keys, vals, next_flags = run(
+        last = step == sections + slices - 2
+        send, *carried = run(
             qkv_attention,
-            [((chips, length, width), BF), ((length, width), F32), ((length, width), F32), ((8, 128), F32)],
+            [((chips, length, width), BF)]
+            + ([] if last else [((length, width), F32), ((length, width), F32), ((8, 128), F32)]),
             flags,
             gathered,
             norm_gains,
@@ -325,11 +331,11 @@
             bytes_accessed=4 * D * width,
         )
         attended = lax.all_to_all(send, PLANE, 0, 0, tiled=True)
-        if step == sections + slices - 2:
+        if last:
             attended, picks, targets = lax.optimization_barrier((attended, picks, targets))
-        rows, done = run(
+        done, *rows = run(
             project_out,
-            [((length, cols), BF), ((slices, length, cols), BF)],
+            [((slices, length, cols), BF)] + ([] if last else [((length, cols), BF)]),
             flags,
             attended,
             w_last,
@@ -338,7 +344,10 @@
             flops=2 * length * chips * width * cols,
             bytes_accessed=2 * chips * width * cols,
         )
-        flags = next_flags
+        if last:
+            break
+        rows = rows[0]
+        keys, vals, flags = carried
         received = {}
         for number in reversed(range(slices)):
             z = step - number
@@ -350,8 +359,9 @@
 
     part_rows = done.reshape(part, cols)
     halves = [part_rows[:, :cols_own], part_rows[:, cols_own:]]
-    keep = jnp.where(core == 0, halves[0], halves[1])
-    other = swap(jnp.where(core == 0, halves[1], halves[0]))
+    own_first = first_flags[2:3, 0:1] == 0.0
+    keep = jnp.where(own_first, halves[0], halves[1])
+    other = swap(jnp.where(own_first, halves[1], halves[0]))
     targets_t = jnp.swapaxes(targets, 0, 1)
     send = run(token_errors, ((2 * chips, 1, row_count), F32), picks, keep, other, targets_t)
     send = lax.all_to_all(send, PLANE + ("core",), 0, 0, tiled=True)

time: 626 us -> 624 us (level)
  no operation moved by 1% of the time
where the time goes in v7:
time: 624 us; the launch traced here: 614 us
  blocking collectives  376 us (60%)
  starting transfers between devices  145 us (23%)
  Pallas kernels  56.1 us (9%)
  waiting for transfers between devices  23.2 us (4%)
  local copies, waits for them, and re-layouts  10 us (2%)
    all_to_all x16, blocking collectives, local(): gathered = lax.all_to_all(send, PLANE, 0, 0, tiled=True)  190 us
    all_to_all x16, blocking collectives, local(): attended = lax.all_to_all(send, PLANE, 0, 0, tiled=True)  177 us
    ppermute x5, starting transfers between devices, swap(): return lax.ppermute(value, 'core', [(0, 1), (1, 0)])  64.1 us
    all_to_all x1, starting transfers between devices, local(): send = lax.all_to_all(send, 'section', 0, 0, tiled=True)  50 us
    pallas_call x56, Pallas kernels, run(): pl.pallas_call(kernel, out_shape=shapes if several else shapes[0], in_spe...  48.6 us
    ppermute x30, starting transfers between devices, local(): received[number] = lax.ppermute(rows, 'section', [(z, z + 1)])  24.1 us
  transfers between devices with their start and end apart: 38, of which 7 were waited for; matrix products, arithmetic and copies ran while one was open for 0% of the time, Pallas kernels for 1%

profile of v7, /device:TPU:1, one launch (start us, length us, event | category | flops | bytes accessed | tf_op | source)
XLA Modules:
  0.0 613.8 jit_solution(13044322685952020361)
XLA Ops:
  0.6 8.8 %collective-permute-start = (bf16[192,128]{1,0:T(8,128)(2,1)}, bf16[192,128]{1,0:T(8,128)(2,1)S(1)}, u32[]{:S(2)}, u32[]{:S(2)}) collective-permute-start(bf16[192,128]{1,0:T(8,128)(2,1)} %bitcast.17), channel_id=1, source_target_pairs={{0,1},{1,0},{2,3},{3,2},{4,5},{5,4},{6,7},{7,6},{8,9},{9,8},{10,11... | collective-permute-start | bytes 147464 | tf_op jit(solution)/shard_map/ppermute | solution.py:261
  13.3 2.2 collective-permute-start.1
  15.5 2.1 collective-permute-start.2
  17.6 2.3 collective-permute-start.3
  19.9 3.6 all-to-all-start
  24.7 7.5 %shard_map.88 = (bf16[6144,512]{1,0:T(8,128)(2,1)}, bf16[4096,384]{1,0:T(8,128)(2,1)}) custom-call(bf16[6144,128]{1,0:T(8,128)(2,1)} %bitcast.23, bf16[6144,128]{1,0:T(8,128)(2,1)} %copy-done.11, bf16[6144,128]{1,0:T(8,128)(2,1)} %bitcast.25, bf16[6144,128]{1,0:T(8,128)(2,1)} %collective-permute-done.2.val_other_ref, bf16[192,4096]{1,0:T(8,128)(2,1)} %bitcast.27, ...), custom_call_target="tpu_custom_call" | custom-call | bytes 18874368 | tf_op jit(solution)/shard_map/pallas_call | solution.py:299
  32.2 2.1 all-to-all-done.rows_ref
  34.3 2.8 copy-done
  37.1 2.0 shard_map.89
  39.2 13.1 %all_to_all.180.heads_ref = bf16[16,40,256]{2,1,0:T(8,128)(2,1)S(1)} all-to-all(bf16[16,40,256]{2,1,0:T(8,128)(2,1)S(1)} %get-tuple-element.163), channel_id=1, replica_groups=mesh['section'=16,'y'=4,'x'=4,'core'=2] {'y','x'}, dimensions={0} | all-to-all | bytes 655360 | tf_op jit(solution)/shard_map/all_to_all | solution.py:333
  57.1 11.7 %all_to_all.181.rows_ref = bf16[16,40,384]{2,1,0:T(8,128)(2,1)S(1)} all-to-all(bf16[16,40,384]{2,1,0:T(8,128)(2,1)S(1)} %get-tuple-element.167), channel_id=1, replica_groups=mesh['section'=16,'y'=4,'x'=4,'core'=2] {'y','x'}, dimensions={0} | all-to-all | bytes 983040 | tf_op jit(solution)/shard_map/all_to_all | solution.py:297
  68.8 2.0 shard_map.92
  70.8 10.5 %all_to_all.182.heads_ref = bf16[16,40,256]{2,1,0:T(8,128)(2,1)S(1)} all-to-all(bf16[16,40,256]{2,1,0:T(8,128)(2,1)S(1)} %get-tuple-element.171), channel_id=1, replica_groups=mesh['section'=16,'y'=4,'x'=4,'core'=2] {'y','x'}, dimensions={0} | all-to-all | bytes 655360 | tf_op jit(solution)/shard_map/all_to_all | solution.py:333
  82.6 4.2 collective-permute-start.6
  87.9 11.4 %all_to_all.183.rows_ref = bf16[16,40,384]{2,1,0:T(8,128)(2,1)S(1)} all-to-all(bf16[16,40,384]{2,1,0:T(8,128)(2,1)S(1)} %get-tuple-element.175), channel_id=1, replica_groups=mesh['section'=16,'y'=4,'x'=4,'core'=2] {'y','x'}, dimensions={0} | all-to-all | bytes 983040 | tf_op jit(solution)/shard_map/all_to_all | solution.py:297
  99.3 2.0 shard_map.95
  101.3 10.5 %all_to_all.184.heads_ref = bf16[16,40,256]{2,1,0:T(8,128)(2,1)S(1)} all-to-all(bf16[16,40,256]{2,1,0:T(8,128)(2,1)S(1)} %get-tuple-element.179), channel_id=1, replica_groups=mesh['section'=16,'y'=4,'x'=4,'core'=2] {'y','x'}, dimensions={0} | all-to-all | bytes 655360 | tf_op jit(solution)/shard_map/all_to_all | solution.py:333
  113.9 11.4 %all_to_all.185.rows_ref = bf16[16,40,384]{2,1,0:T(8,128)(2,1)S(1)} all-to-all(bf16[16,40,384]{2,1,0:T(8,128)(2,1)S(1)} %get-tuple-element.183), channel_id=1, replica_groups=mesh['section'=16,'y'=4,'x'=4,'core'=2] {'y','x'}, dimensions={0} | all-to-all | bytes 983040 | tf_op jit(solution)/shard_map/all_to_all | solution.py:297
  125.3 2.0 shard_map.98
  127.4 10.5 %all_to_all.186.heads_ref = bf16[16,40,256]{2,1,0:T(8,128)(2,1)S(1)} all-to-all(bf16[16,40,256]{2,1,0:T(8,128)(2,1)S(1)} %get-tuple-element.187), channel_id=1, replica_groups=mesh['section'=16,'y'=4,'x'=4,'core'=2] {'y','x'}, dimensions={0} | all-to-all | bytes 655360 | tf_op jit(solution)/shard_map/all_to_all | solution.py:333
  139.9 12.0 %all_to_all.187.rows_ref = bf16[16,40,384]{2,1,0:T(8,128)(2,1)S(1)} all-to-all(bf16[16,40,384]{2,1,0:T(8,128)(2,1)S(1)} %get-tuple-element.191), channel_id=1, replica_groups=mesh['section'=16,'y'=4,'x'=4,'core'=2] {'y','x'}, dimensions={0} | all-to-all | bytes 983040 | tf_op jit(solution)/shard_map/all_to_all | solution.py:297
  151.9 2.0 shard_map.101
  153.9 12.6 %all_to_all.188.heads_ref = bf16[16,40,256]{2,1,0:T(8,128)(2,1)S(1)} all-to-all(bf16[16,40,256]{2,1,0:T(8,128)(2,1)S(1)} %get-tuple-element.195), channel_id=1, replica_groups=mesh['section'=16,'y'=4,'x'=4,'core'=2] {'y','x'}, dimensions={0} | all-to-all | bytes 655360 | tf_op jit(solution)/shard_map/all_to_all | solution.py:333
  168.6 12.7 %all_to_all.189.rows_ref = bf16[16,40,384]{2,1,0:T(8,128)(2,1)S(1)} all-to-all(bf16[16,40,384]{2,1,0:T(8,128)(2,1)S(1)} %get-tuple-element.199), channel_id=1, replica_groups=mesh['section'=16,'y'=4,'x'=4,'core'=2] {'y','x'}, dimensions={0} | all-to-all | bytes 983040 | tf_op jit(solution)/shard_map/all_to_all | solution.py:297
  181.2 2.0 shard_map.104
  183.3 11.1 %all_to_all.190.heads_ref = bf16[16,40,256]{2,1,0:T(8,128)(2,1)S(1)} all-to-all(bf16[16,40,256]{2,1,0:T(8,128)(2,1)S(1)} %get-tuple-element.203), channel_id=1, replica_groups=mesh['section'=16,'y'=4,'x'=4,'core'=2] {'y','x'}, dimensions={0} | all-to-all | bytes 655360 | tf_op jit(solution)/shard_map/all_to_all | solution.py:333
  196.4 11.4 %all_to_all.191.rows_ref = bf16[16,40,384]{2,1,0:T(8,128)(2,1)S(1)} all-to-all(bf16[16,40,384]{2,1,0:T(8,128)(2,1)S(1)} %get-tuple-element.207), channel_id=1, replica_groups=mesh['section'=16,'y'=4,'x'=4,'core'=2] {'y','x'}, dimensions={0} | all-to-all | bytes 983040 | tf_op jit(solution)/shard_map/all_to_all | solution.py:297
  207.8 2.0 shard_map.107
  209.8 10.5 %all_to_all.192.heads_ref = bf16[16,40,256]{2,1,0:T(8,128)(2,1)S(1)} all-to-all(bf16[16,40,256]{2,1,0:T(8,128)(2,1)S(1)} %get-tuple-element.211), channel_id=1, replica_groups=mesh['section'=16,'y'=4,'x'=4,'core'=2] {'y','x'}, dimensions={0} | all-to-all | bytes 655360 | tf_op jit(solution)/shard_map/all_to_all | solution.py:333
  222.4 11.4 %all_to_all.193.rows_ref = bf16[16,40,384]{2,1,0:T(8,128)(2,1)S(1)} all-to-all(bf16[16,40,384]{2,1,0:T(8,128)(2,1)S(1)} %get-tuple-element.215), channel_id=1, replica_groups=mesh['section'=16,'y'=4,'x'=4,'core'=2] {'y','x'}, dimensions={0} | all-to-all | bytes 983040 | tf_op jit(solution)/shard_map/all_to_all | solution.py:297
  233.8 2.0 shard_map.110
  235.9 10.5 %all_to_all.194.heads_ref = bf16[16,40,256]{2,1,0:T(8,128)(2,1)S(1)} all-to-all(bf16[16,40,256]{2,1,0:T(8,128)(2,1)S(1)} %get-tuple-element.219), channel_id=1, replica_groups=mesh['section'=16,'y'=4,'x'=4,'core'=2] {'y','x'}, dimensions={0} | all-to-all | bytes 655360 | tf_op jit(solution)/shard_map/all_to_all | solution.py:333
  248.4 11.4 %all_to_all.195.rows_ref = bf16[16,40,384]{2,1,0:T(8,128)(2,1)S(1)} all-to-all(bf16[16,40,384]{2,1,0:T(8,128)(2,1)S(1)} %get-tuple-element.223), channel_id=1, replica_groups=mesh['section'=16,'y'=4,'x'=4,'core'=2] {'y','x'}, dimensions={0} | all-to-all | bytes 983040 | tf_op jit(solution)/shard_map/all_to_all | solution.py:297
  259.9 2.0 shard_map.113
  261.9 10.5 %all_to_all.196.heads_ref = bf16[16,40,256]{2,1,0:T(8,128)(2,1)S(1)} all-to-all(bf16[16,40,256]{2,1,0:T(8,128)(2,1)S(1)} %get-tuple-element.227), channel_id=1, replica_groups=mesh['section'=16,'y'=4,'x'=4,'core'=2] {'y','x'}, dimensions={0} | all-to-all | bytes 655360 | tf_op jit(solution)/shard_map/all_to_all | solution.py:333
  274.4 11.6 %all_to_all.197.rows_ref = bf16[16,40,384]{2,1,0:T(8,128)(2,1)S(1)} all-to-all(bf16[16,40,384]{2,1,0:T(8,128)(2,1)S(1)} %get-tuple-element.231), channel_id=1, replica_groups=mesh['section'=16,'y'=4,'x'=4,'core'=2] {'y','x'}, dimensions={0} | all-to-all | bytes 983040 | tf_op jit(solution)/shard_map/all_to_all | solution.py:297
  286.0 2.0 shard_map.116
  288.1 11.0 %all_to_all.198.heads_ref = bf16[16,40,256]{2,1,0:T(8,128)(2,1)S(1)} all-to-all(bf16[16,40,256]{2,1,0:T(8,128)(2,1)S(1)} %get-tuple-element.235), channel_id=1, replica_groups=mesh['section'=16,'y'=4,'x'=4,'core'=2] {'y','x'}, dimensions={0} | all-to-all | bytes 655360 | tf_op jit(solution)/shard_map/all_to_all | solution.py:333
  301.1 13.7 %all_to_all.199.rows_ref = bf16[16,40,384]{2,1,0:T(8,128)(2,1)S(1)} all-to-all(bf16[16,40,384]{2,1,0:T(8,128)(2,1)S(1)} %get-tuple-element.239), channel_id=1, replica_groups=mesh['section'=16,'y'=4,'x'=4,'core'=2] {'y','x'}, dimensions={0} | all-to-all | bytes 983040 | tf_op jit(solution)/shard_map/all_to_all | solution.py:297
  314.8 2.0 shard_map.119
  316.8 11.4 %all_to_all.200.heads_ref = bf16[16,40,256]{2,1,0:T(8,128)(2,1)S(1)} all-to-all(bf16[16,40,256]{2,1,0:T(8,128)(2,1)S(1)} %get-tuple-element.243), channel_id=1, replica_groups=mesh['section'=16,'y'=4,'x'=4,'core'=2] {'y','x'}, dimensions={0} | all-to-all | bytes 655360 | tf_op jit(solution)/shard_map/all_to_all | solution.py:333
  330.3 11.6 %all_to_all.201.rows_ref = bf16[16,40,384]{2,1,0:T(8,128)(2,1)S(1)} all-to-all(bf16[16,40,384]{2,1,0:T(8,128)(2,1)S(1)} %get-tuple-element.247), channel_id=1, replica_groups=mesh['section'=16,'y'=4,'x'=4,'core'=2] {'y','x'}, dimensions={0} | all-to-all | bytes 983040 | tf_op jit(solution)/shard_map/all_to_all | solution.py:297
  341.9 2.0 shard_map.122
  343.9 10.5 %all_to_all.202.heads_ref = bf16[16,40,256]{2,1,0:T(8,128)(2,1)S(1)} all-to-all(bf16[16,40,256]{2,1,0:T(8,128)(2,1)S(1)} %get-tuple-element.251), channel_id=1, replica_groups=mesh['section'=16,'y'=4,'x'=4,'core'=2] {'y','x'}, dimensions={0} | all-to-all | bytes 655360 | tf_op jit(solution)/shard_map/all_to_all | solution.py:333
  356.5 11.4 %all_to_all.203.rows_ref = bf16[16,40,384]{2,1,0:T(8,128)(2,1)S(1)} all-to-all(bf16[16,40,384]{2,1,0:T(8,128)(2,1)S(1)} %get-tuple-element.255), channel_id=1, replica_groups=mesh['section'=16,'y'=4,'x'=4,'core'=2] {'y','x'}, dimensions={0} | all-to-all | bytes 983040 | tf_op jit(solution)/shard_map/all_to_all | solution.py:297
  367.9 2.0 shard_map.125
  369.9 10.5 %all_to_all.204.heads_ref = bf16[16,40,256]{2,1,0:T(8,128)(2,1)S(1)} all-to-all(bf16[16,40,256]{2,1,0:T(8,128)(2,1)S(1)} %get-tuple-element.259), channel_id=1, replica_groups=mesh['section'=16,'y'=4,'x'=4,'core'=2] {'y','x'}, dimensions={0} | all-to-all | bytes 655360 | tf_op jit(solution)/shard_map/all_to_all | solution.py:333
  382.5 11.4 %all_to_all.205.rows_ref = bf16[16,40,384]{2,1,0:T(8,128)(2,1)S(1)} all-to-all(bf16[16,40,384]{2,1,0:T(8,128)(2,1)S(1)} %get-tuple-element.263), channel_id=1, replica_groups=mesh['section'=16,'y'=4,'x'=4,'core'=2] {'y','x'}, dimensions={0} | all-to-all | bytes 983040 | tf_op jit(solution)/shard_map/all_to_all | solution.py:297
  393.9 2.0 shard_map.128
  396.0 10.5 %all_to_all.206.heads_ref = bf16[16,40,256]{2,1,0:T(8,128)(2,1)S(1)} all-to-all(bf16[16,40,256]{2,1,0:T(8,128)(2,1)S(1)} %get-tuple-element.267), channel_id=1, replica_groups=mesh['section'=16,'y'=4,'x'=4,'core'=2] {'y','x'}, dimensions={0} | all-to-all | bytes 655360 | tf_op jit(solution)/shard_map/all_to_all | solution.py:333
  408.5 11.7 %all_to_all.207.rows_ref = bf16[16,40,384]{2,1,0:T(8,128)(2,1)S(1)} all-to-all(bf16[16,40,384]{2,1,0:T(8,128)(2,1)S(1)} %get-tuple-element.271), channel_id=1, replica_groups=mesh['section'=16,'y'=4,'x'=4,'core'=2] {'y','x'}, dimensions={0} | all-to-all | bytes 983040 | tf_op jit(solution)/shard_map/all_to_all | solution.py:297
  420.2 2.0 shard_map.131
  422.2 10.5 %all_to_all.208.heads_ref = bf16[16,40,256]{2,1,0:T(8,128)(2,1)S(1)} all-to-all(bf16[16,40,256]{2,1,0:T(8,128)(2,1)S(1)} %get-tuple-element.275), channel_id=1, replica_groups=mesh['section'=16,'y'=4,'x'=4,'core'=2] {'y','x'}, dimensions={0} | all-to-all | bytes 655360 | tf_op jit(solution)/shard_map/all_to_all | solution.py:333
  434.8 12.9 %all_to_all.209.rows_ref = bf16[16,40,384]{2,1,0:T(8,128)(2,1)S(1)} all-to-all(bf16[16,40,384]{2,1,0:T(8,128)(2,1)S(1)} %get-tuple-element.279), channel_id=1, replica_groups=mesh['section'=16,'y'=4,'x'=4,'core'=2] {'y','x'}, dimensions={0} | all-to-all | bytes 983040 | tf_op jit(solution)/shard_map/all_to_all | solution.py:297
  447.7 2.0 shard_map.134
  449.7 12.1 %all_to_all.210.heads_ref = bf16[16,40,256]{2,1,0:T(8,128)(2,1)S(1)} all-to-all(bf16[16,40,256]{2,1,0:T(8,128)(2,1)S(1)} %get-tuple-element.283), channel_id=1, replica_groups=mesh['section'=16,'y'=4,'x'=4,'core'=2] {'y','x'}, dimensions={0} | all-to-all | bytes 655360 | tf_op jit(solution)/shard_map/all_to_all | solution.py:333
  463.2 11.8 %all_to_all.211.rows_ref = bf16[16,40,384]{2,1,0:T(8,128)(2,1)S(1)} all-to-all(bf16[16,40,384]{2,1,0:T(8,128)(2,1)S(1)} %get-tuple-element.287), channel_id=1, replica_groups=mesh['section'=16,'y'=4,'x'=4,'core'=2] {'y','x'}, dimensions={0} | all-to-all | bytes 983040 | tf_op jit(solution)/shard_map/all_to_all | solution.py:297
  475.0 2.8 shard_map.137
  477.7 3.5 all-to-all-start.33
  482.4 6.8 %all-to-all-done.33.heads_ref = bf16[16,40,256]{2,1,0:T(8,128)(2,1)S(1)} async-done(((bf16[16,40,256]{2,1,0:T(8,128)(2,1)}), bf16[16,40,256]{2,1,0:T(8,128)(2,1)S(1)}, u32[]{:S(2)}, u32[]{:S(2)}) %all-to-all-start.33) | async-done | bytes 327712 | tf_op jit(solution)/shard_map/all_to_all | solution.py:333
  490.7 48.7 %collective-permute-start.34 = (bf16[80,192]{1,0:T(8,128)(2,1)S(1)}, bf16[80,192]{1,0:T(8,128)(2,1)S(1)}, u32[]{:S(2)}, u32[]{:S(2)}) collective-permute-start(bf16[80,192]{1,0:T(8,128)(2,1)S(1)} %get-tuple-element.300), channel_id=1, source_target_pairs={{0,1},{1,0},{2,3},{3,2},{4,5},{5,4},{6,7},{7,6},{8,9},{9,8},{10,11... | collective-permute-start | bytes 92168 | tf_op jit(solution)/shard_map/ppermute | solution.py:261
  540.5 10.2 %all_to_all.212.pieces_ref = f32[32,1,128]{2,1,0:T(1,128)S(1)} all-to-all(f32[32,1,128]{2,1,0:T(1,128)S(1)} %shard_map.140), channel_id=1, replica_groups=mesh['section'=16,'y'=4,'x'=4,'core'=2] {'y','x','core'}, dimensions={0} | all-to-all | bytes 32768 | tf_op jit(solution)/shard_map/all_to_all | solution.py:367
  551.3 50.0 %all-to-all-start.35 = ((f32[16,1,128]{2,1,0:T(1,128)}), f32[16,1,128]{2,1,0:T(1,128)S(1)}, u32[]{:S(2)}, u32[]{:S(2)}) async-start(f32[16,1,128]{2,1,0:T(1,128)} %shard_map.141), calls=%async_computation.35 | async-start | bytes 16384 | tf_op jit(solution)/shard_map/all_to_all | solution.py:369
  602.3 10.4 %all-to-all-done.35.pieces_ref = f32[16,1,128]{2,1,0:T(1,128)S(1)} async-done(((f32[16,1,128]{2,1,0:T(1,128)}), f32[16,1,128]{2,1,0:T(1,128)S(1)}, u32[]{:S(2)}, u32[]{:S(2)}) %all-to-all-start.35) | async-done | bytes 8224 | tf_op jit(solution)/shard_map/all_to_all | solution.py:369
  (135 shorter events, 44.5 us)
Async XLA Ops:
  0.6 9.9 %collective-permute-start = (bf16[192,128]{1,0:T(8,128)(2,1)}, bf16[192,128]{1,0:T(8,128)(2,1)S(1)}, u32[]{:S(2)}, u32[]{:S(2)}) collective-permute-start(bf16[192,128]{1,0:T(8,128)(2,1)} %bitcast.17), channel_id=1, source_target_pairs={{0,1},{1,0},{2,3},{3,2},{4,5},{5,4},{6,7},{7,6},{8,9},{9,8},{10,11... | collective-permute-start | bytes 147464 | tf_op jit(solution)/shard_map/ppermute | solution.py:261
  10.5 0.8 copy-start.7
  11.3 0.7 copy-start.9
  13.3 10.2 %collective-permute-start.1 = (bf16[6144,128]{1,0:T(8,128)(2,1)}, bf16[6144,128]{1,0:T(8,128)(2,1)S(1)}, u32[]{:S(2)}, u32[]{:S(2)}) collective-permute-start(bf16[6144,128]{1,0:T(8,128)(2,1)} %bitcast.22), channel_id=1, source_target_pairs={{0,1},{1,0},{2,3},{3,2},{4,5},{5,4},{6,7},{7,6},{8,9},{9,8},{10,11... | collective-permute-start | bytes 4718600 | tf_op jit(solution)/shard_map/ppermute | solution.py:261
  15.5 8.0 %collective-permute-start.2 = (bf16[6144,128]{1,0:T(8,128)(2,1)}, bf16[6144,128]{1,0:T(8,128)(2,1)}, u32[]{:S(2)}, u32[]{:S(2)}) collective-permute-start(bf16[6144,128]{1,0:T(8,128)(2,1)} %bitcast.24), channel_id=1, source_target_pairs={{0,1},{1,0},{2,3},{3,2},{4,5},{5,4},{6,7},{7,6},{8,9},{9,8},{10,11... | collective-permute-start | bytes 4718600 | tf_op jit(solution)/shard_map/ppermute | solution.py:261
  17.6 5.9 collective-permute-start.3
  19.9 14.4 %all-to-all-start = ((bf16[16,40,384]{2,1,0:T(8,128)(2,1)}), bf16[16,40,384]{2,1,0:T(8,128)(2,1)S(1)}, u32[]{:S(2)}, u32[]{:S(2)}) async-start(bf16[16,40,384]{2,1,0:T(8,128)(2,1)} %get-tuple-element.152), calls=%async_computation | async-start | bytes 983040 | tf_op jit(solution)/shard_map/all_to_all | solution.py:297
  23.5 10.9 %copy-start.4 = (f32[1,6144]{1,0:T(1,128)S(1)}, f32[1,6144]{1,0:T(1,128)}, u32[]{:S(2)}) copy-start(f32[1,6144]{1,0:T(1,128)} %gain_ref.33) | copy-start | bytes 73732
  23.5 1.2 copy-start.11
  34.3 2.8 copy-start
  37.1 31.7 %copy-start.1 = (bf16[6144,512]{1,0:T(8,128)(2,1)S(1)}, bf16[6144,512]{1,0:T(8,128)(2,1)}, u32[]{:S(2)}) copy-start(bf16[6144,512]{1,0:T(8,128)(2,1)} %get-tuple-element.159.w_ref) | copy-start | bytes 18874372
  52.2 1.9 copy-start.2
  54.7 2.3 collective-permute-start.4
  68.8 12.5 %copy-start.3 = (bf16[4096,384]{1,0:T(8,128)(2,1)S(1)}, bf16[4096,384]{1,0:T(8,128)(2,1)}, u32[]{:S(2)}) copy-start(bf16[4096,384]{1,0:T(8,128)(2,1)} %get-tuple-element.164.w_ref) | copy-start | bytes 9437188
  81.9 4.9 collective-permute-start.5
  82.6 5.2 collective-permute-start.6
  112.4 1.3 collective-permute-start.7
  113.1 0.7 collective-permute-start.8
  138.5 1.3 collective-permute-start.9
  139.1 0.7 collective-permute-start.10
  167.1 1.3 collective-permute-start.11
  167.8 0.7 collective-permute-start.12
  194.9 1.3 collective-permute-start.13
  195.6 0.7 collective-permute-start.14
  220.9 1.3 collective-permute-start.15
  221.6 0.7 collective-permute-start.16
  247.0 1.3 collective-permute-start.17
  247.6 0.7 collective-permute-start.18
  273.0 1.3 collective-permute-start.19
  273.7 0.7 collective-permute-start.20
  299.7 1.3 collective-permute-start.21
  300.3 0.7 collective-permute-start.22
  328.8 1.3 collective-permute-start.23
  329.5 0.7 collective-permute-start.24
  355.0 1.3 collective-permute-start.25
  355.7 0.7 collective-permute-start.26
  381.0 1.3 collective-permute-start.27
  381.7 0.7 collective-permute-start.28
  407.1 1.3 collective-permute-start.29
  407.7 0.7 collective-permute-start.30
  433.3 1.3 collective-permute-start.31
  434.0 0.7 collective-permute-start.32
  462.4 12.6 %copy-start.5 = (bf16[2,40,384]{2,1,0:T(8,128)(2,1)}, bf16[2,40,384]{2,1,0:T(8,128)(2,1)S(1)}, u32[]{:S(2)}) copy-start(bf16[2,40,384]{2,1,0:T(8,128)(2,1)S(1)} %get-tuple-element.294.kept_ref) | copy-start | bytes 184324
  462.4 0.7 collective-permute-start.33
  477.7 11.5 %all-to-all-start.33 = ((bf16[16,40,256]{2,1,0:T(8,128)(2,1)}), bf16[16,40,256]{2,1,0:T(8,128)(2,1)S(1)}, u32[]{:S(2)}, u32[]{:S(2)}) async-start(bf16[16,40,256]{2,1,0:T(8,128)(2,1)} %shard_map.137), calls=%async_computation.33 | async-start | bytes 655360 | tf_op jit(solution)/shard_map/all_to_all | solution.py:333
  489.2 0.8 copy-start.6
  490.1 50.2 %copy-start.8 = (bf16[128,192]{0,1:T(8,128)(2,1)S(1)}, bf16[128,192]{0,1:T(8,128)(2,1)}, u32[]{:S(2)}) copy-start(bf16[128,192]{0,1:T(8,128)(2,1)} %param.8) | copy-start | bytes 147460
  490.1 122.6 %copy-start.10 = (s32[128]{0:T(128)S(1)}, s32[128]{0:T(128)}, u32[]{:S(2)}) copy-start(s32[128]{0:T(128)} %param.9) | copy-start | bytes 1540
  490.7 49.6 %collective-permute-start.34 = (bf16[80,192]{1,0:T(8,128)(2,1)S(1)}, bf16[80,192]{1,0:T(8,128)(2,1)S(1)}, u32[]{:S(2)}, u32[]{:S(2)}) collective-permute-start(bf16[80,192]{1,0:T(8,128)(2,1)S(1)} %get-tuple-element.300), channel_id=1, source_target_pairs={{0,1},{1,0},{2,3},{3,2},{4,5},{5,4},{6,7},{7,6},{8,9},{9,8},{10,11... | collective-permute-start | bytes 92168 | tf_op jit(solution)/shard_map/ppermute | solution.py:261
  551.3 61.3 %all-to-all-start.35 = ((f32[16,1,128]{2,1,0:T(1,128)}), f32[16,1,128]{2,1,0:T(1,128)S(1)}, u32[]{:S(2)}, u32[]{:S(2)}) async-start(f32[16,1,128]{2,1,0:T(1,128)} %shard_map.141), calls=%async_computation.35 | async-start | bytes 16384 | tf_op jit(solution)/shard_map/all_to_all | solution.py:369

commit v8 on v7

--- a/solution.py
+++ b/solution.py
@@ -66,8 +66,7 @@
     section = lax.axis_index("section")
     row = iota(flag_ref.shape, 0)
     order = jnp.where(row == 0, -section, 0)
-    order = jnp.where((row == 1) & (section == 0), 1, order)
-    flag_ref[...] = jnp.where(row == 2, lax.axis_index("core"), order).astype(F32)
+    flag_ref[...] = jnp.where((row == 1) & (section == 0), 1, order).astype(F32)
 
 
 def qkv_attention(
@@ -188,6 +187,16 @@
         send_ref[chip] = rows
 
 
+def split_columns(done_ref, keep_ref, give_ref):
+    half = keep_ref.shape[2]
+    first = lax.axis_index("core") == 0
+    for number in range(done_ref.shape[0]):
+        rows = done_ref[number].astype(F32)
+        low, high = rows[:, :half], rows[:, half:]
+        keep_ref[number] = jnp.where(first, low, high).astype(BF)
+        give_ref[number] = jnp.where(first, high, low).astype(BF)
+
+
 def row_parts(keep_ref, other_ref):
     first = lax.axis_index("core") == 0
     keep, other = keep_ref[...], other_ref[...]
@@ -275,7 +284,6 @@
         swap(tokens_t),
     )
 
-    first_flags = flags
     keys = jnp.zeros((length, width), F32)
     vals = jnp.zeros((length, width), F32)
     done = jnp.zeros((slices, length, cols), BF)
@@ -357,11 +365,9 @@
                 received[number] = jnp.zeros_like(rows)
         received = [received[number] for number in range(slices)]
 
-    part_rows = done.reshape(part, cols)
-    halves = [part_rows[:, :cols_own], part_rows[:, cols_own:]]
-    own_first = first_flags[2:3, 0:1] == 0.0
-    keep = jnp.where(own_first, halves[0], halves[1])
-    other = swap(jnp.where(own_first, halves[1], halves[0]))
+    keep, give = run(split_columns, [((slices, length, cols_own), BF)] * 2, done)
+    keep = keep.reshape(part, cols_own)
+    other = swap(give.reshape(part, cols_own))
     targets_t = jnp.swapaxes(targets, 0, 1)
     send = run(token_errors, ((2 * chips, 1, row_count), F32), picks, keep, other, targets_t)
     send = lax.all_to_all(send, PLANE + ("core",), 0, 0, tiled=True)

time: 624 us -> 624 us (level)
  blocking collectives: 376 us -> 387 us
  waiting for transfers between devices: 23.2 us -> 16.5 us
    all_to_all x16 -> x17, blocking collectives: 177 us -> 187 us  [local(): attended = lax.all_to_all(send, PLANE, 0, 0, tiled=True)]
    all_to_all x1 -> x0, waiting for transfers between devices: 6.79 us -> none  [local(): attended = lax.all_to_all(send, PLANE, 0, 0, tiled=True)]
    pallas_call x56 -> x57, Pallas kernels: 48.6 us -> 48.6 us  [run(): pl.pallas_call(kernel, out_shape=shapes if several else shapes[0], in_spe...]
  transfers between devices with their start and end apart: 38 -> 37, of which waited for: 7 -> 6; matrix products, arithmetic and copies ran while one was open for 0% -> 0% of each run, Pallas kernels for 1% -> 1%
where the time goes in v8:
time: 624 us; the launch traced here: 614 us
  blocking collectives  387 us (62%)
  starting transfers between devices  144 us (23%)
  Pallas kernels  56.1 us (9%)
  waiting for transfers between devices  16.5 us (3%)
  local copies, waits for them, and re-layouts  8.63 us (1%)
    all_to_all x16, blocking collectives, local(): gathered = lax.all_to_all(send, PLANE, 0, 0, tiled=True)  190 us
    all_to_all x17, blocking collectives, local(): attended = lax.all_to_all(send, PLANE, 0, 0, tiled=True)  187 us
    ppermute x5, starting transfers between devices, swap(): return lax.ppermute(value, 'core', [(0, 1), (1, 0)])  64.5 us
    all_to_all x1, starting transfers between devices, local(): send = lax.all_to_all(send, 'section', 0, 0, tiled=True)  51.6 us
    pallas_call x57, Pallas kernels, run(): pl.pallas_call(kernel, out_shape=shapes if several else shapes[0], in_spe...  48.6 us
    ppermute x30, starting transfers between devices, local(): received[number] = lax.ppermute(rows, 'section', [(z, z + 1)])  24.1 us
  transfers between devices with their start and end apart: 37, of which 6 were waited for; matrix products, arithmetic and copies ran while one was open for 0% of the time, Pallas kernels for 1%

profile of v8, /device:TPU:1, one launch (start us, length us, event | category | flops | bytes accessed | tf_op | source)
XLA Modules:
  0.0 613.9 jit_solution(8616781147018785637)
XLA Ops:
  0.6 8.8 %collective-permute-start = (bf16[192,128]{1,0:T(8,128)(2,1)}, bf16[192,128]{1,0:T(8,128)(2,1)S(1)}, u32[]{:S(2)}, u32[]{:S(2)}) collective-permute-start(bf16[192,128]{1,0:T(8,128)(2,1)} %bitcast.18), channel_id=1, source_target_pairs={{0,1},{1,0},{2,3},{3,2},{4,5},{5,4},{6,7},{7,6},{8,9},{9,8},{10,11... | collective-permute-start | bytes 147464 | tf_op jit(solution)/shard_map/ppermute | solution.py:270
  13.3 2.2 collective-permute-start.1
  15.5 2.1 collective-permute-start.2
  17.6 2.3 collective-permute-start.3
  19.9 3.6 all-to-all-start
  24.6 7.5 %shard_map.88 = (bf16[6144,512]{1,0:T(8,128)(2,1)}, bf16[4096,384]{1,0:T(8,128)(2,1)}) custom-call(bf16[6144,128]{1,0:T(8,128)(2,1)} %bitcast.25, bf16[6144,128]{1,0:T(8,128)(2,1)} %copy-done.9, bf16[6144,128]{1,0:T(8,128)(2,1)} %bitcast.27, bf16[6144,128]{1,0:T(8,128)(2,1)} %collective-permute-done.2.val_other_ref, bf16[192,4096]{1,0:T(8,128)(2,1)} %bitcast.29, ...), custom_call_target="tpu_custom_call" | custom-call | bytes 18874368 | tf_op jit(solution)/shard_map/pallas_call | solution.py:307
  32.1 2.2 all-to-all-done.rows_ref
  34.3 2.8 copy-done
  37.1 2.0 shard_map.89
  39.2 13.0 %all_to_all.180.heads_ref = bf16[16,40,256]{2,1,0:T(8,128)(2,1)S(1)} all-to-all(bf16[16,40,256]{2,1,0:T(8,128)(2,1)S(1)} %get-tuple-element.165), channel_id=1, replica_groups=mesh['section'=16,'y'=4,'x'=4,'core'=2] {'y','x'}, dimensions={0} | all-to-all | bytes 655360 | tf_op jit(solution)/shard_map/all_to_all | solution.py:341
  52.2 1.9 copy-done.2
  57.0 11.7 %all_to_all.181.rows_ref = bf16[16,40,384]{2,1,0:T(8,128)(2,1)S(1)} all-to-all(bf16[16,40,384]{2,1,0:T(8,128)(2,1)S(1)} %get-tuple-element.169), channel_id=1, replica_groups=mesh['section'=16,'y'=4,'x'=4,'core'=2] {'y','x'}, dimensions={0} | all-to-all | bytes 983040 | tf_op jit(solution)/shard_map/all_to_all | solution.py:305
  68.7 2.0 shard_map.92
  70.7 10.5 %all_to_all.182.heads_ref = bf16[16,40,256]{2,1,0:T(8,128)(2,1)S(1)} all-to-all(bf16[16,40,256]{2,1,0:T(8,128)(2,1)S(1)} %get-tuple-element.173), channel_id=1, replica_groups=mesh['section'=16,'y'=4,'x'=4,'core'=2] {'y','x'}, dimensions={0} | all-to-all | bytes 655360 | tf_op jit(solution)/shard_map/all_to_all | solution.py:341
  82.5 4.2 collective-permute-start.6
  87.8 11.4 %all_to_all.183.rows_ref = bf16[16,40,384]{2,1,0:T(8,128)(2,1)S(1)} all-to-all(bf16[16,40,384]{2,1,0:T(8,128)(2,1)S(1)} %get-tuple-element.177), channel_id=1, replica_groups=mesh['section'=16,'y'=4,'x'=4,'core'=2] {'y','x'}, dimensions={0} | all-to-all | bytes 983040 | tf_op jit(solution)/shard_map/all_to_all | solution.py:305
  99.3 2.0 shard_map.95
  101.3 10.5 %all_to_all.184.heads_ref = bf16[16,40,256]{2,1,0:T(8,128)(2,1)S(1)} all-to-all(bf16[16,40,256]{2,1,0:T(8,128)(2,1)S(1)} %get-tuple-element.181), channel_id=1, replica_groups=mesh['section'=16,'y'=4,'x'=4,'core'=2] {'y','x'}, dimensions={0} | all-to-all | bytes 655360 | tf_op jit(solution)/shard_map/all_to_all | solution.py:341
  113.9 11.4 %all_to_all.185.rows_ref = bf16[16,40,384]{2,1,0:T(8,128)(2,1)S(1)} all-to-all(bf16[16,40,384]{2,1,0:T(8,128)(2,1)S(1)} %get-tuple-element.185), channel_id=1, replica_groups=mesh['section'=16,'y'=4,'x'=4,'core'=2] {'y','x'}, dimensions={0} | all-to-all | bytes 983040 | tf_op jit(solution)/shard_map/all_to_all | solution.py:305
  125.3 2.0 shard_map.98
  127.4 10.5 %all_to_all.186.heads_ref = bf16[16,40,256]{2,1,0:T(8,128)(2,1)S(1)} all-to-all(bf16[16,40,256]{2,1,0:T(8,128)(2,1)S(1)} %get-tuple-element.189), channel_id=1, replica_groups=mesh['section'=16,'y'=4,'x'=4,'core'=2] {'y','x'}, dimensions={0} | all-to-all | bytes 655360 | tf_op jit(solution)/shard_map/all_to_all | solution.py:341
  139.9 11.9 %all_to_all.187.rows_ref = bf16[16,40,384]{2,1,0:T(8,128)(2,1)S(1)} all-to-all(bf16[16,40,384]{2,1,0:T(8,128)(2,1)S(1)} %get-tuple-element.193), channel_id=1, replica_groups=mesh['section'=16,'y'=4,'x'=4,'core'=2] {'y','x'}, dimensions={0} | all-to-all | bytes 983040 | tf_op jit(solution)/shard_map/all_to_all | solution.py:305
  151.9 2.0 shard_map.101
  153.9 12.6 %all_to_all.188.heads_ref = bf16[16,40,256]{2,1,0:T(8,128)(2,1)S(1)} all-to-all(bf16[16,40,256]{2,1,0:T(8,128)(2,1)S(1)} %get-tuple-element.197), channel_id=1, replica_groups=mesh['section'=16,'y'=4,'x'=4,'core'=2] {'y','x'}, dimensions={0} | all-to-all | bytes 655360 | tf_op jit(solution)/shard_map/all_to_all | solution.py:341
  168.6 12.7 %all_to_all.189.rows_ref = bf16[16,40,384]{2,1,0:T(8,128)(2,1)S(1)} all-to-all(bf16[16,40,384]{2,1,0:T(8,128)(2,1)S(1)} %get-tuple-element.201), channel_id=1, replica_groups=mesh['section'=16,'y'=4,'x'=4,'core'=2] {'y','x'}, dimensions={0} | all-to-all | bytes 983040 | tf_op jit(solution)/shard_map/all_to_all | solution.py:305
  181.3 2.0 shard_map.104
  183.3 11.1 %all_to_all.190.heads_ref = bf16[16,40,256]{2,1,0:T(8,128)(2,1)S(1)} all-to-all(bf16[16,40,256]{2,1,0:T(8,128)(2,1)S(1)} %get-tuple-element.205), channel_id=1, replica_groups=mesh['section'=16,'y'=4,'x'=4,'core'=2] {'y','x'}, dimensions={0} | all-to-all | bytes 655360 | tf_op jit(solution)/shard_map/all_to_all | solution.py:341
  196.5 11.4 %all_to_all.191.rows_ref = bf16[16,40,384]{2,1,0:T(8,128)(2,1)S(1)} all-to-all(bf16[16,40,384]{2,1,0:T(8,128)(2,1)S(1)} %get-tuple-element.209), channel_id=1, replica_groups=mesh['section'=16,'y'=4,'x'=4,'core'=2] {'y','x'}, dimensions={0} | all-to-all | bytes 983040 | tf_op jit(solution)/shard_map/all_to_all | solution.py:305
  207.9 2.0 shard_map.107
  209.9 10.5 %all_to_all.192.heads_ref = bf16[16,40,256]{2,1,0:T(8,128)(2,1)S(1)} all-to-all(bf16[16,40,256]{2,1,0:T(8,128)(2,1)S(1)} %get-tuple-element.213), channel_id=1, replica_groups=mesh['section'=16,'y'=4,'x'=4,'core'=2] {'y','x'}, dimensions={0} | all-to-all | bytes 655360 | tf_op jit(solution)/shard_map/all_to_all | solution.py:341
  222.5 11.4 %all_to_all.193.rows_ref = bf16[16,40,384]{2,1,0:T(8,128)(2,1)S(1)} all-to-all(bf16[16,40,384]{2,1,0:T(8,128)(2,1)S(1)} %get-tuple-element.217), channel_id=1, replica_groups=mesh['section'=16,'y'=4,'x'=4,'core'=2] {'y','x'}, dimensions={0} | all-to-all | bytes 983040 | tf_op jit(solution)/shard_map/all_to_all | solution.py:305
  234.0 2.0 shard_map.110
  236.0 10.5 %all_to_all.194.heads_ref = bf16[16,40,256]{2,1,0:T(8,128)(2,1)S(1)} all-to-all(bf16[16,40,256]{2,1,0:T(8,128)(2,1)S(1)} %get-tuple-element.221), channel_id=1, replica_groups=mesh['section'=16,'y'=4,'x'=4,'core'=2] {'y','x'}, dimensions={0} | all-to-all | bytes 655360 | tf_op jit(solution)/shard_map/all_to_all | solution.py:341
  248.6 11.4 %all_to_all.195.rows_ref = bf16[16,40,384]{2,1,0:T(8,128)(2,1)S(1)} all-to-all(bf16[16,40,384]{2,1,0:T(8,128)(2,1)S(1)} %get-tuple-element.225), channel_id=1, replica_groups=mesh['section'=16,'y'=4,'x'=4,'core'=2] {'y','x'}, dimensions={0} | all-to-all | bytes 983040 | tf_op jit(solution)/shard_map/all_to_all | solution.py:305
  260.0 2.0 shard_map.113
  262.0 10.5 %all_to_all.196.heads_ref = bf16[16,40,256]{2,1,0:T(8,128)(2,1)S(1)} all-to-all(bf16[16,40,256]{2,1,0:T(8,128)(2,1)S(1)} %get-tuple-element.229), channel_id=1, replica_groups=mesh['section'=16,'y'=4,'x'=4,'core'=2] {'y','x'}, dimensions={0} | all-to-all | bytes 655360 | tf_op jit(solution)/shard_map/all_to_all | solution.py:341
  274.6 11.6 %all_to_all.197.rows_ref = bf16[16,40,384]{2,1,0:T(8,128)(2,1)S(1)} all-to-all(bf16[16,40,384]{2,1,0:T(8,128)(2,1)S(1)} %get-tuple-element.233), channel_id=1, replica_groups=mesh['section'=16,'y'=4,'x'=4,'core'=2] {'y','x'}, dimensions={0} | all-to-all | bytes 983040 | tf_op jit(solution)/shard_map/all_to_all | solution.py:305
  286.2 2.0 shard_map.116
  288.3 11.0 %all_to_all.198.heads_ref = bf16[16,40,256]{2,1,0:T(8,128)(2,1)S(1)} all-to-all(bf16[16,40,256]{2,1,0:T(8,128)(2,1)S(1)} %get-tuple-element.237), channel_id=1, replica_groups=mesh['section'=16,'y'=4,'x'=4,'core'=2] {'y','x'}, dimensions={0} | all-to-all | bytes 655360 | tf_op jit(solution)/shard_map/all_to_all | solution.py:341
  301.3 13.7 %all_to_all.199.rows_ref = bf16[16,40,384]{2,1,0:T(8,128)(2,1)S(1)} all-to-all(bf16[16,40,384]{2,1,0:T(8,128)(2,1)S(1)} %get-tuple-element.241), channel_id=1, replica_groups=mesh['section'=16,'y'=4,'x'=4,'core'=2] {'y','x'}, dimensions={0} | all-to-all | bytes 983040 | tf_op jit(solution)/shard_map/all_to_all | solution.py:305
  315.1 2.0 shard_map.119
  317.1 11.4 %all_to_all.200.heads_ref = bf16[16,40,256]{2,1,0:T(8,128)(2,1)S(1)} all-to-all(bf16[16,40,256]{2,1,0:T(8,128)(2,1)S(1)} %get-tuple-element.245), channel_id=1, replica_groups=mesh['section'=16,'y'=4,'x'=4,'core'=2] {'y','x'}, dimensions={0} | all-to-all | bytes 655360 | tf_op jit(solution)/shard_map/all_to_all | solution.py:341
  330.5 11.6 %all_to_all.201.rows_ref = bf16[16,40,384]{2,1,0:T(8,128)(2,1)S(1)} all-to-all(bf16[16,40,384]{2,1,0:T(8,128)(2,1)S(1)} %get-tuple-element.249), channel_id=1, replica_groups=mesh['section'=16,'y'=4,'x'=4,'core'=2] {'y','x'}, dimensions={0} | all-to-all | bytes 983040 | tf_op jit(solution)/shard_map/all_to_all | solution.py:305
  342.2 2.0 shard_map.122
  344.2 10.5 %all_to_all.202.heads_ref = bf16[16,40,256]{2,1,0:T(8,128)(2,1)S(1)} all-to-all(bf16[16,40,256]{2,1,0:T(8,128)(2,1)S(1)} %get-tuple-element.253), channel_id=1, replica_groups=mesh['section'=16,'y'=4,'x'=4,'core'=2] {'y','x'}, dimensions={0} | all-to-all | bytes 655360 | tf_op jit(solution)/shard_map/all_to_all | solution.py:341
  356.8 11.4 %all_to_all.203.rows_ref = bf16[16,40,384]{2,1,0:T(8,128)(2,1)S(1)} all-to-all(bf16[16,40,384]{2,1,0:T(8,128)(2,1)S(1)} %get-tuple-element.257), channel_id=1, replica_groups=mesh['section'=16,'y'=4,'x'=4,'core'=2] {'y','x'}, dimensions={0} | all-to-all | bytes 983040 | tf_op jit(solution)/shard_map/all_to_all | solution.py:305
  368.2 2.0 shard_map.125
  370.3 10.5 %all_to_all.204.heads_ref = bf16[16,40,256]{2,1,0:T(8,128)(2,1)S(1)} all-to-all(bf16[16,40,256]{2,1,0:T(8,128)(2,1)S(1)} %get-tuple-element.261), channel_id=1, replica_groups=mesh['section'=16,'y'=4,'x'=4,'core'=2] {'y','x'}, dimensions={0} | all-to-all | bytes 655360 | tf_op jit(solution)/shard_map/all_to_all | solution.py:341
  382.9 11.4 %all_to_all.205.rows_ref = bf16[16,40,384]{2,1,0:T(8,128)(2,1)S(1)} all-to-all(bf16[16,40,384]{2,1,0:T(8,128)(2,1)S(1)} %get-tuple-element.265), channel_id=1, replica_groups=mesh['section'=16,'y'=4,'x'=4,'core'=2] {'y','x'}, dimensions={0} | all-to-all | bytes 983040 | tf_op jit(solution)/shard_map/all_to_all | solution.py:305
  394.3 2.0 shard_map.128
  396.3 10.5 %all_to_all.206.heads_ref = bf16[16,40,256]{2,1,0:T(8,128)(2,1)S(1)} all-to-all(bf16[16,40,256]{2,1,0:T(8,128)(2,1)S(1)} %get-tuple-element.269), channel_id=1, replica_groups=mesh['section'=16,'y'=4,'x'=4,'core'=2] {'y','x'}, dimensions={0} | all-to-all | bytes 655360 | tf_op jit(solution)/shard_map/all_to_all | solution.py:341
  408.9 11.7 %all_to_all.207.rows_ref = bf16[16,40,384]{2,1,0:T(8,128)(2,1)S(1)} all-to-all(bf16[16,40,384]{2,1,0:T(8,128)(2,1)S(1)} %get-tuple-element.273), channel_id=1, replica_groups=mesh['section'=16,'y'=4,'x'=4,'core'=2] {'y','x'}, dimensions={0} | all-to-all | bytes 983040 | tf_op jit(solution)/shard_map/all_to_all | solution.py:305
  420.6 2.0 shard_map.131
  422.6 10.5 %all_to_all.208.heads_ref = bf16[16,40,256]{2,1,0:T(8,128)(2,1)S(1)} all-to-all(bf16[16,40,256]{2,1,0:T(8,128)(2,1)S(1)} %get-tuple-element.277), channel_id=1, replica_groups=mesh['section'=16,'y'=4,'x'=4,'core'=2] {'y','x'}, dimensions={0} | all-to-all | bytes 655360 | tf_op jit(solution)/shard_map/all_to_all | solution.py:341
  435.2 12.9 %all_to_all.209.rows_ref = bf16[16,40,384]{2,1,0:T(8,128)(2,1)S(1)} all-to-all(bf16[16,40,384]{2,1,0:T(8,128)(2,1)S(1)} %get-tuple-element.281), channel_id=1, replica_groups=mesh['section'=16,'y'=4,'x'=4,'core'=2] {'y','x'}, dimensions={0} | all-to-all | bytes 983040 | tf_op jit(solution)/shard_map/all_to_all | solution.py:305
  448.1 2.0 shard_map.134
  450.1 12.1 %all_to_all.210.heads_ref = bf16[16,40,256]{2,1,0:T(8,128)(2,1)S(1)} all-to-all(bf16[16,40,256]{2,1,0:T(8,128)(2,1)S(1)} %get-tuple-element.285), channel_id=1, replica_groups=mesh['section'=16,'y'=4,'x'=4,'core'=2] {'y','x'}, dimensions={0} | all-to-all | bytes 655360 | tf_op jit(solution)/shard_map/all_to_all | solution.py:341
  463.6 11.8 %all_to_all.211.rows_ref = bf16[16,40,384]{2,1,0:T(8,128)(2,1)S(1)} all-to-all(bf16[16,40,384]{2,1,0:T(8,128)(2,1)S(1)} %get-tuple-element.289), channel_id=1, replica_groups=mesh['section'=16,'y'=4,'x'=4,'core'=2] {'y','x'}, dimensions={0} | all-to-all | bytes 983040 | tf_op jit(solution)/shard_map/all_to_all | solution.py:305
  475.4 2.0 shard_map.137
  477.4 10.6 %all_to_all.212.heads_ref = bf16[16,40,256]{2,1,0:T(8,128)(2,1)S(1)} all-to-all(bf16[16,40,256]{2,1,0:T(8,128)(2,1)S(1)} %shard_map.137), channel_id=1, replica_groups=mesh['section'=16,'y'=4,'x'=4,'core'=2] {'y','x'}, dimensions={0} | all-to-all | bytes 655360 | tf_op jit(solution)/shard_map/all_to_all | solution.py:341
  488.7 49.1 %collective-permute-start.34 = (bf16[80,192]{1,0:T(8,128)(2,1)S(1)}, bf16[80,192]{1,0:T(8,128)(2,1)S(1)}, u32[]{:S(2)}, u32[]{:S(2)}) collective-permute-start(bf16[80,192]{1,0:T(8,128)(2,1)S(1)} %bitcast.23), channel_id=1, source_target_pairs={{0,1},{1,0},{2,3},{3,2},{4,5},{5,4},{6,7},{7,6},{8,9},{9,8},{10,11... | collective-permute-start | bytes 92168 | tf_op jit(solution)/shard_map/ppermute | solution.py:270
  539.0 10.2 %all_to_all.213.pieces_ref = f32[32,1,128]{2,1,0:T(1,128)S(1)} all-to-all(f32[32,1,128]{2,1,0:T(1,128)S(1)} %shard_map.141), channel_id=1, replica_groups=mesh['section'=16,'y'=4,'x'=4,'core'=2] {'y','x','core'}, dimensions={0} | all-to-all | bytes 32768 | tf_op jit(solution)/shard_map/all_to_all | solution.py:373
  549.8 51.6 %all-to-all-start.35 = ((f32[16,1,128]{2,1,0:T(1,128)}), f32[16,1,128]{2,1,0:T(1,128)S(1)}, u32[]{:S(2)}, u32[]{:S(2)}) async-start(f32[16,1,128]{2,1,0:T(1,128)} %shard_map.142), calls=%async_computation.35 | async-start | bytes 16384 | tf_op jit(solution)/shard_map/all_to_all | solution.py:375
  602.3 10.4 %all-to-all-done.35.pieces_ref = f32[16,1,128]{2,1,0:T(1,128)S(1)} async-done(((f32[16,1,128]{2,1,0:T(1,128)}), f32[16,1,128]{2,1,0:T(1,128)S(1)}, u32[]{:S(2)}, u32[]{:S(2)}) %all-to-all-start.35) | async-done | bytes 8224 | tf_op jit(solution)/shard_map/all_to_all | solution.py:375
  (129 shorter events, 41.9 us)
Async XLA Ops:
  0.6 9.9 %collective-permute-start = (bf16[192,128]{1,0:T(8,128)(2,1)}, bf16[192,128]{1,0:T(8,128)(2,1)S(1)}, u32[]{:S(2)}, u32[]{:S(2)}) collective-permute-start(bf16[192,128]{1,0:T(8,128)(2,1)} %bitcast.18), channel_id=1, source_target_pairs={{0,1},{1,0},{2,3},{3,2},{4,5},{5,4},{6,7},{7,6},{8,9},{9,8},{10,11... | collective-permute-start | bytes 147464 | tf_op jit(solution)/shard_map/ppermute | solution.py:270
  10.5 0.8 copy-start.5
  11.3 0.7 copy-start.7
  13.3 10.2 %collective-permute-start.1 = (bf16[6144,128]{1,0:T(8,128)(2,1)}, bf16[6144,128]{1,0:T(8,128)(2,1)S(1)}, u32[]{:S(2)}, u32[]{:S(2)}) collective-permute-start(bf16[6144,128]{1,0:T(8,128)(2,1)} %bitcast.24), channel_id=1, source_target_pairs={{0,1},{1,0},{2,3},{3,2},{4,5},{5,4},{6,7},{7,6},{8,9},{9,8},{10,11... | collective-permute-start | bytes 4718600 | tf_op jit(solution)/shard_map/ppermute | solution.py:270
  15.5 8.0 %collective-permute-start.2 = (bf16[6144,128]{1,0:T(8,128)(2,1)}, bf16[6144,128]{1,0:T(8,128)(2,1)}, u32[]{:S(2)}, u32[]{:S(2)}) collective-permute-start(bf16[6144,128]{1,0:T(8,128)(2,1)} %bitcast.26), channel_id=1, source_target_pairs={{0,1},{1,0},{2,3},{3,2},{4,5},{5,4},{6,7},{7,6},{8,9},{9,8},{10,11... | collective-permute-start | bytes 4718600 | tf_op jit(solution)/shard_map/ppermute | solution.py:270
  17.6 5.9 collective-permute-start.3
  19.9 14.4 %all-to-all-start = ((bf16[16,40,384]{2,1,0:T(8,128)(2,1)}), bf16[16,40,384]{2,1,0:T(8,128)(2,1)S(1)}, u32[]{:S(2)}, u32[]{:S(2)}) async-start(bf16[16,40,384]{2,1,0:T(8,128)(2,1)} %get-tuple-element.154), calls=%async_computation | async-start | bytes 983040 | tf_op jit(solution)/shard_map/all_to_all | solution.py:305
  23.5 10.9 %copy-start.4 = (f32[1,6144]{1,0:T(1,128)S(1)}, f32[1,6144]{1,0:T(1,128)}, u32[]{:S(2)}) copy-start(f32[1,6144]{1,0:T(1,128)} %gain_ref.33) | copy-start | bytes 73732
  23.5 1.1 copy-start.9
  34.3 2.8 copy-start
  37.1 31.6 %copy-start.1 = (bf16[6144,512]{1,0:T(8,128)(2,1)S(1)}, bf16[6144,512]{1,0:T(8,128)(2,1)}, u32[]{:S(2)}) copy-start(bf16[6144,512]{1,0:T(8,128)(2,1)} %get-tuple-element.161.w_ref) | copy-start | bytes 18874372
  52.2 1.9 copy-start.2
  54.6 2.3 collective-permute-start.4
  68.7 12.5 %copy-start.3 = (bf16[4096,384]{1,0:T(8,128)(2,1)S(1)}, bf16[4096,384]{1,0:T(8,128)(2,1)}, u32[]{:S(2)}) copy-start(bf16[4096,384]{1,0:T(8,128)(2,1)} %get-tuple-element.166.w_ref) | copy-start | bytes 9437188
  81.9 4.9 collective-permute-start.5
  82.5 5.2 collective-permute-start.6
  112.4 1.3 collective-permute-start.7
  113.1 0.7 collective-permute-start.8
  138.5 1.3 collective-permute-start.9
  139.2 0.7 collective-permute-start.10
  167.2 1.3 collective-permute-start.11
  167.8 0.7 collective-permute-start.12
  195.0 1.3 collective-permute-start.13
  195.7 0.7 collective-permute-start.14
  221.1 1.3 collective-permute-start.15
  221.7 0.7 collective-permute-start.16
  247.1 1.3 collective-permute-start.17
  247.8 0.7 collective-permute-start.18
  273.2 1.3 collective-permute-start.19
  273.9 0.7 collective-permute-start.20
  299.9 1.3 collective-permute-start.21
  300.5 0.7 collective-permute-start.22
  329.1 1.3 collective-permute-start.23
  329.8 0.7 collective-permute-start.24
  355.3 1.3 collective-permute-start.25
  356.0 0.7 collective-permute-start.26
  381.4 1.3 collective-permute-start.27
  382.1 0.7 collective-permute-start.28
  407.5 1.3 collective-permute-start.29
  408.1 0.7 collective-permute-start.30
  433.8 1.3 collective-permute-start.31
  434.4 0.7 collective-permute-start.32
  462.8 0.7 collective-permute-start.33
  488.0 50.8 %copy-start.6 = (bf16[128,192]{0,1:T(8,128)(2,1)S(1)}, bf16[128,192]{0,1:T(8,128)(2,1)}, u32[]{:S(2)}) copy-start(bf16[128,192]{0,1:T(8,128)(2,1)} %param.8) | copy-start | bytes 147460
  488.0 124.7 %copy-start.8 = (s32[128]{0:T(128)S(1)}, s32[128]{0:T(128)}, u32[]{:S(2)}) copy-start(s32[128]{0:T(128)} %param.9) | copy-start | bytes 1540
  488.7 50.0 %collective-permute-start.34 = (bf16[80,192]{1,0:T(8,128)(2,1)S(1)}, bf16[80,192]{1,0:T(8,128)(2,1)S(1)}, u32[]{:S(2)}, u32[]{:S(2)}) collective-permute-start(bf16[80,192]{1,0:T(8,128)(2,1)S(1)} %bitcast.23), channel_id=1, source_target_pairs={{0,1},{1,0},{2,3},{3,2},{4,5},{5,4},{6,7},{7,6},{8,9},{9,8},{10,11... | collective-permute-start | bytes 92168 | tf_op jit(solution)/shard_map/ppermute | solution.py:270
  549.8 62.9 %all-to-all-start.35 = ((f32[16,1,128]{2,1,0:T(1,128)}), f32[16,1,128]{2,1,0:T(1,128)S(1)}, u32[]{:S(2)}, u32[]{:S(2)}) async-start(f32[16,1,128]{2,1,0:T(1,128)} %shard_map.142), calls=%async_computation.35 | async-start | bytes 16384 | tf_op jit(solution)/shard_map/all_to_all | solution.py:375
